TPU v7x, 32 devices: a whole 2x2x4 slice. The times are simulated.
32 devices in a mesh: stream: 8 (over y, x, core), dp: 4 (over z).
Axes of the slice: x: 2, y: 2, z: 4, core: 2. Of those that a mesh axis runs over, the one named last changes fastest.
Arguments:
- regions: bfloat16 [16384, 768], P(('stream', 'dp')), may hold values from -6 to 6
- cotangent: bfloat16 [16384, 768], P(('stream', 'dp')), may hold values from -6 to 6
- page_lens: int32 [16, 16], replicated, may hold values from 1 to 96, 512 in all within a row
- qkv_weight: float32 [1536, 2304], P('stream'), may hold values from -0.21875 to 0.21875
- out_weight: float32 [1536, 768], P('stream'), may hold values from -1.25 to 1.25
- up_weight: float32 [1536, 3072], P('stream'), may hold values from -0.21875 to 0.21875
- down_weight: float32 [6144, 768], P('stream'), may hold values from -0.109375 to 0.109375
- ln1_gain: float32 [1536], P('stream'), may hold values from 0.5 to 1.5
- ln1_bias: float32 [1536], P('stream'), may hold values from -3 to 3
- ln2_gain: float32 [1536], P('stream'), may hold values from 0.5 to 1.5
- ln2_bias: float32 [1536], P('stream'), may hold values from -3 to 3
- up_bias: float32 [6144], P('stream'), may hold values from -3 to 3
- down_bias: float32 [1536], P('stream'), may hold values from -3 to 3
- gate_own: float32 [1536], P('stream'), may hold values from -0.21875 to 0.21875
- gate_other: float32 [1536], P('stream'), may hold values from -0.21875 to 0.21875
Outputs:
- mixed_rows: bfloat16 [16384, 768], P(('stream', 'dp'))
- region_grad: float32 [16384, 768], P(('stream', 'dp'))
- qkv_weight_grad: float32 [1536, 2304], P('stream')
- out_weight_grad: float32 [1536, 768], P('stream')
- up_weight_grad: float32 [1536, 3072], P('stream')
- down_weight_grad: float32 [6144, 768], P('stream')
- ln1_gain_grad: float32 [1536], P('stream')
- ln1_bias_grad: float32 [1536], P('stream')
- ln2_gain_grad: float32 [1536], P('stream')
- ln2_bias_grad: float32 [1536], P('stream')
- up_bias_grad: float32 [6144], P('stream')
- down_bias_grad: float32 [1536], P('stream')
- gate_own_grad: float32 [1536], P('stream')
- gate_other_grad: float32 [1536], P('stream')
Inputs may be any that keep to these rules, and one draw needn't show every extreme that they name: `page_lens`: each row holds the region counts of the pages packed into one row of 512 regions, in order; a row sums to 512 and its largest count is 96.
All inputs are finite; a program needn't handle non-finite values.
Results may differ from a plain program's by a relative error of at most 0.014.
The roundings to bfloat16 on the way count: a program that leaves them out, or rounds other values in their place, can miss the bound.
Values may be sent and summed in bfloat16 or wider, within the bound.
No kernel may reach another device: no remote copies, remote signals or barrier semaphores. Data moves between devices by JAX's collectives and lax.ppermute only.
A program may use at most 256 MiB of HBM per device.

v0:
```python
import jax
import jax.numpy as jnp
from jax import lax
from jax.sharding import PartitionSpec as P

D = 768
HEADS = 12
HEAD_DIM = 64
SEQ = 512


epsilon = 1e-05
masked_score = -1e30


def from_partner_2(block, axis, stride):
    count = lax.axis_size(axis)
    route = []
    for low in range(count):
        high = low | 1 << stride
        if high != low and high < count:
            route += [(low, high), (high, low)]
    return lax.ppermute(block, axis, route)


def from_behind(value, axis, steps):
    count = lax.axis_size(axis)
    pairs = [(source, (source + steps) % count) for source in range(count)]
    return lax.ppermute(value, axis, pairs)


def layer_norm(values, norm_gain, norm_bias):
    average = jnp.mean(values, axis=-1, keepdims=True)
    centred = values - average
    spread = jnp.mean(centred * centred, axis=-1, keepdims=True)
    return centred * lax.rsqrt(spread + epsilon) * norm_gain + norm_bias


def norm_backward(values, norm_gain, norm_bias, incoming):
    return jax.vjp(layer_norm, values, norm_gain, norm_bias)[1](incoming)


def gelu_tanh(values):
    return jax.nn.gelu(values, approximate=True)


def page_allowed(lengths):
    positions = jnp.arange(SEQ, dtype=jnp.int32)
    page_ends = jnp.cumsum(lengths, dtype=jnp.int32)
    page_index = jnp.sum(
        (page_ends[None, :] <= positions[:, None]).astype(jnp.int32), axis=1, dtype=jnp.int32
    )
    same_page = page_index[:, None] == page_index[None, :]
    return jnp.concatenate([same_page, same_page], axis=1)


def as_low(master):
    return master.astype(jnp.bfloat16)


def flat_shards(masters):
    return jnp.concatenate([as_low(member).reshape(1, -1) for member in masters], axis=1)


def split_gathered(gathered, masters):
    group = gathered.shape[0]
    pieces = []
    offset = 0
    for member in masters:
        count = member.size
        block = gathered[:, offset : offset + count]
        pieces.append(block.reshape((group * member.shape[0],) + member.shape[1:]))
        offset += count
    return tuple(pieces[:4]) + tuple((member.astype(jnp.float32) for member in pieces[4:]))


def double_up(piece, side_index, bit_count, partner_of):
    for bit in range(bit_count):
        other = partner_of(piece, bit)
        upper = side_index // 2**bit % 2 == 1
        piece = jnp.where(
            upper, jnp.concatenate([other, piece], axis=0), jnp.concatenate([piece, other], axis=0)
        )
    return piece


def halve_sum(flat, side_index, bit_count, partner_of):
    for step in range(bit_count):
        bit = bit_count - 1 - step
        size_half = flat.shape[0] // 2
        lower_part = flat[:size_half]
        upper_part = flat[size_half:]
        upper = side_index // 2**bit % 2 == 1
        outgoing = jnp.where(upper, lower_part, upper_part)
        keeping = jnp.where(upper, upper_part, lower_part)
        flat = keeping + partner_of(outgoing, bit)
    return flat


def flat_grads(grads, group):
    return jnp.concatenate([member.reshape(group, -1) for member in grads], axis=1)


def split_grads(flat, grads, group):
    pieces = []
    offset = 0
    for member in grads:
        count = member.size // group
        pieces.append(
            flat[0, offset : offset + count].reshape((member.shape[0] // group,) + member.shape[1:])
        )
        offset += count
    return tuple(pieces)


def pair_rows(pack_own, pack_other, start):
    joined = jnp.concatenate(
        [pack_own[:, start : start + D], pack_other[:, start : start + D]], axis=0
    )
    return joined.reshape(2 * SEQ, HEADS, HEAD_DIM)


def pack_scores(query_rows, key_rows, lengths):
    allowed = page_allowed(lengths)
    scores = jnp.einsum(
        "qhd,khd->hqk", query_rows, key_rows, preferred_element_type=jnp.float32
    ) * HEAD_DIM ** (-0.5)
    return jnp.where(allowed[None], scores, masked_score)


def pack_forward(pieces):
    pack_queries, pack_own, pack_other, lengths = pieces
    query_rows = pack_queries.reshape(SEQ, HEADS, HEAD_DIM)
    scores = pack_scores(query_rows, pair_rows(pack_own, pack_other, 0), lengths)
    largest = jnp.max(scores, axis=-1, keepdims=True)
    exponent = jnp.exp(scores - largest)
    denominator = jnp.sum(exponent, axis=-1, keepdims=True)
    shares = (exponent / denominator).astype(jnp.bfloat16)
    context = jnp.einsum(
        "hqk,khd->qhd",
        shares,
        pair_rows(pack_own, pack_other, D),
        preferred_element_type=jnp.float32,
    )
    return (context.reshape(SEQ, D).astype(jnp.bfloat16), largest + jnp.log(denominator))


def pack_backward(pieces):
    pack_queries, pack_own, pack_other, lengths, pack_log, pack_grad = pieces
    query_rows = pack_queries.reshape(SEQ, HEADS, HEAD_DIM)
    key_rows = pair_rows(pack_own, pack_other, 0)
    value_rows = pair_rows(pack_own, pack_other, D)
    shares = jnp.exp(pack_scores(query_rows, key_rows, lengths) - pack_log)
    grad_rows = pack_grad.reshape(SEQ, HEADS, HEAD_DIM)
    share_grad = jnp.einsum(
        "qhd,khd->hqk", grad_rows, value_rows, preferred_element_type=jnp.float32
    )
    value_grad = jnp.einsum(
        "hqk,qhd->khd", shares.astype(jnp.bfloat16), grad_rows, preferred_element_type=jnp.float32
    )
    centre = jnp.sum(shares * share_grad, axis=-1, keepdims=True)
    score_grad = (shares * (share_grad - centre)).astype(jnp.bfloat16)
    query_grad = jnp.einsum(
        "hqk,khd->qhd", score_grad, key_rows, preferred_element_type=jnp.float32
    ) * HEAD_DIM ** (-0.5)
    key_grad = jnp.einsum(
        "hqk,qhd->khd", score_grad, query_rows, preferred_element_type=jnp.float32
    ) * HEAD_DIM ** (-0.5)
    key_grad = key_grad.reshape(2 * SEQ, D)
    value_grad = value_grad.reshape(2 * SEQ, D)
    own_grad = jnp.concatenate([key_grad[:SEQ], value_grad[:SEQ]], axis=1)
    other_grad = jnp.concatenate([key_grad[SEQ:], value_grad[SEQ:]], axis=1)
    return (query_grad.reshape(SEQ, D), own_grad, other_grad)


def body(
    regions,
    cotangent,
    page_lens,
    qkv_weight,
    out_weight,
    up_weight,
    down_weight,
    ln1_gain,
    ln1_bias,
    ln2_gain,
    ln2_bias,
    up_bias,
    down_bias,
    gate_own,
    gate_other,
):
    axis_size = lax.axis_size("stream")
    half_size = axis_size // 2
    bit_count = half_size.bit_length() - 1
    side_index = lax.axis_index("stream")
    slab_index = side_index % half_size * lax.axis_size("dp") + lax.axis_index("dp")
    rows_dev = regions.shape[0]
    pack_count = rows_dev // SEQ
    lens_own = lax.dynamic_slice_in_dim(page_lens, slab_index * pack_count, pack_count, 0)
    masters = (
        qkv_weight,
        out_weight,
        up_weight,
        down_weight,
        ln1_gain,
        ln1_bias,
        ln2_gain,
        ln2_bias,
        up_bias,
        down_bias,
        gate_own,
        gate_other,
    )
    forward_set = split_gathered(
        double_up(
            flat_shards(masters),
            side_index,
            bit_count,
            lambda piece, bit: from_partner_2(piece, "stream", bit),
        ),
        masters,
    )
    (
        w_qkv,
        w_out,
        w_up,
        w_down,
        first_gain,
        first_bias,
        second_gain,
        second_bias,
        hidden_bias,
        output_bias,
        gate_self,
        gate_cross,
    ) = forward_set
    inputs = regions.astype(jnp.float32)
    normed_low = layer_norm(inputs, first_gain, first_bias).astype(jnp.bfloat16)
    projected = jnp.dot(normed_low, w_qkv, preferred_element_type=jnp.float32).astype(jnp.bfloat16)
    queries = projected[:, :D].reshape(pack_count, SEQ, D)
    own_pairs = projected[:, D:]
    other_pairs = from_behind(own_pairs, "stream", half_size)
    own_packs = own_pairs.reshape(pack_count, SEQ, 2 * D)
    other_packs = other_pairs.reshape(pack_count, SEQ, 2 * D)
    context, log_total = lax.map(pack_forward, (queries, own_packs, other_packs, lens_own))
    context = context.reshape(rows_dev, D)
    middle = inputs + jnp.dot(context, w_out, preferred_element_type=jnp.float32)
    second_low = layer_norm(middle, second_gain, second_bias).astype(jnp.bfloat16)
    upper_in = jnp.dot(second_low, w_up, preferred_element_type=jnp.float32) + hidden_bias
    hidden_low = gelu_tanh(upper_in).astype(jnp.bfloat16)
    modal_out = (
        middle + (jnp.dot(hidden_low, w_down, preferred_element_type=jnp.float32) + output_bias)
    ).astype(jnp.bfloat16)
    partner_out = from_behind(modal_out, "stream", half_size)
    own_rows = modal_out.astype(jnp.float32)
    other_rows = partner_out.astype(jnp.float32)
    logits = jnp.sum(own_rows * gate_self, axis=-1) + jnp.sum(other_rows * gate_cross, axis=-1)
    gate_rows = jax.nn.sigmoid(logits)[:, None]
    mixed_rows = (own_rows + gate_rows * other_rows).astype(jnp.bfloat16)
    back_set = split_gathered(
        double_up(
            flat_shards(masters),
            side_index,
            bit_count,
            lambda piece, bit: from_partner_2(piece, "stream", bit),
        ),
        masters,
    )
    (
        w_qkv,
        w_out,
        w_up,
        w_down,
        first_gain,
        first_bias,
        second_gain,
        second_bias,
        hidden_bias,
        output_bias,
        gate_self,
        gate_cross,
    ) = back_set
    tangent = cotangent.astype(jnp.float32)
    logit_grad = (
        jnp.sum(tangent * other_rows, axis=-1, keepdims=True) * gate_rows * (1.0 - gate_rows)
    )
    to_partner = tangent * gate_rows + logit_grad * gate_cross
    from_partner = from_behind(to_partner, "stream", half_size)
    modal_grad = tangent + logit_grad * gate_self + from_partner
    gate_self_grad = jnp.sum(logit_grad * own_rows, axis=0)
    gate_cross_grad = jnp.sum(logit_grad * other_rows, axis=0)
    branch_low = modal_grad.astype(jnp.bfloat16)
    output_bias_grad = jnp.sum(modal_grad, axis=0)
    down_grad = jnp.einsum("rf,rd->fd", hidden_low, branch_low, preferred_element_type=jnp.float32)
    hidden_grad = jnp.einsum("rd,fd->rf", branch_low, w_down, preferred_element_type=jnp.float32)
    upper_grad = jax.vjp(gelu_tanh, upper_in)[1](hidden_grad)[0]
    hidden_bias_grad = jnp.sum(upper_grad, axis=0)
    upper_low = upper_grad.astype(jnp.bfloat16)
    up_grad = jnp.einsum("rd,rf->df", second_low, upper_low, preferred_element_type=jnp.float32)
    normed_two_grad = jnp.einsum("rf,df->rd", upper_low, w_up, preferred_element_type=jnp.float32)
    middle_part, second_gain_grad, second_bias_grad = norm_backward(
        middle, second_gain, second_bias, normed_two_grad
    )
    middle_grad = modal_grad + middle_part
    attended_low = middle_grad.astype(jnp.bfloat16)
    out_weight_grad = jnp.einsum(
        "rd,re->de", context, attended_low, preferred_element_type=jnp.float32
    )
    context_grad = jnp.einsum(
        "re,de->rd", attended_low, w_out, preferred_element_type=jnp.float32
    ).astype(jnp.bfloat16)
    query_grad, own_grad, other_grad = lax.map(
        pack_backward,
        (
            queries,
            own_packs,
            other_packs,
            lens_own,
            log_total,
            context_grad.reshape(pack_count, SEQ, D),
        ),
    )
    returned = from_behind(other_grad.reshape(rows_dev, 2 * D), "stream", half_size)
    projected_grad = jnp.concatenate(
        [query_grad.reshape(rows_dev, D), own_grad.reshape(rows_dev, 2 * D) + returned], axis=1
    ).astype(jnp.bfloat16)
    qkv_grad = jnp.einsum(
        "rd,re->de", normed_low, projected_grad, preferred_element_type=jnp.float32
    )
    normed_one_grad = jnp.einsum(
        "re,de->rd", projected_grad, w_qkv, preferred_element_type=jnp.float32
    )
    input_part, first_gain_grad, first_bias_grad = norm_backward(
        inputs, first_gain, first_bias, normed_one_grad
    )
    region_grad = middle_grad + input_part
    own_grads = (
        qkv_grad,
        out_weight_grad,
        up_grad,
        down_grad,
        first_gain_grad,
        first_bias_grad,
        second_gain_grad,
        second_bias_grad,
        hidden_bias_grad,
        output_bias_grad,
        gate_self_grad,
        gate_cross_grad,
    )
    flat = flat_grads(own_grads, half_size)
    flat = lax.psum(flat, "dp")
    flat = halve_sum(
        flat, side_index, bit_count, lambda piece, bit: from_partner_2(piece, "stream", bit)
    )
    reduced = split_grads(flat, own_grads, half_size)
    return (
        mixed_rows,
        region_grad,
        reduced[0],
        reduced[1],
        reduced[2],
        reduced[3],
        reduced[4],
        reduced[5],
        reduced[6],
        reduced[7],
        reduced[8],
        reduced[9],
        reduced[10],
        reduced[11],
    )


def solution(mesh):
    in_specs = (
        P(("stream", "dp"), None),
        P(("stream", "dp"), None),
        P(),
        P("stream", None),
        P("stream", None),
        P("stream", None),
        P("stream", None),
        P("stream"),
        P("stream"),
        P("stream"),
        P("stream"),
        P("stream"),
        P("stream"),
        P("stream"),
        P("stream"),
    )
    out_specs = (
        P(("stream", "dp"), None),
        P(("stream", "dp"), None),
        P("stream", None),
        P("stream", None),
        P("stream", None),
        P("stream", None),
        P("stream"),
        P("stream"),
        P("stream"),
        P("stream"),
        P("stream"),
        P("stream"),
        P("stream"),
        P("stream"),
    )
    return jax.shard_map(body, mesh=mesh, in_specs=in_specs, out_specs=out_specs, check_vma=False)
```

profile of v0, /device:TPU:0, one launch (start us, length us, event | category | flops | bytes accessed | tf_op | source)
XLA Modules:
  0.0 2074.1 jit_solution(9339933395745553156)
XLA Ops:
  19.3 3.9 constant_dynamic-update-slice_fusion.3
  23.2 3.9 constant_dynamic-update-slice_fusion.2
  36.7 11.3 collective-permute-done
  48.0 45.3 %broadcast_select_fusion.3 = bf16[2,1771584]{1,0:T(2,128)(2,1)} fusion(pred[]{:T(512)S(6)} %eq.53, bf16[1,1771584]{1,0:T(2,128)(2,1)} %constant_dynamic-update-slice_fusion, bf16[1,1771584]{1,0:T(2,128)(2,1)} %collective-permute-done), kind=kLoop, calls=%fused_computation.13 | loop fusion | flops 31888512 | bytes 14172673 | tf_op jit(solution)/shard_map/jit(_where)/select_n | solution.py:81
  98.3 151.1 %collective-permute-done.1 = bf16[2,1771584]{1,0:T(2,128)(2,1)} collective-permute-done((bf16[2,1771584]{1,0:T(2,128)(2,1)}, bf16[2,1771584]{1,0:T(2,128)(2,1)}, u32[]{:S(2)}, u32[]{:S(2)}) %collective-permute-start.1) | collective-permute-done | bytes 7086368 | tf_op jit(solution)/shard_map/ppermute | solution.py:23
  249.4 45.0 %maximum_select_fusion = bf16[4,1771584]{1,0:T(4,128)(2,1)S(1)} fusion(bf16[2,1771584]{1,0:T(2,128)(2,1)} %broadcast_select_fusion.3, bf16[2,1771584]{1,0:T(2,128)(2,1)} %collective-permute-done.1, pred[]{:T(512)S(6)} %eq.52), kind=kLoop, calls=%fused_computation.8 | loop fusion | flops 63777024 | bytes 28345344 | tf_op jit(solution)/shard_map/jit(_where)/select_n | solution.py:81
  294.6 5.0 copy-done.5
  302.3 7.3 reshape.395
  309.9 4.3 convolution_convert_fusion
  317.4 6.1 fusion.70
  329.9 9.1 reshape.403
  338.9 8.8 reshape.402
  359.3 12.9 fusion.6
  372.2 12.3 fusion
  387.6 8.5 fusion.43
  398.6 5.0 fusion.64
  403.7 4.9 fusion.29
  410.1 16.9 collective-permute-done.3
  429.0 33.0 %collective-permute-done.4 = f32[512,768]{1,0:T(8,128)S(1)} collective-permute-done((f32[512,768]{1,0:T(8,128)S(1)}, f32[512,768]{1,0:T(8,128)S(1)}, u32[]{:S(2)}, u32[]{:S(2)}) %collective-permute-start.4) | collective-permute-done | bytes 1572896 | tf_op jit(solution)/shard_map/ppermute | solution.py:29
  461.9 10.0 fusion.77
  483.4 13.3 fusion.19
  496.8 18.5 multiply_reduce_fusion
  515.3 3.4 fusion.73
  518.7 16.9 multiply_convert_fusion
  546.7 4.4 reshape.407
  551.0 7.4 fusion.37
  558.5 13.8 reshape.408
  572.3 10.5 fusion.47
  582.8 12.4 reshape.409
  595.6 8.7 multiply_convert_fusion.2
  604.3 6.6 collective-permute-done.5
  616.2 5.2 fusion.41
  621.4 9.8 reshape.406
  631.3 6.4 constant_dynamic-update-slice_fusion.11
  641.6 9.5 constant_dynamic-update-slice_fusion.9
  651.1 4.4 constant_dynamic-update-slice_fusion.8
  665.1 936.5 %all-reduce.2.cloned.1.call-done = f32[4,1771584]{1,0:T(4,128)} async-done(((f32[4,1771584]{1,0:T(4,128)}), f32[4,1771584]{1,0:T(4,128)}) %all-reduce.2.cloned.1.call-update) | async-done | bytes 28345360 | tf_op jit(solution)/shard_map/psum | solution.py:353
  1601.6 24.1 %broadcast_select_fusion = f32[2,1771584]{1,0:T(2,128)} fusion(pred[]{:T(512)S(6)} %eq.52, f32[4,1771584]{1,0:T(4,128)} %all-reduce.2.cloned.1.call-done), kind=kLoop, calls=%fused_computation.10 | loop fusion | flops 3543168 | bytes 42518016 | tf_op jit(solution)/shard_map/jit(_where)/select_n | solution.py:94
  1627.1 305.0 %collective-permute-done.6 = f32[2,1771584]{1,0:T(2,128)} collective-permute-done((f32[2,1771584]{1,0:T(2,128)}, f32[2,1771584]{1,0:T(2,128)}, u32[]{:S(2)}, u32[]{:S(2)}) %collective-permute-start.6) | collective-permute-done | bytes 14172704 | tf_op jit(solution)/shard_map/ppermute | solution.py:23
  1932.2 28.6 %select_add_fusion = f32[2,1771584]{1,0:T(2,128)} fusion(f32[2,1771584]{1,0:T(2,128)} %collective-permute-done.6, pred[]{:T(512)S(6)} %eq.52, f32[4,1771584]{1,0:T(4,128)} %all-reduce.2.cloned.1.call-done), kind=kLoop, calls=%fused_computation.9 | loop fusion | flops 7086336 | bytes 56690688 | tf_op jit(solution)/shard_map/add | solution.py:96
  1960.8 15.9 broadcast_select_fusion.1
  1976.9 3.1 add_add_fusion.2
  1980.0 8.5 collective-permute-done.7
  1988.5 12.4 fusion.7
  2000.9 20.6 slice_reduce_fusion.2
  2021.5 7.0 slice_reduce_fusion.3
  2028.6 27.3 %slice_reduce_fusion = (f32[589824]{0:T(1024)S(1)}, f32[589824]{0:T(1024)}) fusion(f32[1,1771584]{1,0:T(1,128)} %fusion.7), kind=kLoop, calls=%fused_computation.51 | loop fusion | bytes 9437184 | tf_op jit(solution)/shard_map/slice | solution.py:110
  2062.2 3.3 reshape_squeeze.14
  (251 shorter events, 110.6 us)
Async XLA Ops:
  7.2 89.1 %copy-start = (s32[16,16]{1,0:T(8,128)S(1)}, s32[16,16]{1,0:T(8,128)}, u32[]{:S(2)}) copy-start(s32[16,16]{1,0:T(8,128)} %param.17) | copy-start | bytes 3076
  7.2 1594.4 %all-reduce.2.cloned.1.call-start = ((), (), s32[]{:S(2)}) async-start(), calls=%async_computation | async-start | bytes 56692736 | tf_op jit(solution)/shard_map/psum | solution.py:353
  36.3 11.7 collective-permute-start
  36.7 61.0 %copy-start.12 = (bf16[512,768]{1,0:T(8,128)(2,1)S(1)}, bf16[512,768]{1,0:T(8,128)(2,1)}, u32[]{:S(2)}) copy-start(bf16[512,768]{1,0:T(8,128)(2,1)} %param.15) | copy-start | bytes 2359300
  93.3 156.1 %collective-permute-start.1 = (bf16[2,1771584]{1,0:T(2,128)(2,1)}, bf16[2,1771584]{1,0:T(2,128)(2,1)}, u32[]{:S(2)}, u32[]{:S(2)}) collective-permute-start(bf16[2,1771584]{1,0:T(2,128)(2,1)} %broadcast_select_fusion.3), channel_id=1, source_target_pairs={{0,8},{8,0},{4,12},{12,4},{16,24},{24,16},{20,28},{28,20},{1,9},{9... | collective-permute-start | bytes 21259016 | tf_op jit(solution)/shard_map/ppermute | solution.py:23
  97.9 211.9 %copy-start.39 = (f32[512]{0:T(512)}, f32[512]{0:T(512)S(1)}, u32[]{:S(2)}) copy-start(f32[512]{0:T(512)S(1)} %broadcast_multiply_fusion.1) | copy-start | bytes 6148
  98.3 196.2 %copy-start.43 = (f32[512]{0:T(512)}, f32[512]{0:T(512)S(1)}, u32[]{:S(2)}) copy-start(f32[512]{0:T(512)S(1)} %fusion.27) | copy-start | bytes 6148
  98.3 211.5 %copy-start.41 = (f32[512]{0:T(512)}, f32[512]{0:T(512)S(1)}, u32[]{:S(2)}) copy-start(f32[512]{0:T(512)S(1)} %fusion.53) | copy-start | bytes 6148
  294.5 5.0 copy-start.5
  302.3 7.5 copy-start.13
  309.8 7.5 copy-start.6
  314.2 9.3 copy-start.19
  315.5 36.2 %collective-permute-start.2 = (bf16[512,1536]{1,0:T(8,128)(2,1)}, bf16[512,1536]{1,0:T(8,128)(2,1)}, u32[]{:S(2)}, u32[]{:S(2)}) collective-permute-start(bf16[512,1536]{1,0:T(8,128)(2,1)} %slice.198), channel_id=1, source_target_pairs={{0,16},{4,20},{8,24},{12,28},{16,0},{20,4},{24,8},{28,12},{1,17},{... | collective-permute-start | bytes 4718600 | tf_op jit(solution)/shard_map/ppermute | solution.py:29
  359.2 13.0 copy-start.9
  359.3 25.3 %copy-start.20 = (bf16[1024,768]{0,1:T(8,128)(2,1)S(1)}, bf16[1024,768]{0,1:T(8,128)(2,1)}, u32[]{:S(2)}) copy-start(bf16[1024,768]{0,1:T(8,128)(2,1)} %copy.43) | copy-start | bytes 4718596
  372.2 15.4 copy-start.2
  387.6 8.5 copy-start.33
  396.1 7.5 slice-start.6
  398.3 5.3 copy-start.21
  398.6 5.0 slice-start.7
  403.6 4.9 copy-start.55
  403.7 23.3 %copy-start.16 = (bf16[512,768]{1,0:T(8,128)(2,1)S(1)}, bf16[512,768]{1,0:T(8,128)(2,1)}, u32[]{:S(2)}) copy-start(bf16[512,768]{1,0:T(8,128)(2,1)} %param.16) | copy-start | bytes 2359300
  408.6 18.4 collective-permute-start.3
  427.0 45.0 %copy-start.28 = (bf16[512,768]{1,0:T(8,128)(2,1)}, bf16[512,768]{1,0:T(8,128)(2,1)S(1)}, u32[]{:S(2)}) copy-start(bf16[512,768]{1,0:T(8,128)(2,1)S(1)} %collective-permute-done.3) | copy-start | bytes 2359300
  427.8 34.2 %collective-permute-start.4 = (f32[512,768]{1,0:T(8,128)S(1)}, f32[512,768]{1,0:T(8,128)S(1)}, u32[]{:S(2)}, u32[]{:S(2)}) collective-permute-start(f32[512,768]{1,0:T(8,128)S(1)} %fusion.33), channel_id=1, source_target_pairs={{0,16},{4,20},{8,24},{12,28},{16,0},{20,4},{24,8},{28,12},{1,17},{... | collective-permute-start | bytes 4718600 | tf_op jit(solution)/shard_map/ppermute | solution.py:29
  428.9 43.0 %slice-start.4 = ((s8[4718592]{0:T(1024)(128)(4,1)}), s8[4194304]{0:T(1024)(128)(4,1)S(1)}, s32[]{:S(2)}) async-start(s8[4718592]{0:T(1024)(128)(4,1)} %bitcast.80), calls=%async_computation.5 | async-start | bytes 8388608
  428.9 43.0 %copy-start.22 = (f32[512,768]{1,0:T(8,128)S(1)}, f32[512,768]{1,0:T(8,128)}, u32[]{:S(2)}) copy-start(f32[512,768]{1,0:T(8,128)} %copy-done.21) | copy-start | bytes 4718596
  429.0 43.0 %slice-start.5 = ((s8[4718592]{0:T(1024)(128)(4,1)}), s8[524288]{0:T(1024)(128)(4,1)S(1)}, s32[]{:S(2)}) async-start(s8[4718592]{0:T(1024)(128)(4,1)} %bitcast.80), calls=%async_computation.6 | async-start | bytes 1048576
  461.9 13.8 copy-start.32
  479.4 65.0 %copy-start.7 = (f32[512,768]{1,0:T(8,128)}, f32[512,768]{1,0:T(8,128)S(1)}, u32[]{:S(2)}) copy-start(f32[512,768]{1,0:T(8,128)S(1)} %get-tuple-element.103) | copy-start | bytes 4718596
  518.7 16.9 copy-start.15
  535.6 4.6 copy-start.3
  543.7 67.2 %collective-permute-start.5 = (f32[512,1536]{0,1:T(8,128)}, f32[512,1536]{0,1:T(8,128)}, u32[]{:S(2)}, u32[]{:S(2)}) collective-permute-start(f32[512,1536]{0,1:T(8,128)} %pad_maximum_fusion), channel_id=1, source_target_pairs={{0,16},{4,20},{8,24},{12,28},{16,0},{20,4},{24,8},{28,12},{1,17},{... | collective-permute-start | bytes 9437192 | tf_op jit(solution)/shard_map/ppermute | solution.py:29
  558.5 13.8 copy-start.18
  582.8 12.8 copy-start.10
  595.6 15.3 copy-start.25
  595.6 15.3 copy-start.26
  616.2 21.5 %copy-start.24 = (f32[512,768]{1,0:T(8,128)}, f32[512,768]{1,0:T(8,128)S(1)}, u32[]{:S(2)}) copy-start(f32[512,768]{1,0:T(8,128)S(1)} %get-tuple-element.119) | copy-start | bytes 4718596
  616.2 5.2 copy-start.44
  638.6 12.5 slice-start.1
  641.6 9.5 slice-start.2
  641.6 9.5 slice-start.3
  1625.6 306.5 %collective-permute-start.6 = (f32[2,1771584]{1,0:T(2,128)}, f32[2,1771584]{1,0:T(2,128)}, u32[]{:S(2)}, u32[]{:S(2)}) collective-permute-start(f32[2,1771584]{1,0:T(2,128)} %broadcast_select_fusion), channel_id=1, source_target_pairs={{0,8},{8,0},{4,12},{12,4},{16,24},{24,16},{20,28},{28,20},{1,9},{9... | collective-permute-start | bytes 42518024 | tf_op jit(solution)/shard_map/ppermute | solution.py:23
  1960.8 16.1 copy-start.8
  1960.8 16.1 copy-start.14
  1960.8 27.7 %copy-start.4 = (f32[2,1771584]{1,0:T(2,128)S(1)}, f32[2,1771584]{1,0:T(2,128)}, u32[]{:S(2)}) copy-start(f32[2,1771584]{1,0:T(2,128)} %select_add_fusion) | copy-start | bytes 42518020
  1976.8 11.7 collective-permute-start.7
  2062.2 4.9 copy-start.1
  (26 other events, 72.2 us)
Sparse Core Ops, SparseCore 0:
  665.2 936.3 all-reduce.1
where the time goes:
time: 2080 us; the launch traced here: 2070 us
  waiting for transfers between devices  1470 us (71%)
  local copies, waits for them, and re-layouts  233 us (11%)
  other arithmetic  221 us (11%)
  matrix products  123 us (6%)
    psum x1, waiting for transfers between devices, body(): flat = lax.psum(flat, 'dp')  936 us
    ppermute x4, waiting for transfers between devices, from_partner_2(): return lax.ppermute(block, axis, route)  476 us
    select_n x2, other arithmetic, double_up(): jnp.where(upper, jnp.concatenate([other, piece], axis=0), jnp.concatenate...  90.4 us
    unnamed x154, local copies, waits for them, and re-layouts  69.9 us
    ppermute x4, waiting for transfers between devices, from_behind(): return lax.ppermute(value, axis, pairs)  59.5 us
    slice x5, local copies, waits for them, and re-layouts, split_grads(): flat[0, offset:offset + count]  57.7 us
  transfers between devices with their start and end apart: 9, of which 9 were waited for; matrix products, arithmetic and copies ran while one was open for 5% of the time, Pallas kernels for 0%

commit v1 on v0

v1 whole, which is shorter than its diff:
```python
import functools
import math

import jax
import jax.numpy as jnp
from jax import lax
from jax.experimental import pallas as pl
from jax.experimental.pallas import tpu as pltpu
from jax.sharding import PartitionSpec as P

D = 768
HEADS = 12
HEAD_DIM = 64
FF = 3072
SEQ = 512
GROUPS = 3
WIDE = D // GROUPS
PAIR = 2 * HEAD_DIM
BLOCK = 128
REACH = 96
ROWS = 256
MIB = 1024 * 1024

epsilon = 1e-05
masked_score = -1e30
score_scale = HEAD_DIM ** (-0.5)
gelu_scale = math.sqrt(2.0 / math.pi)
gelu_cubic = 0.044715

f32 = jnp.float32
bf16 = jnp.bfloat16

WINDOWS = [
    (max(0, start - REACH), min(SEQ, start + BLOCK + REACH)) for start in range(0, SEQ, BLOCK)
]
WINDOW = BLOCK + 2 * REACH

in_smem = pl.BlockSpec(memory_space=pltpu.SMEM)
in_vmem = pl.BlockSpec(memory_space=pltpu.VMEM)
in_any = pl.BlockSpec(memory_space=pl.ANY)


def shape_of(dims, dtype):
    return jax.ShapeDtypeStruct(dims, dtype)


def params(limit):
    return pltpu.CompilerParams(vmem_limit_bytes=limit * MIB)


def dot(left, right):
    return lax.dot_general(left, right, (((1,), (0,)), ((), ())), preferred_element_type=f32)


def dot_nt(left, right):
    return lax.dot_general(left, right, (((1,), (1,)), ((), ())), preferred_element_type=f32)


def dot_tn(left, right):
    return lax.dot_general(left, right, (((0,), (0,)), ((), ())), preferred_element_type=f32)


def normalise(values):
    average = jnp.mean(values, axis=-1, keepdims=True)
    centred = values - average
    spread = jnp.mean(centred * centred, axis=-1, keepdims=True)
    root = lax.rsqrt(spread + epsilon)
    return centred * root, root


def norm_back(scaled, root, gain, incoming):
    weighted = incoming * gain
    average = jnp.mean(weighted, axis=-1, keepdims=True)
    slope = jnp.mean(weighted * scaled, axis=-1, keepdims=True)
    return root * (weighted - average - scaled * slope)


def column_sums(values):
    return jnp.sum(values, axis=0, keepdims=True)


def part_copies(places, parts, whole, sems):
    rows = whole.shape[0] // len(parts)
    return [
        pltpu.make_async_copy(
            part.at[pl.ds(0, rows)],
            whole.at[pl.ds(pl.multiple_of(places[k] * rows, 16), rows)],
            sems.at[k],
        )
        for k, part in enumerate(parts)
    ]


def start_all(copies):
    for copy in copies:
        copy.start()


def wait_all(copies):
    for copy in copies:
        copy.wait()


def project_kernel(count, places, rows, gain, bias, *rest):
    parts = rest[:count]
    query_out, pair_outs, normed_out = rest[count], rest[count + 1 : count + 4], rest[count + 4]
    weight, sems = rest[count + 5 :]
    copies = part_copies(places, parts, weight, sems)
    start_all(copies)
    scaled, _ = normalise(rows[...].astype(f32))
    normed_out[...] = (scaled * gain[...] + bias[...]).astype(bf16)
    wait_all(copies)
    normed = normed_out[...]

    def block(column):
        return dot(normed, weight[:, column : column + WIDE]).astype(bf16)

    for group in range(GROUPS):
        first = group * WIDE
        pair_outs[group][0] = block(D + first)
        pair_outs[group][1] = block(2 * D + first)
    for group in range(GROUPS):
        first = group * WIDE
        query_out[:, first : first + WIDE] = block(first)


def project(places, rows, gain, bias, parts):
    count = len(parts)
    outs = pl.pallas_call(
        functools.partial(project_kernel, count),
        out_shape=[shape_of((SEQ, D), bf16)]
        + [shape_of((2, SEQ, WIDE), bf16)] * GROUPS
        + [shape_of((SEQ, D), bf16)],
        in_specs=[in_smem] + [in_vmem] * 3 + [in_any] * count,
        out_specs=[in_vmem] * (GROUPS + 2),
        scratch_shapes=[pltpu.VMEM((D, 3 * D), bf16), pltpu.SemaphoreType.DMA((count,))],
        compiler_params=params(24),
        cost_estimate=pl.CostEstimate(
            flops=2 * SEQ * D * 3 * D, bytes_accessed=7 * MIB, transcendentals=0
        ),
        name="project",
    )(places, rows, gain, bias, *parts)
    return outs[0], outs[1:4], outs[4]


def fill_page_bias(page_row, page_column, bias):
    for index, (low, high) in enumerate(WINDOWS):
        start = index * BLOCK
        same = page_column[low:high] == page_row[:, start : start + BLOCK]
        bias[index, : high - low] = jnp.where(same, 0.0, masked_score)


def two_heads(block):
    lane = lax.broadcasted_iota(jnp.int32, block.shape, 1)
    zero = jnp.zeros_like(block)
    return jnp.concatenate(
        [jnp.where(lane < HEAD_DIM, block, zero), jnp.where(lane < HEAD_DIM, zero, block)], axis=0
    )


def head_rows(both):
    return jnp.concatenate([both[:HEAD_DIM, :BLOCK], both[HEAD_DIM:, BLOCK:]], axis=0).T


def page_bias(bias, index, size):
    block = bias[index, :size]
    return jnp.concatenate([block, block], axis=1)


def attend_kernel(
    query, key, value, key_two, value_two, page_row, page_column, context, log_total, bias
):
    @pl.when(pl.program_id(0) == 0)
    def _():
        fill_page_bias(page_row, page_column, bias)

    for index, (low, high) in enumerate(WINDOWS):
        start = index * BLOCK
        queries = two_heads(query[start : start + BLOCK] * score_scale)
        allowed = page_bias(bias, index, high - low)
        scores = dot_nt(key[0, low:high], queries) + allowed
        scores_two = dot_nt(key_two[0, low:high], queries) + allowed
        largest = jnp.maximum(
            jnp.max(scores, axis=0, keepdims=True), jnp.max(scores_two, axis=0, keepdims=True)
        )
        exponent = jnp.exp(scores - largest)
        exponent_two = jnp.exp(scores_two - largest)
        total = column_sums(exponent) + column_sums(exponent_two)
        inverse = 1.0 / total
        shares = (exponent * inverse).astype(bf16)
        shares_two = (exponent_two * inverse).astype(bf16)
        both = dot_tn(value[0, low:high], shares) + dot_tn(value_two[0, low:high], shares_two)
        context[start : start + BLOCK] = head_rows(both).astype(bf16)
        log_row = largest + jnp.log(total)
        log_total[0, 0:1, start : start + BLOCK] = log_row[:, :BLOCK]
        log_total[0, 1:2, start : start + BLOCK] = log_row[:, BLOCK:]


def attention_specs(group):
    steps = WIDE // PAIR
    wide_query = pl.BlockSpec((SEQ, PAIR), lambda step: (0, steps * group + step))
    key = pl.BlockSpec((1, SEQ, PAIR), lambda step: (0, 0, step))
    value = pl.BlockSpec((1, SEQ, PAIR), lambda step: (1, 0, step))
    page_row = pl.BlockSpec((1, SEQ), lambda step: (0, 0))
    page_column = pl.BlockSpec((SEQ, 1), lambda step: (0, 0))
    narrow = pl.BlockSpec((SEQ, PAIR), lambda step: (0, step))
    logs = pl.BlockSpec((1, 2, SEQ), lambda step: (step, 0, 0))
    return wide_query, key, value, page_row, page_column, narrow, logs


def attend(group, queries, own, other, page_row, page_column):
    steps = WIDE // PAIR
    wide_query, key, value, row_spec, column_spec, narrow, logs = attention_specs(group)
    return pl.pallas_call(
        attend_kernel,
        grid=(steps,),
        out_shape=[shape_of((SEQ, WIDE), bf16), shape_of((steps, 2, SEQ), f32)],
        in_specs=[wide_query, key, value, key, value, row_spec, column_spec],
        out_specs=[narrow, logs],
        scratch_shapes=[pltpu.VMEM((len(WINDOWS), WINDOW, BLOCK), f32)],
        compiler_params=params(24),
        cost_estimate=pl.CostEstimate(
            flops=4 * SEQ * SEQ * WIDE, bytes_accessed=2 * MIB, transcendentals=SEQ * SEQ
        ),
        name="attend",
    )(queries, own, own, other, other, page_row, page_column)


def attend_back_kernel(
    query,
    key,
    value,
    key_two,
    value_two,
    context_grad,
    log_total,
    page_row,
    page_column,
    query_grad,
    own_grad,
    other_grad,
    bias,
    other_sum,
):
    @pl.when(pl.program_id(0) == 0)
    def _():
        fill_page_bias(page_row, page_column, bias)

    own_grad[...] = jnp.zeros_like(own_grad)
    other_sum[...] = jnp.zeros_like(other_sum)
    for index, (low, high) in enumerate(WINDOWS):
        start = index * BLOCK
        queries = two_heads(query[start : start + BLOCK] * score_scale)
        grads = two_heads(context_grad[start : start + BLOCK])
        log_row = jnp.concatenate(
            [
                log_total[0, 0:1, start : start + BLOCK],
                log_total[0, 1:2, start : start + BLOCK],
            ],
            axis=1,
        )
        allowed = page_bias(bias, index, high - low)
        keys, keys_two = key[0, low:high], key_two[0, low:high]
        shares = jnp.exp(dot_nt(keys, queries) + allowed - log_row)
        shares_two = jnp.exp(dot_nt(keys_two, queries) + allowed - log_row)
        share_grad = dot_nt(value[0, low:high], grads)
        share_grad_two = dot_nt(value_two[0, low:high], grads)
        centre = column_sums(shares * share_grad) + column_sums(shares_two * share_grad_two)
        score_grad = (shares * (share_grad - centre)).astype(bf16)
        score_grad_two = (shares_two * (share_grad_two - centre)).astype(bf16)
        own_grad[0, low:high] += dot(score_grad, queries)
        own_grad[1, low:high] += dot(shares.astype(bf16), grads)
        other_sum[0, low:high] += dot(score_grad_two, queries)
        other_sum[1, low:high] += dot(shares_two.astype(bf16), grads)
        both = dot_tn(keys, score_grad) + dot_tn(keys_two, score_grad_two)
        query_grad[start : start + BLOCK] = (head_rows(both) * score_scale).astype(bf16)
    other_grad[...] = other_sum[...].astype(bf16)


def attend_back(group, queries, own, other, context_grad, log_total, page_row, page_column):
    steps = WIDE // PAIR
    wide_query, key, value, row_spec, column_spec, narrow, logs = attention_specs(group)
    pair = pl.BlockSpec((2, SEQ, PAIR), lambda step: (0, 0, step))
    return pl.pallas_call(
        attend_back_kernel,
        grid=(steps,),
        out_shape=[
            shape_of((SEQ, WIDE), bf16),
            shape_of((2, SEQ, WIDE), f32),
            shape_of((2, SEQ, WIDE), bf16),
        ],
        in_specs=[wide_query, key, value, key, value, wide_query, logs, row_spec, column_spec],
        out_specs=[narrow, pair, pair],
        scratch_shapes=[
            pltpu.VMEM((len(WINDOWS), WINDOW, BLOCK), f32),
            pltpu.VMEM((2, SEQ, PAIR), f32),
        ],
        compiler_params=params(24),
        cost_estimate=pl.CostEstimate(
            flops=10 * SEQ * SEQ * WIDE, bytes_accessed=4 * MIB, transcendentals=SEQ * SEQ
        ),
        name="attend_back",
    )(queries, own, own, other, other, context_grad, log_total, page_row, page_column)


def middle_kernel(count, places, rows, contexts, partner_tangent, vectors, hidden_bias, *rest):
    out_parts, up_parts, down_parts = (rest[k * count : (k + 1) * count] for k in range(3))
    middle_out, second_out, hidden_out, slope_out, modal_out, inner_out = rest[3 * count : 3 * count + 6]
    w_out, w_up, w_down, sems = rest[3 * count + 6 :]
    out_copies = part_copies(places, out_parts, w_out, sems.at[0])
    up_copies = part_copies(places, up_parts, w_up, sems.at[1])
    down_copies = part_copies(places, down_parts, w_down, sems.at[2])
    first_step = pl.program_id(0) == 0

    @pl.when(first_step)
    def _():
        start_all(out_copies)
        start_all(up_copies)
        start_all(down_copies)
        wait_all(out_copies)

    middle = rows[...].astype(f32)
    for group in range(GROUPS):
        middle += dot(contexts[group], w_out[group * WIDE : (group + 1) * WIDE])
    middle_out[...] = middle
    scaled, _ = normalise(middle)
    second = (scaled * vectors[0:1] + vectors[1:2]).astype(bf16)
    second_out[...] = second

    @pl.when(first_step)
    def _():
        wait_all(up_copies)
        wait_all(down_copies)

    branch = jnp.zeros((ROWS, D), f32) + vectors[2:3]
    size = 512
    for first in range(0, FF, size):
        part = slice(first, first + size)
        upper = dot(second, w_up[:, part]) + hidden_bias[:, part]
        square = upper * upper
        angle = jnp.tanh(gelu_scale * (upper + gelu_cubic * (square * upper)))
        half = 0.5 * (1.0 + angle)
        hidden = (upper * half).astype(bf16)
        hidden_out[:, part] = hidden
        bend = gelu_scale + (3.0 * gelu_cubic * gelu_scale) * square
        slope_out[:, part] = (half + 0.5 * upper * (1.0 - angle * angle) * bend).astype(bf16)
        branch += dot(hidden, w_down[part])
    modal = (middle + branch).astype(bf16)
    modal_out[...] = modal
    modal = modal.astype(f32)
    own = jnp.sum(modal * vectors[3:4], axis=1, keepdims=True)
    cross = jnp.sum(modal * vectors[4:5], axis=1, keepdims=True)
    met = jnp.sum(modal * partner_tangent[...].astype(f32), axis=1, keepdims=True)
    lane = lax.broadcasted_iota(jnp.int32, (ROWS, 128), 1)
    columns = jnp.where(lane == 0, own, jnp.where(lane == 1, cross, met))
    inner_out[...] = columns.T[:8]


def middle_pass(places, rows, contexts, partner_tangent, vectors, hidden_bias, outs, ups, downs):
    count = len(outs)
    by_rows = lambda width: pl.BlockSpec((ROWS, width), lambda step: (step, 0))
    whole = lambda dims: pl.BlockSpec(dims, lambda step: (0, 0))

    def kernel(places_ref, rows_ref, c0, c1, c2, *rest):
        middle_kernel(count, places_ref, rows_ref, (c0[...], c1[...], c2[...]), *rest)

    return pl.pallas_call(
        kernel,
        grid=(SEQ // ROWS,),
        out_shape=[
            shape_of((SEQ, D), f32),
            shape_of((SEQ, D), bf16),
            shape_of((SEQ, FF), bf16),
            shape_of((SEQ, FF), bf16),
            shape_of((SEQ, D), bf16),
            shape_of((8, SEQ), f32),
        ],
        in_specs=[in_smem, by_rows(D)]
        + [by_rows(WIDE)] * GROUPS
        + [by_rows(D), whole((8, D)), whole((1, FF))]
        + [in_any] * (3 * count),
        out_specs=[
            by_rows(D),
            by_rows(D),
            by_rows(FF),
            by_rows(FF),
            by_rows(D),
            pl.BlockSpec((8, ROWS), lambda step: (0, step)),
        ],
        scratch_shapes=[
            pltpu.VMEM((D, D), bf16),
            pltpu.VMEM((D, FF), bf16),
            pltpu.VMEM((FF, D), bf16),
            pltpu.SemaphoreType.DMA((3, count)),
        ],
        compiler_params=params(44),
        cost_estimate=pl.CostEstimate(
            flops=2 * SEQ * D * (D + 2 * FF), bytes_accessed=21 * MIB, transcendentals=SEQ * FF
        ),
        name="middle",
    )(places, rows, *contexts, partner_tangent, vectors, hidden_bias, *outs, *ups, *downs)


def gate_kernel(own, other, tangent, partner_tangent, vectors, grad_out, low_out, columns_out, sums):
    gate = jax.nn.sigmoid(own[0:1] + other[1:2])
    gate_two = jax.nn.sigmoid(other[0:1] + own[1:2])
    logit = other[2:3] * gate * (1.0 - gate)
    logit_two = own[2:3] * gate_two * (1.0 - gate_two)
    padding = jnp.zeros((124, SEQ), f32)
    columns = jnp.concatenate([gate, logit, gate_two, logit_two, padding], axis=0).T
    columns_out[...] = columns
    grad = (
        tangent[...].astype(f32)
        + columns[:, 1:2] * vectors[3:4]
        + partner_tangent[...].astype(f32) * columns[:, 2:3]
        + columns[:, 3:4] * vectors[4:5]
    )
    grad_out[...] = grad
    low_out[...] = grad.astype(bf16)
    sums[...] = column_sums(grad)


def gate_pass(own, other, tangent, partner_tangent, vectors):
    return pl.pallas_call(
        gate_kernel,
        out_shape=[
            shape_of((SEQ, D), f32),
            shape_of((SEQ, D), bf16),
            shape_of((SEQ, 128), f32),
            shape_of((1, D), f32),
        ],
        in_specs=[in_vmem] * 5,
        out_specs=[in_vmem] * 4,
        compiler_params=params(24),
        cost_estimate=pl.CostEstimate(
            flops=8 * SEQ * D, bytes_accessed=5 * MIB, transcendentals=2 * SEQ
        ),
        name="gate",
    )(own, other, tangent, partner_tangent, vectors)


def mix_kernel(own, other, columns, mixed, own_sums, other_sums):
    own_rows = own[...].astype(f32)
    other_rows = other[...].astype(f32)
    mixed[...] = (own_rows + columns[:, 0:1] * other_rows).astype(bf16)
    own_sums[...] = column_sums(columns[:, 1:2] * own_rows)
    other_sums[...] = column_sums(columns[:, 1:2] * other_rows)


def mix_pass(own, other, columns):
    return pl.pallas_call(
        mix_kernel,
        out_shape=[shape_of((SEQ, D), bf16), shape_of((1, D), f32), shape_of((1, D), f32)],
        in_specs=[in_vmem] * 3,
        out_specs=[in_vmem] * 3,
        compiler_params=params(24),
        cost_estimate=pl.CostEstimate(
            flops=6 * SEQ * D, bytes_accessed=3 * MIB, transcendentals=0
        ),
        name="mix",
    )(own, other, columns)


def chain_kernel(count, places, low, grad, slope, middle, gain, *rest):
    out_parts, up_parts, down_parts = (rest[k * count : (k + 1) * count] for k in range(3))
    upper_out, total_out, total_low_out, context_out, upper_sums, gain_sums, bias_sums = rest[
        3 * count : 3 * count + 7
    ]
    w_out, w_up, w_down, sems = rest[3 * count + 7 :]
    out_copies = part_copies(places, out_parts, w_out, sems.at[0])
    up_copies = part_copies(places, up_parts, w_up, sems.at[1])
    down_copies = part_copies(places, down_parts, w_down, sems.at[2])
    first_step = pl.program_id(0) == 0

    @pl.when(first_step)
    def _():
        start_all(down_copies)
        start_all(up_copies)
        start_all(out_copies)
        upper_sums[...] = jnp.zeros_like(upper_sums)
        gain_sums[...] = jnp.zeros_like(gain_sums)
        bias_sums[...] = jnp.zeros_like(bias_sums)
        wait_all(down_copies)
        wait_all(up_copies)

    incoming = low[...]
    normed_grad = jnp.zeros((ROWS, D), f32)
    size = 512
    for first in range(0, FF, size):
        part = slice(first, first + size)
        upper = dot_nt(incoming, w_down[part]) * slope[:, part].astype(f32)
        upper_sums[:, part] += column_sums(upper)
        upper_low = upper.astype(bf16)
        upper_out[:, part] = upper_low
        normed_grad += dot_nt(upper_low, w_up[:, part])
    scaled, root = normalise(middle[...])
    gain_sums[...] += column_sums(normed_grad * scaled)
    bias_sums[...] += column_sums(normed_grad)
    total = grad[...] + norm_back(scaled, root, gain[...], normed_grad)
    total_out[...] = total
    total_low = total.astype(bf16)
    total_low_out[...] = total_low

    @pl.when(first_step)
    def _():
        wait_all(out_copies)

    context_out[...] = dot_nt(total_low, w_out[...]).astype(bf16)


def chain_pass(places, low, grad, slope, middle, gain, outs, ups, downs):
    count = len(outs)
    by_rows = lambda width: pl.BlockSpec((ROWS, width), lambda step: (step, 0))
    whole = lambda dims: pl.BlockSpec(dims, lambda step: (0, 0))
    return pl.pallas_call(
        functools.partial(chain_kernel, count),
        grid=(SEQ // ROWS,),
        out_shape=[
            shape_of((SEQ, FF), bf16),
            shape_of((SEQ, D), f32),
            shape_of((SEQ, D), bf16),
            shape_of((SEQ, D), bf16),
            shape_of((1, FF), f32),
            shape_of((1, D), f32),
            shape_of((1, D), f32),
        ],
        in_specs=[in_smem, by_rows(D), by_rows(D), by_rows(FF), by_rows(D), whole((1, D))]
        + [in_any] * (3 * count),
        out_specs=[by_rows(FF), by_rows(D), by_rows(D), by_rows(D)]
        + [whole((1, FF)), whole((1, D)), whole((1, D))],
        scratch_shapes=[
            pltpu.VMEM((D, D), bf16),
            pltpu.VMEM((D, FF), bf16),
            pltpu.VMEM((FF, D), bf16),
            pltpu.SemaphoreType.DMA((3, count)),
        ],
        compiler_params=params(44),
        cost_estimate=pl.CostEstimate(
            flops=2 * SEQ * D * (D + 2 * FF), bytes_accessed=21 * MIB, transcendentals=0
        ),
        name="chain",
    )(places, low, grad, slope, middle, gain, *outs, *ups, *downs)


def slots_of(count):
    return (list(range(0, count, 2)), list(range(1, count, 2)))


def row_grads_kernel(count, widths, summed, places, left, *rest):
    sources = rest[: 2 if summed else 1]
    rest = rest[len(sources) :]
    if summed:
        pair_low = rest[0]
        rest = rest[1:]
    outs, whole = rest[:-1], rest[-1]
    near, far = slots_of(count)
    rows = D // count
    turned = left[...].T
    first = 0
    each = 2 if far else 1
    if summed:
        total = (sources[0][...] + sources[1][...].astype(f32)).astype(bf16)
        pair_low[...] = total
    for index, width in enumerate(widths):
        for low in range(first, first + width, WIDE):
            if summed:
                right = pair_low[low // WIDE]
            else:
                right = sources[0][:, low : low + WIDE]
            whole[:, low - first : low - first + WIDE] = dot(turned, right).astype(bf16)
        for out, slots in zip(outs[each * index : each * index + each], (near, far)):
            for place, slot in enumerate(slots):
                begin = pl.multiple_of(places[slot] * rows, 16)
                out[place] = whole[pl.ds(begin, rows), :width]
        first += width


def row_grads(places, left, sources, widths, count):
    near, far = slots_of(count)
    rows = D // count
    outs = []
    for width in widths:
        outs.append(shape_of((len(near), rows, width), bf16))
        if far:
            outs.append(shape_of((len(far), rows, width), bf16))
    summed = len(sources) == 2
    low = [shape_of((2, SEQ, WIDE), bf16)] if summed else []
    total = sum(widths)
    return pl.pallas_call(
        functools.partial(row_grads_kernel, count, widths, summed),
        out_shape=low + outs,
        in_specs=[in_smem] + [in_vmem] * (1 + len(sources)),
        out_specs=[in_vmem] * len(low + outs),
        scratch_shapes=[pltpu.VMEM((D, max(widths)), bf16)],
        compiler_params=params(32),
        cost_estimate=pl.CostEstimate(
            flops=2 * SEQ * D * total, bytes_accessed=2 * D * total + 2 * MIB, transcendentals=0
        ),
        name="row_grads",
    )(places, left, *sources)


def down_grads_kernel(count, heights, places, low, hidden, *outs):
    near, far = slots_of(count)
    width = FF // count
    each = 2 if far else 1
    first = 0
    for index, height in enumerate(heights):
        turned = low[:, first : first + height].T
        for out, slots in zip(outs[each * index : each * index + each], (near, far)):
            for place, slot in enumerate(slots):
                begin = pl.multiple_of(places[slot] * width, 128)
                out[place] = dot(turned, hidden[:, pl.ds(begin, width)]).astype(bf16)
        first += height


def down_grads(places, low, hidden, heights, count):
    near, far = slots_of(count)
    width = FF // count
    outs = []
    for height in heights:
        outs.append(shape_of((len(near), height, width), bf16))
        if far:
            outs.append(shape_of((len(far), height, width), bf16))
    return pl.pallas_call(
        functools.partial(down_grads_kernel, count, heights),
        out_shape=outs,
        in_specs=[in_smem] + [in_vmem] * 2,
        out_specs=[in_vmem] * len(outs),
        compiler_params=params(32),
        cost_estimate=pl.CostEstimate(
            flops=2 * SEQ * D * FF, bytes_accessed=9 * MIB, transcendentals=0
        ),
        name="down_grads",
    )(places, low, hidden)


def first_kernel(count, places, queries, pairs, total, rows, gain, *rest):
    parts = rest[:count]
    grad_out, gain_sums, bias_sums, weight, sems = rest[count:]
    copies = part_copies(places, parts, weight, sems)

    @pl.when(pl.program_id(0) == 0)
    def _():
        start_all(copies)
        gain_sums[...] = jnp.zeros_like(gain_sums)
        bias_sums[...] = jnp.zeros_like(bias_sums)
        wait_all(copies)

    normed_grad = jnp.zeros((ROWS, D), f32)
    for group in range(GROUPS):
        first = group * WIDE
        normed_grad += dot_nt(queries[group][...], weight[:, first : first + WIDE])
        for kind in range(2):
            start = (kind + 1) * D + first
            normed_grad += dot_nt(pairs[group][kind], weight[:, start : start + WIDE])
    scaled, root = normalise(rows[...].astype(f32))
    gain_sums[...] += column_sums(normed_grad * scaled)
    bias_sums[...] += column_sums(normed_grad)
    grad_out[...] = total[...] + norm_back(scaled, root, gain[...], normed_grad)


def first_pass(places, queries, pairs, total, rows, gain, parts):
    count = len(parts)
    by_rows = lambda width: pl.BlockSpec((ROWS, width), lambda step: (step, 0))
    whole = lambda dims: pl.BlockSpec(dims, lambda step: (0, 0))
    pair = pl.BlockSpec((2, ROWS, WIDE), lambda step: (0, step, 0))

    def kernel(places_ref, q0, q1, q2, p0, p1, p2, *rest):
        first_kernel(count, places_ref, (q0, q1, q2), (p0, p1, p2), *rest)

    return pl.pallas_call(
        kernel,
        grid=(SEQ // ROWS,),
        out_shape=[shape_of((SEQ, D), f32), shape_of((1, D), f32), shape_of((1, D), f32)],
        in_specs=[in_smem]
        + [by_rows(WIDE)] * GROUPS
        + [pair] * GROUPS
        + [by_rows(D), by_rows(D), whole((1, D))]
        + [in_any] * count,
        out_specs=[by_rows(D), whole((1, D)), whole((1, D))],
        scratch_shapes=[pltpu.VMEM((D, 3 * D), bf16), pltpu.SemaphoreType.DMA((count,))],
        compiler_params=params(24),
        cost_estimate=pl.CostEstimate(
            flops=2 * SEQ * D * 3 * D, bytes_accessed=10 * MIB, transcendentals=0
        ),
        name="first",
    )(places, *queries, *pairs, total, rows, gain, *parts)


def swap_bit(value, axis, bit):
    size = lax.axis_size(axis)
    return lax.ppermute(value, axis, [(source, source ^ (1 << bit)) for source in range(size)])


def from_partner(value):
    size = lax.axis_size("stream")
    half = size // 2
    return lax.ppermute(value, "stream", [(source, (source + half) % size) for source in range(size)])


def add_low(left, right):
    return (left.astype(f32) + right.astype(f32)).astype(left.dtype)


def line_sum(value, inner):
    received = lax.ppermute(value, "dp", [(0, 1), (3, 2)])
    near = add_low(value, received)
    across = lax.ppermute(near, "dp", [(1, 2), (2, 1)])
    total = add_low(near, across)
    returned = lax.ppermute(total, "dp", [(1, 0), (2, 3)])
    return jnp.where(inner, total, returned)


def modality_groups():
    size = lax.axis_size("stream")
    half = size // 2
    return [list(range(half)), list(range(half, size))]


def body(
    regions,
    cotangent,
    page_lens,
    qkv_weight,
    out_weight,
    up_weight,
    down_weight,
    ln1_gain,
    ln1_bias,
    ln2_gain,
    ln2_bias,
    up_bias,
    down_bias,
    gate_own,
    gate_other,
):
    half = lax.axis_size("stream") // 2
    depth = lax.axis_size("dp")
    paired = half == 4 and depth == 4
    side = lax.axis_index("stream") % half
    floor = lax.axis_index("dp")
    inner = jnp.logical_and(floor > 0, floor < depth - 1)
    count = 4 if paired else 1
    slots = jnp.arange(count, dtype=jnp.int32)
    places = jnp.bitwise_xor(side.astype(jnp.int32), slots) if paired else slots

    def gather(shard):
        if not paired:
            return [
                lax.all_gather(shard, "stream", axis_index_groups=modality_groups(), tiled=True)
            ]
        across = swap_bit(shard, "stream", 1)
        return [shard, swap_bit(shard, "stream", 0), across, swap_bit(across, "stream", 0)]

    short = (ln1_gain, ln1_bias, ln2_gain, ln2_bias, down_bias, gate_own, gate_other, up_bias)
    packed = jnp.concatenate([member.astype(bf16) for member in short])[None]
    qkv_low = qkv_weight.astype(bf16)
    if paired:
        padded = jnp.pad(packed, ((0, 15), (0, 3 * D - packed.shape[1])))
        qkv_parts = gather(jnp.concatenate([qkv_low, padded], axis=0))
        rows_qkv = qkv_low.shape[0]
        found = jnp.stack([part[rows_qkv, : packed.shape[1]] for part in qkv_parts]).astype(f32)
        picks = places[None, :] == slots[:, None]
        found = jnp.sum(jnp.where(picks[:, :, None], found[None], 0.0), axis=1)
    else:
        qkv_parts = gather(qkv_low)
        found = gather(packed)[0].astype(f32)
    partner_tangent = from_partner(cotangent)
    out_parts = gather(out_weight.astype(bf16))
    up_parts = gather(up_weight.astype(bf16))
    down_parts = gather(down_weight.astype(bf16))
    vectors = []
    offset = 0
    for member in short:
        vectors.append(found[:, offset : offset + member.size].reshape(1, -1))
        offset += member.size
    gain_one, bias_one, gain_two, bias_two, output_bias, gate_self, gate_cross, hidden_bias = vectors
    partner_cross = from_partner(gate_cross.astype(bf16)).astype(f32)
    middle_vectors = jnp.concatenate(
        [gain_two, bias_two, output_bias, gate_self, partner_cross, jnp.zeros((3, D), f32)], axis=0
    )

    lengths = lax.dynamic_slice_in_dim(page_lens, side * depth + floor, 1, 0)
    positions = jnp.arange(SEQ, dtype=jnp.int32)
    page_ends = jnp.cumsum(lengths[0], dtype=jnp.int32)
    pages = jnp.sum((page_ends[:, None] <= positions[None, :]).astype(jnp.int32), axis=0)
    page_row, page_column = pages[None, :], pages[:, None]

    queries, own_pairs, normed = project(places, regions, gain_one, bias_one, qkv_parts)
    other_pairs = [from_partner(pair) for pair in own_pairs]
    contexts, logs = [], []
    for group in range(GROUPS):
        context, log_total = attend(
            group, queries, own_pairs[group], other_pairs[group], page_row, page_column
        )
        contexts.append(context)
        logs.append(log_total)
    middle, second, hidden, slope, modal, inner_own = middle_pass(
        places,
        regions,
        contexts,
        partner_tangent,
        middle_vectors,
        hidden_bias,
        out_parts,
        up_parts,
        down_parts,
    )
    inner_other = from_partner(inner_own)
    modal_grad, modal_low, columns, output_bias_grad = gate_pass(
        inner_own, inner_other, cotangent, partner_tangent, middle_vectors
    )
    partner_modal = from_partner(modal)
    mixed_rows, gate_self_grad, gate_cross_grad = mix_pass(modal, partner_modal, columns)

    def settle(near, far=None):
        if far is None:
            return near
        received = swap_bit(far, "stream", 0)
        away = add_low(near[1], received[1])
        across = swap_bit(away, "stream", 1)
        mine = add_low(add_low(near[0], received[0]), across)
        return line_sum(mine, inner)

    def settle_all(flat):
        each = 2 if paired else 1
        return [settle(*flat[k : k + each]) for k in range(0, len(flat), each)]

    heights = [384, 384] if paired else [D]
    down_sums = settle_all(down_grads(places, modal_low, hidden, heights, count))
    upper_low, middle_grad, middle_low, context_grad, hidden_bias_grad, gain_two_grad, bias_two_grad = (
        chain_pass(
            places,
            modal_low,
            modal_grad,
            slope,
            middle,
            gain_two,
            out_parts,
            up_parts,
            down_parts,
        )
    )
    widths = [FF // 2, FF // 2] if paired else [FF]
    up_sums = settle_all(row_grads(places, second, [upper_low], widths, count))
    context_all = jnp.concatenate(contexts, axis=1)
    out_sums = settle_all(row_grads(places, context_all, [middle_low], [D], count))
    query_grads, own_grads, returned = [], [], []
    for group in range(GROUPS):
        query_grad, own_grad, other_grad = attend_back(
            group,
            queries,
            own_pairs[group],
            other_pairs[group],
            context_grad,
            logs[group],
            page_row,
            page_column,
        )
        query_grads.append(query_grad)
        own_grads.append(own_grad)
        returned.append(from_partner(other_grad))
    query_all = jnp.concatenate(query_grads, axis=1)
    query_sums = settle_all(row_grads(places, normed, [query_all], [D], count))
    pair_grads, pair_sums = [], []
    for group in range(GROUPS):
        pair_grad, *flat = row_grads(
            places, normed, [own_grads[group], returned[group]], [2 * WIDE], count
        )
        pair_grads.append(pair_grad)
        pair_sums += settle_all(flat)
    region_grad, gain_one_grad, bias_one_grad = first_pass(
        places, query_grads, pair_grads, middle_grad, regions, gain_one, qkv_parts
    )

    short_grads = (
        gain_one_grad,
        bias_one_grad,
        gain_two_grad,
        bias_two_grad,
        output_bias_grad,
        gate_self_grad,
        gate_cross_grad,
        hidden_bias_grad,
    )
    short_sum = jnp.concatenate([member.reshape(half, -1) for member in short_grads], axis=1)
    if paired:
        short_sum = short_sum + swap_bit(short_sum, "stream", 0)
        short_sum = short_sum + swap_bit(short_sum, "stream", 1)
        short_sum = line_sum(short_sum, inner)
    else:
        short_sum = lax.psum(
            lax.psum(short_sum, "stream", axis_index_groups=modality_groups()), "dp"
        )
    short_own = lax.dynamic_slice_in_dim(short_sum, side, 1, 0)[0]
    short_outs = []
    offset = 0
    for member in short:
        short_outs.append(short_own[offset : offset + member.size])
        offset += member.size

    def finish(blocks):
        if paired:
            return blocks
        groups = modality_groups()
        return [
            lax.psum(
                lax.psum_scatter(
                    block[0].astype(f32), "stream", axis_index_groups=groups, tiled=True
                ),
                "dp",
            )
            for block in blocks
        ]

    if paired:
        down_grad = jnp.concatenate(down_sums, axis=0).T.astype(f32)
    else:
        down_grad = finish([down_sums[0].transpose(0, 2, 1)])[0]
    up_grad = jnp.concatenate(finish(up_sums), axis=1).astype(f32)
    out_grad = jnp.concatenate(finish(out_sums), axis=1).astype(f32)
    pair_sums = finish(pair_sums)
    qkv_grad = jnp.concatenate(
        finish(query_sums)
        + [block[:, :WIDE] for block in pair_sums]
        + [block[:, WIDE:] for block in pair_sums],
        axis=1,
    ).astype(f32)
    short_by = short_outs[:6]
    return (
        mixed_rows,
        region_grad,
        qkv_grad,
        out_grad,
        up_grad,
        down_grad,
        short_outs[0],
        short_outs[1],
        short_outs[2],
        short_outs[3],
        short_outs[7],
        short_outs[4],
        short_outs[5],
        short_outs[6],
    )


def solution(mesh):
    in_specs = (
        P(("stream", "dp"), None),
        P(("stream", "dp"), None),
        P(),
        P("stream", None),
        P("stream", None),
        P("stream", None),
        P("stream", None),
        P("stream"),
        P("stream"),
        P("stream"),
        P("stream"),
        P("stream"),
        P("stream"),
        P("stream"),
        P("stream"),
    )
    out_specs = (
        P(("stream", "dp"), None),
        P(("stream", "dp"), None),
        P("stream", None),
        P("stream", None),
        P("stream", None),
        P("stream", None),
        P("stream"),
        P("stream"),
        P("stream"),
        P("stream"),
        P("stream"),
        P("stream"),
        P("stream"),
        P("stream"),
    )
    return jax.shard_map(body, mesh=mesh, in_specs=in_specs, out_specs=out_specs, check_vma=False)
```

time: 2080 us -> 472 us (0.23)
  waiting for transfers between devices: 1470 us -> 217 us
  local copies, waits for them, and re-layouts: 233 us -> 32.8 us
  other arithmetic: 221 us -> 31.4 us
  matrix products: 123 us -> 0 us
  Pallas kernels: 0 us -> 97.9 us
  starting transfers between devices: 10.2 us -> 81.7 us
    psum x1 -> x0, waiting for transfers between devices: 936 us -> none  [body(): flat = lax.psum(flat, 'dp')]
    ppermute x8 -> x72, waiting for transfers between devices: 535 us -> 217 us  [the longest x10 91.4 us: line_sum(): returned = lax.ppermute(total, 'dp', [(1, 0), (2, 3)])]
    select_n x4 -> x8, other arithmetic: 130 us -> 2.48 us  [line_sum(): return jnp.where(inner, total, returned)]
    dot_general x18 -> x0, matrix products: 123 us -> none  [the longest x1 18.5 us: pack_backward(): jnp.einsum('qhd,khd->hqk', grad_rows, value_rows, preferred_element_type=...]
    pallas_call x0 -> x19, Pallas kernels: none -> 97.9 us  [the longest x3 20.5 us: attend_back(): pl.pallas_call(attend_back_kernel, grid=(steps,), out_shape=[shape_of((SE...]
    slice x15 -> x7, local copies, waits for them, and re-layouts: 78.4 us -> 2.2 us  [the longest x2 1.33 us: body(): short_outs.append(short_own[offset:offset + member.size])]
    ppermute x8 -> x72, starting transfers between devices: 10.1 us -> 81.7 us  [the longest x10 25.9 us: line_sum(): received = lax.ppermute(value, 'dp', [(0, 1), (3, 2)])]
    reshape x22 -> x14, local copies, waits for them, and re-layouts: 68.2 us -> 1.06 us  [the longest x8 0.56 us: body(): member.reshape(half, -1)]
  transfers between devices with their start and end apart: 9 -> 72, of which waited for: 9 -> 25; matrix products, arithmetic and copies ran while one was open for 5% -> 6% of each run, Pallas kernels for 0% -> 12%
where the time goes in v1:
time: 472 us; the launch traced here: 463 us
  waiting for transfers between devices  217 us (46%)
  Pallas kernels  97.9 us (21%)
  starting transfers between devices  81.7 us (17%)
  local copies, waits for them, and re-layouts  32.8 us (7%)
  other arithmetic  31.4 us (7%)
    ppermute x10, waiting for transfers between devices, line_sum(): returned = lax.ppermute(total, 'dp', [(1, 0), (2, 3)])  91.4 us
    ppermute x32, waiting for transfers between devices, swap_bit(): lax.ppermute(value, axis, [(source, source ^ 1 << bit) for source in rang...  73.4 us
    ppermute x10, waiting for transfers between devices, line_sum(): received = lax.ppermute(value, 'dp', [(0, 1), (3, 2)])  38.3 us
    unnamed x150, local copies, waits for them, and re-layouts  27.7 us
    ppermute x10, starting transfers between devices, line_sum(): received = lax.ppermute(value, 'dp', [(0, 1), (3, 2)])  25.9 us
    ppermute x32, starting transfers between devices, swap_bit(): lax.ppermute(value, axis, [(source, source ^ 1 << bit) for source in rang...  22.9 us
    pallas_call x3, Pallas kernels, attend_back(): pl.pallas_call(attend_back_kernel, grid=(steps,), out_shape=[shape_of((SE...  20.5 us
    pallas_call x1, Pallas kernels, middle_pass(): pl.pallas_call(kernel, grid=(SEQ // ROWS,), out_shape=[shape_of((SEQ, D),...  16.9 us
  transfers between devices with their start and end apart: 72, of which 25 were waited for; matrix products, arithmetic and copies ran while one was open for 6% of the time, Pallas kernels for 12%

profile of v1, /device:TPU:0, one launch (start us, length us, event | category | flops | bytes accessed | tf_op | source)
XLA Modules:
  0.0 463.3 jit_solution(14063962407967739878)
XLA Ops:
  8.0 3.0 collective-permute-start.1
  11.0 21.2 %collective-permute-done.1.rest_2_.rest_5_ = bf16[208,2304]{1,0:T(8,128)(2,1)S(1)} collective-permute-done((bf16[208,2304]{1,0:T(8,128)(2,1)S(1)}, bf16[208,2304]{1,0:T(8,128)(2,1)S(1)}, u32[]{:S(2)}, u32[]{:S(2)}) %collective-permute-start.1) | collective-permute-done | bytes 958496 | tf_op jit(solution)/shard_map/ppermute | solution.py:693
  36.0 2.9 convert_element_type.597.rest_11_.rest_8_
  46.5 4.7 %project.1 = (bf16[512,768]{1,0:T(8,128)(2,1)S(1)}, bf16[2,512,256]{2,1,0:T(8,128)(2,1)}, bf16[2,512,256]{2,1,0:T(8,128)(2,1)S(1)}, bf16[2,512,256]{2,1,0:T(8,128)(2,1)S(1)}, bf16[512,768]{1,0:T(8,128)(2,1)S(1)}) custom-call(s32[4]{0:T(128)S(1)} %iota_xor_fusion.places.places_ref, bf16[512,768]{1,0:T(8,128)(2,1)S(1)} %copy-done.25, ...), custom_call_target="tpu_custom_call" | custom-call | flops 1811939328 | bytes 7340032 | tf_op jit(solution)/shard_map/project/pallas_call | solution.py:129
  58.3 9.8 %collective-permute-done.12.rest_9_.rest_6_ = bf16[192,3072]{1,0:T(8,128)(2,1)} collective-permute-done((bf16[192,3072]{1,0:T(8,128)(2,1)}, bf16[192,3072]{1,0:T(8,128)(2,1)}, u32[]{:S(2)}, u32[]{:S(2)}) %collective-permute-start.12) | collective-permute-done | bytes 1179680 | tf_op jit(solution)/shard_map/ppermute | solution.py:693
  69.8 22.6 %collective-permute-done.15.rest_13_.rest_10_ = bf16[768,768]{1,0:T(8,128)(2,1)} collective-permute-done((bf16[768,768]{1,0:T(8,128)(2,1)}, bf16[768,768]{1,0:T(8,128)(2,1)}, u32[]{:S(2)}, u32[]{:S(2)}) %collective-permute-start.15) | collective-permute-done | bytes 1179680 | tf_op jit(solution)/shard_map/ppermute | solution.py:693
  97.0 4.9 %attend.3 = (bf16[512,256]{1,0:T(8,128)(2,1)S(1)}, f32[2,2,512]{2,1,0:T(2,128)S(1)}) custom-call(bf16[512,768]{1,0:T(8,128)(2,1)S(1)} %get-tuple-element.78.query, bf16[2,512,256]{2,1,0:T(8,128)(2,1)} %get-tuple-element.79.key.value, bf16[2,512,256]{2,1,0:T(8,128)(2,1)} %get-tuple-element.79.key.value, ...), custom_call_target="tpu_custom_call" | custom-call | flops 268435456 | bytes 2097152 | tf_op jit(solution)/shard_map/attend/pallas_call | solution.py:214
  101.8 4.0 attend.4
  105.9 4.0 attend.5
  110.0 3.4 collective-permute-done.6.rest_0_.partner_tangent
  113.5 16.9 %middle.1 = (f32[512,768]{1,0:T(8,128)}, bf16[512,768]{1,0:T(8,128)(2,1)S(1)}, bf16[512,3072]{1,0:T(8,128)(2,1)}, bf16[512,3072]{1,0:T(8,128)(2,1)}, bf16[512,768]{1,0:T(8,128)(2,1)S(1)}, /*index=5*/f32[8,512]{1,0:T(8,128)S(1)}) custom-call(s32[4]{0:T(128)S(1)} %iota_xor_fusion.places.places_ref, bf16[512,768]{1,0:T(8,128)(2,1)S(1)} %copy-done.26, ...), custom_call_target="tpu_custom_call" | custom-call | flops 5435817984 | bytes 22020096 | tf_op jit(solution)/shard_map/middle/pallas_call | solution.py:367
  132.2 2.0 collective-permute-done.18.other
  134.2 1.9 gate.1
  138.0 15.1 %chain.1 = (bf16[512,3072]{1,0:T(8,128)(2,1)}, f32[512,768]{1,0:T(8,128)}, bf16[512,768]{1,0:T(8,128)(2,1)S(1)}, bf16[512,768]{1,0:T(8,128)(2,1)S(1)}, f32[1,307...) custom-call(s32[4]{0:T(128)S(1)} %iota_xor_fusion.places.places_ref, ...), custom_call_target="tpu_custom_call" | custom-call | flops 5435817984 | bytes 22020096 | tf_op jit(solution)/shard_map/chain/pallas_call | solution.py:515
  153.1 7.6 %attend_back.3 = (bf16[512,256]{1,0:T(8,128)(2,1)S(1)}, f32[2,512,256]{2,1,0:T(8,128)S(1)}, bf16[2,512,256]{2,1,0:T(8,128)(2,1)}) custom-call(bf16[512,768]{1,0:T(8,128)(2,1)S(1)} %get-tuple-element.78.query, bf16[2,512,256]{2,1,0:T(8,128)(2,1)} %get-tuple-element.79.key.value, bf16[2,512,256]{2,1,0:T(8,128)(2,1)} %get-tuple-element.79.key.value, ...), custom_call_target="tpu_custom_call" | custom-call | flops 671088640 | bytes 4194304 | tf_op jit(solution)/shard_map/attend_back/pallas_call | solution.py:284
  164.8 6.7 %attend_back.4 = (bf16[512,256]{1,0:T(8,128)(2,1)S(1)}, f32[2,512,256]{2,1,0:T(8,128)S(1)}, bf16[2,512,256]{2,1,0:T(8,128)(2,1)}) custom-call(bf16[512,768]{1,0:T(8,128)(2,1)S(1)} %get-tuple-element.78.query, bf16[2,512,256]{2,1,0:T(8,128)(2,1)S(1)} %get-tuple-element.81.key.value, bf16[2,512,256]{2,1,0:T(8,128)(2,1)S(1)} %get-tuple-element.81.key.value, ...), custom_call_target="tpu_custom_call" | custom-call | flops 671088640 | bytes 4194304 | tf_op jit(solution)/shard_map/attend_back/pallas_call | solution.py:284
  174.3 6.2 %attend_back.5 = (bf16[512,256]{1,0:T(8,128)(2,1)S(1)}, f32[2,512,256]{2,1,0:T(8,128)S(1)}, bf16[2,512,256]{2,1,0:T(8,128)(2,1)}) custom-call(bf16[512,768]{1,0:T(8,128)(2,1)S(1)} %get-tuple-element.78.query, bf16[2,512,256]{2,1,0:T(8,128)(2,1)S(1)} %get-tuple-element.83.key.value, bf16[2,512,256]{2,1,0:T(8,128)(2,1)S(1)} %get-tuple-element.83.key.value, ...), custom_call_target="tpu_custom_call" | custom-call | flops 671088640 | bytes 4194304 | tf_op jit(solution)/shard_map/attend_back/pallas_call | solution.py:284
  182.8 2.3 row_grads.9
  186.4 2.3 row_grads.10
  189.6 3.4 row_grads.11
  197.8 1.9 row_grads.6
  201.2 3.7 collective-permute-done.20.rest_1_
  205.0 1.9 row_grads.7
  208.4 4.9 %collective-permute-done.21.rest_1_ = bf16[2,512,256]{2,1,0:T(8,128)(2,1)} collective-permute-done((bf16[2,512,256]{2,1,0:T(8,128)(2,1)}, bf16[2,512,256]{2,1,0:T(8,128)(2,1)}, u32[]{:S(2)}, u32[]{:S(2)}) %collective-permute-start.21) | collective-permute-done | bytes 524320 | tf_op jit(solution)/shard_map/ppermute | solution.py:699
  216.6 6.4 %first.1 = (f32[512,768]{1,0:T(8,128)}, f32[1,768]{1,0:T(1,128)S(1)}, f32[1,768]{1,0:T(1,128)S(1)}) custom-call(s32[4]{0:T(128)S(1)} %iota_xor_fusion.places.places_ref, bf16[512,256]{1,0:T(8,128)(2,1)S(1)} %get-tuple-element.95.q0, bf16[512,256]{1,0:T(8,128)(2,1)S(1)} %copy-done.16, bf16[512,256]{1,0:T(8,128)(2,1)S(1)} %copy-done.18, ...), custom_call_target="tpu_custom_call" | custom-call | flops 1811939328 | bytes 10485760 | tf_op jit(solution)/shard_map/first/pallas_call | solution.py:672
  224.1 2.6 mix.1
  233.7 5.7 %collective-permute-done.68 = f32[4,2112]{1,0:T(4,128)S(1)} collective-permute-done((f32[4,2112]{1,0:T(4,128)S(1)}, f32[4,2112]{1,0:T(4,128)S(1)}, u32[]{:S(2)}, u32[]{:S(2)}) %collective-permute-start.68) | collective-permute-done | bytes 33824 | tf_op jit(solution)/shard_map/ppermute | solution.py:693
  239.4 3.7 collective-permute-start.69
  245.0 3.2 down_grads.1
  252.7 5.3 %collective-permute-start.24 = (bf16[192,768]{1,0:T(8,128)(2,1)S(1)}, bf16[192,768]{1,0:T(8,128)(2,1)S(1)}, u32[]{:S(2)}, u32[]{:S(2)}) collective-permute-start(bf16[192,768]{1,0:T(8,128)(2,1)S(1)} %fusion.15), channel_id=1, source_target_pairs={{0,1},{3,2},{4,5},{7,6},{8,9},{11,10},{12,13},{15,14},{16,17},{19,... | collective-permute-start | bytes 884744 | tf_op jit(solution)/shard_map/ppermute | solution.py:707
  259.5 4.5 collective-permute-done.71
  266.8 2.8 collective-permute-done.28
  271.2 5.2 %collective-permute-done.33 = bf16[192,512]{1,0:T(8,128)(2,1)S(1)} collective-permute-done((bf16[192,512]{1,0:T(8,128)(2,1)S(1)}, bf16[192,512]{1,0:T(8,128)(2,1)S(1)}, u32[]{:S(2)}, u32[]{:S(2)}) %collective-permute-start.33) | collective-permute-done | bytes 196640 | tf_op jit(solution)/shard_map/ppermute | solution.py:693
  278.0 4.1 collective-permute-done.38
  285.1 5.8 %collective-permute-done.44 = bf16[192,768]{1,0:T(8,128)(2,1)S(1)} collective-permute-done((bf16[192,768]{1,0:T(8,128)(2,1)S(1)}, bf16[192,768]{1,0:T(8,128)(2,1)S(1)}, u32[]{:S(2)}, u32[]{:S(2)}) %collective-permute-start.44) | collective-permute-done | bytes 294944 | tf_op jit(solution)/shard_map/ppermute | solution.py:707
  290.9 4.4 collective-permute-start.34
  309.3 32.3 %collective-permute-done.31 = bf16[192,512]{1,0:T(8,128)(2,1)S(1)} collective-permute-done((bf16[192,512]{1,0:T(8,128)(2,1)S(1)}, bf16[192,512]{1,0:T(8,128)(2,1)S(1)}, u32[]{:S(2)}, u32[]{:S(2)}) %collective-permute-start.31) | collective-permute-done | bytes 196640 | tf_op jit(solution)/shard_map/ppermute | solution.py:711
  343.0 6.9 %collective-permute-done.36 = bf16[192,512]{1,0:T(8,128)(2,1)S(1)} collective-permute-done((bf16[192,512]{1,0:T(8,128)(2,1)S(1)}, bf16[192,512]{1,0:T(8,128)(2,1)S(1)}, u32[]{:S(2)}, u32[]{:S(2)}) %collective-permute-start.36) | collective-permute-done | bytes 196640 | tf_op jit(solution)/shard_map/ppermute | solution.py:711
  351.2 7.8 %collective-permute-done.41 = bf16[192,512]{1,0:T(8,128)(2,1)S(1)} collective-permute-done((bf16[192,512]{1,0:T(8,128)(2,1)S(1)}, bf16[192,512]{1,0:T(8,128)(2,1)S(1)}, u32[]{:S(2)}, u32[]{:S(2)}) %collective-permute-start.41) | collective-permute-done | bytes 196640 | tf_op jit(solution)/shard_map/ppermute | solution.py:711
  363.0 4.6 collective-permute-start.54
  375.8 5.6 %collective-permute-done.54 = bf16[192,1536]{1,0:T(8,128)(2,1)S(1)} collective-permute-done((bf16[192,1536]{1,0:T(8,128)(2,1)S(1)}, bf16[192,1536]{1,0:T(8,128)(2,1)S(1)}, u32[]{:S(2)}, u32[]{:S(2)}) %collective-permute-start.54) | collective-permute-done | bytes 589856 | tf_op jit(solution)/shard_map/ppermute | solution.py:707
  382.2 11.8 %collective-permute-done.49 = bf16[192,1536]{1,0:T(8,128)(2,1)S(1)} collective-permute-done((bf16[192,1536]{1,0:T(8,128)(2,1)S(1)}, bf16[192,1536]{1,0:T(8,128)(2,1)S(1)}, u32[]{:S(2)}, u32[]{:S(2)}) %collective-permute-start.49) | collective-permute-done | bytes 589856 | tf_op jit(solution)/shard_map/ppermute | solution.py:707
  394.8 9.2 %collective-permute-done.64 = bf16[384,768]{1,0:T(8,128)(2,1)S(1)} collective-permute-done((bf16[384,768]{1,0:T(8,128)(2,1)S(1)}, bf16[384,768]{1,0:T(8,128)(2,1)S(1)}, u32[]{:S(2)}, u32[]{:S(2)}) %collective-permute-start.64) | collective-permute-done | bytes 589856 | tf_op jit(solution)/shard_map/ppermute | solution.py:707
  404.8 5.5 %collective-permute-done.59 = bf16[384,768]{1,0:T(8,128)(2,1)S(1)} collective-permute-done((bf16[384,768]{1,0:T(8,128)(2,1)S(1)}, bf16[384,768]{1,0:T(8,128)(2,1)S(1)}, u32[]{:S(2)}, u32[]{:S(2)}) %collective-permute-start.59) | collective-permute-done | bytes 589856 | tf_op jit(solution)/shard_map/ppermute | solution.py:707
  417.0 27.8 %collective-permute-done.66 = bf16[384,768]{1,0:T(8,128)(2,1)S(1)} collective-permute-done((bf16[384,768]{1,0:T(8,128)(2,1)S(1)}, bf16[384,768]{1,0:T(8,128)(2,1)S(1)}, u32[]{:S(2)}, u32[]{:S(2)}) %collective-permute-start.66) | collective-permute-done | bytes 589856 | tf_op jit(solution)/shard_map/ppermute | solution.py:711
  444.8 9.0 %collective-permute-done.61 = bf16[384,768]{1,0:T(8,128)(2,1)S(1)} collective-permute-done((bf16[384,768]{1,0:T(8,128)(2,1)S(1)}, bf16[384,768]{1,0:T(8,128)(2,1)S(1)}, u32[]{:S(2)}, u32[]{:S(2)}) %collective-permute-start.61) | collective-permute-done | bytes 589856 | tf_op jit(solution)/shard_map/ppermute | solution.py:711
  454.1 2.0 copy.46
  457.2 3.1 collective-permute-done.51
  (380 shorter events, 124.3 us)
Async XLA Ops:
  8.0 24.2 %collective-permute-start.1 = (bf16[208,2304]{1,0:T(8,128)(2,1)S(1)}, bf16[208,2304]{1,0:T(8,128)(2,1)S(1)}, u32[]{:S(2)}, u32[]{:S(2)}) collective-permute-start(bf16[208,2304]{1,0:T(8,128)(2,1)S(1)} %fusion.5.rest_0_.rest_3_), channel_id=1, source_target_pairs={{0,8},{4,12},{8,0},{12,4},{16,24},{20,28},{24,16},{28,20},{1,9},{5... | collective-permute-start | bytes 2875400 | tf_op jit(solution)/shard_map/ppermute | solution.py:693
  11.0 28.0 %collective-permute-start = (bf16[208,2304]{1,0:T(8,128)(2,1)S(1)}, bf16[208,2304]{1,0:T(8,128)(2,1)S(1)}, u32[]{:S(2)}, u32[]{:S(2)}) collective-permute-start(bf16[208,2304]{1,0:T(8,128)(2,1)S(1)} %fusion.5.rest_0_.rest_3_), channel_id=1, source_target_pairs={{0,4},{4,0},{8,12},{12,8},{16,20},{20,16},{24,28},{28,24},{1,5},{5... | collective-permute-start | bytes 2875400 | tf_op jit(solution)/shard_map/ppermute | solution.py:693
  32.2 9.5 %collective-permute-start.2 = (bf16[208,2304]{1,0:T(8,128)(2,1)S(1)}, bf16[208,2304]{1,0:T(8,128)(2,1)}, u32[]{:S(2)}, u32[]{:S(2)}) collective-permute-start(bf16[208,2304]{1,0:T(8,128)(2,1)S(1)} %collective-permute-done.1.rest_2_.rest_5_), channel_id=1, source_target_pairs={{0,4},{4,0},{8,12},{12,8},{16,20},{20,16},{24,28},{28,24},{1,5},{5... | collective-permute-start | bytes 2875400 | tf_op jit(solution)/shard_map/ppermute | solution.py:693
  32.2 21.4 %collective-permute-start.8 = (bf16[192,768]{1,0:T(8,128)(2,1)S(1)}, bf16[192,768]{1,0:T(8,128)(2,1)}, u32[]{:S(2)}, u32[]{:S(2)}) collective-permute-start(bf16[192,768]{1,0:T(8,128)(2,1)S(1)} %convert_element_type.595.rest_3_.rest_0_), channel_id=1, source_target_pairs={{0,4},{4,0},{8,12},{12,8},{16,20},{20,16},{24,28},{28,24},{1,5},{5... | collective-permute-start | bytes 884744 | tf_op jit(solution)/shard_map/ppermute | solution.py:693
  32.8 21.3 %collective-permute-start.9 = (bf16[192,768]{1,0:T(8,128)(2,1)S(1)}, bf16[192,768]{1,0:T(8,128)(2,1)}, u32[]{:S(2)}, u32[]{:S(2)}) collective-permute-start(bf16[192,768]{1,0:T(8,128)(2,1)S(1)} %convert_element_type.595.rest_3_.rest_0_), channel_id=1, source_target_pairs={{0,8},{4,12},{8,0},{12,4},{16,24},{20,28},{24,16},{28,20},{1,9},{5... | collective-permute-start | bytes 884744 | tf_op jit(solution)/shard_map/ppermute | solution.py:693
  35.7 32.3 %collective-permute-start.12 = (bf16[192,3072]{1,0:T(8,128)(2,1)}, bf16[192,3072]{1,0:T(8,128)(2,1)}, u32[]{:S(2)}, u32[]{:S(2)}) collective-permute-start(bf16[192,3072]{1,0:T(8,128)(2,1)} %convert_element_type.596.rest_7_.rest_4_), channel_id=1, source_target_pairs={{0,8},{4,12},{8,0},{12,4},{16,24},{20,28},{24,16},{28,20},{1,9},{5... | collective-permute-start | bytes 3538952 | tf_op jit(solution)/shard_map/ppermute | solution.py:693
  38.9 53.5 %collective-permute-start.15 = (bf16[768,768]{1,0:T(8,128)(2,1)}, bf16[768,768]{1,0:T(8,128)(2,1)}, u32[]{:S(2)}, u32[]{:S(2)}) collective-permute-start(bf16[768,768]{1,0:T(8,128)(2,1)} %convert_element_type.597.rest_11_.rest_8_), channel_id=1, source_target_pairs={{0,8},{4,12},{8,0},{12,4},{16,24},{20,28},{24,16},{28,20},{1,9},{5... | collective-permute-start | bytes 3538952 | tf_op jit(solution)/shard_map/ppermute | solution.py:693
  52.1 40.9 %collective-permute-start.3 = (bf16[2,512,256]{2,1,0:T(8,128)(2,1)}, bf16[2,512,256]{2,1,0:T(8,128)(2,1)}, u32[]{:S(2)}, u32[]{:S(2)}) collective-permute-start(bf16[2,512,256]{2,1,0:T(8,128)(2,1)} %get-tuple-element.79.key.value), channel_id=1, source_target_pairs={{0,16},{4,20},{8,24},{12,28},{16,0},{20,4},{24,8},{28,12},{1,17},{... | collective-permute-start | bytes 1572872 | tf_op jit(solution)/shard_map/ppermute | solution.py:699
  53.6 39.4 %collective-permute-start.4 = (bf16[2,512,256]{2,1,0:T(8,128)(2,1)S(1)}, bf16[2,512,256]{2,1,0:T(8,128)(2,1)S(1)}, u32[]{:S(2)}, u32[]{:S(2)}) collective-permute-start(bf16[2,512,256]{2,1,0:T(8,128)(2,1)S(1)} %get-tuple-element.81.key.value), channel_id=1, source_target_pairs={{0,16},{4,20},{8,24},{12,28},{16,0},{20,4},{24,8},{28,12},{1,17},{... | collective-permute-start | bytes 1572872 | tf_op jit(solution)/shard_map/ppermute | solution.py:699
  56.7 36.8 %collective-permute-start.5 = (bf16[2,512,256]{2,1,0:T(8,128)(2,1)S(1)}, bf16[2,512,256]{2,1,0:T(8,128)(2,1)S(1)}, u32[]{:S(2)}, u32[]{:S(2)}) collective-permute-start(bf16[2,512,256]{2,1,0:T(8,128)(2,1)S(1)} %get-tuple-element.83.key.value), channel_id=1, source_target_pairs={{0,16},{4,20},{8,24},{12,28},{16,0},{20,4},{24,8},{28,12},{1,17},{... | collective-permute-start | bytes 1572872 | tf_op jit(solution)/shard_map/ppermute | solution.py:699
  68.1 24.4 %collective-permute-start.7 = (bf16[1,768]{1,0:T(2,128)(2,1)S(1)}, bf16[1,768]{1,0:T(2,128)(2,1)S(1)}, u32[]{:S(2)}, u32[]{:S(2)}) collective-permute-start(bf16[1,768]{1,0:T(2,128)(2,1)S(1)} %convert_element_type.593), channel_id=1, source_target_pairs={{0,16},{4,20},{8,24},{12,28},{16,0},{20,4},{24,8},{28,12},{1,17},{... | collective-permute-start | bytes 4616 | tf_op jit(solution)/shard_map/ppermute | solution.py:699
  92.5 20.9 %collective-permute-start.11 = (bf16[192,3072]{1,0:T(8,128)(2,1)}, bf16[192,3072]{1,0:T(8,128)(2,1)}, u32[]{:S(2)}, u32[]{:S(2)}) collective-permute-start(bf16[192,3072]{1,0:T(8,128)(2,1)} %convert_element_type.596.rest_7_.rest_4_), channel_id=1, source_target_pairs={{0,4},{4,0},{8,12},{12,8},{16,20},{20,16},{24,28},{28,24},{1,5},{5... | collective-permute-start | bytes 3538952 | tf_op jit(solution)/shard_map/ppermute | solution.py:693
  92.5 20.9 %collective-permute-start.14 = (bf16[768,768]{1,0:T(8,128)(2,1)}, bf16[768,768]{1,0:T(8,128)(2,1)}, u32[]{:S(2)}, u32[]{:S(2)}) collective-permute-start(bf16[768,768]{1,0:T(8,128)(2,1)} %convert_element_type.597.rest_11_.rest_8_), channel_id=1, source_target_pairs={{0,4},{4,0},{8,12},{12,8},{16,20},{20,16},{24,28},{28,24},{1,5},{5... | collective-permute-start | bytes 3538952 | tf_op jit(solution)/shard_map/ppermute | solution.py:693
  93.0 20.4 %collective-permute-start.13 = (bf16[192,3072]{1,0:T(8,128)(2,1)}, bf16[192,3072]{1,0:T(8,128)(2,1)}, u32[]{:S(2)}, u32[]{:S(2)}) collective-permute-start(bf16[192,3072]{1,0:T(8,128)(2,1)} %collective-permute-done.12.rest_9_.rest_6_), channel_id=1, source_target_pairs={{0,4},{4,0},{8,12},{12,8},{16,20},{20,16},{24,28},{28,24},{1,5},{5... | collective-permute-start | bytes 3538952 | tf_op jit(solution)/shard_map/ppermute | solution.py:693
  93.1 20.3 %collective-permute-start.16 = (bf16[768,768]{1,0:T(8,128)(2,1)}, bf16[768,768]{1,0:T(8,128)(2,1)}, u32[]{:S(2)}, u32[]{:S(2)}) collective-permute-start(bf16[768,768]{1,0:T(8,128)(2,1)} %collective-permute-done.15.rest_13_.rest_10_), channel_id=1, source_target_pairs={{0,4},{4,0},{8,12},{12,8},{16,20},{20,16},{24,28},{28,24},{1,5},{5... | collective-permute-start | bytes 3538952 | tf_op jit(solution)/shard_map/ppermute | solution.py:693
  93.5 19.9 %collective-permute-start.6 = (bf16[512,768]{1,0:T(8,128)(2,1)}, bf16[512,768]{1,0:T(8,128)(2,1)}, u32[]{:S(2)}, u32[]{:S(2)}) collective-permute-start(bf16[512,768]{1,0:T(8,128)(2,1)} %tangent.1), channel_id=1, source_target_pairs={{0,16},{4,20},{8,24},{12,28},{16,0},{20,4},{24,8},{28,12},{1,17},{... | collective-permute-start | bytes 2359304 | tf_op jit(solution)/shard_map/ppermute | solution.py:699
  161.7 27.9 %collective-permute-start.19 = (bf16[2,512,256]{2,1,0:T(8,128)(2,1)}, bf16[2,512,256]{2,1,0:T(8,128)(2,1)}, u32[]{:S(2)}, u32[]{:S(2)}) collective-permute-start(bf16[2,512,256]{2,1,0:T(8,128)(2,1)} %get-tuple-element.102), channel_id=1, source_target_pairs={{0,16},{4,20},{8,24},{12,28},{16,0},{20,4},{24,8},{28,12},{1,17},{... | collective-permute-start | bytes 1572872 | tf_op jit(solution)/shard_map/ppermute | solution.py:699
  163.4 59.8 %collective-permute-start.17 = (bf16[512,768]{1,0:T(8,128)(2,1)}, bf16[512,768]{1,0:T(8,128)(2,1)}, u32[]{:S(2)}, u32[]{:S(2)}) collective-permute-start(bf16[512,768]{1,0:T(8,128)(2,1)} %copy-done.28), channel_id=1, source_target_pairs={{0,16},{4,20},{8,24},{12,28},{16,0},{20,4},{24,8},{28,12},{1,17},{... | collective-permute-start | bytes 2359304 | tf_op jit(solution)/shard_map/ppermute | solution.py:699
  172.5 32.4 %collective-permute-start.20 = (bf16[2,512,256]{2,1,0:T(8,128)(2,1)}, bf16[2,512,256]{2,1,0:T(8,128)(2,1)}, u32[]{:S(2)}, u32[]{:S(2)}) collective-permute-start(bf16[2,512,256]{2,1,0:T(8,128)(2,1)} %get-tuple-element.105), channel_id=1, source_target_pairs={{0,16},{4,20},{8,24},{12,28},{16,0},{20,4},{24,8},{28,12},{1,17},{... | collective-permute-start | bytes 1572872 | tf_op jit(solution)/shard_map/ppermute | solution.py:699
  181.6 31.7 %collective-permute-start.21 = (bf16[2,512,256]{2,1,0:T(8,128)(2,1)}, bf16[2,512,256]{2,1,0:T(8,128)(2,1)}, u32[]{:S(2)}, u32[]{:S(2)}) collective-permute-start(bf16[2,512,256]{2,1,0:T(8,128)(2,1)} %get-tuple-element.108), channel_id=1, source_target_pairs={{0,16},{4,20},{8,24},{12,28},{16,0},{20,4},{24,8},{28,12},{1,17},{... | collective-permute-start | bytes 1572872 | tf_op jit(solution)/shard_map/ppermute | solution.py:699
  185.9 41.7 %collective-permute-start.22 = (bf16[2,192,768]{2,1,0:T(8,128)(2,1)}, bf16[2,192,768]{2,1,0:T(8,128)(2,1)}, u32[]{:S(2)}, u32[]{:S(2)}) collective-permute-start(bf16[2,192,768]{2,1,0:T(8,128)(2,1)} %get-tuple-element.113), channel_id=1, source_target_pairs={{0,4},{4,0},{8,12},{12,8},{16,20},{20,16},{24,28},{28,24},{1,5},{5... | collective-permute-start | bytes 1769480 | tf_op jit(solution)/shard_map/ppermute | solution.py:693
  189.6 41.3 %collective-permute-start.42 = (bf16[2,192,768]{2,1,0:T(8,128)(2,1)}, bf16[2,192,768]{2,1,0:T(8,128)(2,1)}, u32[]{:S(2)}, u32[]{:S(2)}) collective-permute-start(bf16[2,192,768]{2,1,0:T(8,128)(2,1)} %get-tuple-element.122), channel_id=1, source_target_pairs={{0,4},{4,0},{8,12},{12,8},{16,20},{20,16},{24,28},{28,24},{1,5},{5... | collective-permute-start | bytes 1769480 | tf_op jit(solution)/shard_map/ppermute | solution.py:693
  204.9 90.4 %collective-permute-start.52 = (bf16[2,192,1536]{2,1,0:T(8,128)(2,1)}, bf16[2,192,1536]{2,1,0:T(8,128)(2,1)}, u32[]{:S(2)}, u32[]{:S(2)}) collective-permute-start(bf16[2,192,1536]{2,1,0:T(8,128)(2,1)} %copy-done.51), channel_id=1, source_target_pairs={{0,4},{4,0},{8,12},{12,8},{16,20},{20,16},{24,28},{28,24},{1,5},{5... | collective-permute-start | bytes 3538952 | tf_op jit(solution)/shard_map/ppermute | solution.py:693
  213.2 84.7 %collective-permute-start.47 = (bf16[2,192,1536]{2,1,0:T(8,128)(2,1)}, bf16[2,192,1536]{2,1,0:T(8,128)(2,1)}, u32[]{:S(2)}, u32[]{:S(2)}) collective-permute-start(bf16[2,192,1536]{2,1,0:T(8,128)(2,1)} %copy-done.50), channel_id=1, source_target_pairs={{0,4},{4,0},{8,12},{12,8},{16,20},{20,16},{24,28},{28,24},{1,5},{5... | collective-permute-start | bytes 3538952 | tf_op jit(solution)/shard_map/ppermute | solution.py:693
  228.7 19.7 %collective-permute-start.23 = (bf16[192,768]{1,0:T(8,128)(2,1)S(1)}, bf16[192,768]{1,0:T(8,128)(2,1)S(1)}, u32[]{:S(2)}, u32[]{:S(2)}) collective-permute-start(bf16[192,768]{1,0:T(8,128)(2,1)S(1)} %fusion.20), channel_id=1, source_target_pairs={{0,8},{4,12},{8,0},{12,4},{16,24},{20,28},{24,16},{28,20},{1,9},{5... | collective-permute-start | bytes 884744 | tf_op jit(solution)/shard_map/ppermute | solution.py:693
  231.9 18.2 %collective-permute-start.43 = (bf16[192,768]{1,0:T(8,128)(2,1)S(1)}, bf16[192,768]{1,0:T(8,128)(2,1)S(1)}, u32[]{:S(2)}, u32[]{:S(2)}) collective-permute-start(bf16[192,768]{1,0:T(8,128)(2,1)S(1)} %fusion.22), channel_id=1, source_target_pairs={{0,8},{4,12},{8,0},{12,4},{16,24},{20,28},{24,16},{28,20},{1,9},{5... | collective-permute-start | bytes 884744 | tf_op jit(solution)/shard_map/ppermute | solution.py:693
  252.0 31.6 %collective-permute-start.62 = (bf16[2,384,768]{2,1,0:T(8,128)(2,1)S(1)}, bf16[2,384,768]{2,1,0:T(8,128)(2,1)S(1)}, u32[]{:S(2)}, u32[]{:S(2)}) collective-permute-start(bf16[2,384,768]{2,1,0:T(8,128)(2,1)S(1)} %get-tuple-element.133), channel_id=1, source_target_pairs={{0,4},{4,0},{8,12},{12,8},{16,20},{20,16},{24,28},{28,24},{1,5},{5... | collective-permute-start | bytes 3538952 | tf_op jit(solution)/shard_map/ppermute | solution.py:693
  252.7 29.4 %collective-permute-start.24 = (bf16[192,768]{1,0:T(8,128)(2,1)S(1)}, bf16[192,768]{1,0:T(8,128)(2,1)S(1)}, u32[]{:S(2)}, u32[]{:S(2)}) collective-permute-start(bf16[192,768]{1,0:T(8,128)(2,1)S(1)} %fusion.15), channel_id=1, source_target_pairs={{0,1},{3,2},{4,5},{7,6},{8,9},{11,10},{12,13},{15,14},{16,17},{19,... | collective-permute-start | bytes 884744 | tf_op jit(solution)/shard_map/ppermute | solution.py:707
  282.1 17.7 %collective-permute-start.57 = (bf16[2,384,768]{2,1,0:T(8,128)(2,1)S(1)}, bf16[2,384,768]{2,1,0:T(8,128)(2,1)S(1)}, u32[]{:S(2)}, u32[]{:S(2)}) collective-permute-start(bf16[2,384,768]{2,1,0:T(8,128)(2,1)S(1)} %get-tuple-element.131), channel_id=1, source_target_pairs={{0,4},{4,0},{8,12},{12,8},{16,20},{20,16},{24,28},{28,24},{1,5},{5... | collective-permute-start | bytes 3538952 | tf_op jit(solution)/shard_map/ppermute | solution.py:693
  283.6 17.0 %collective-permute-start.29 = (bf16[192,512]{1,0:T(8,128)(2,1)S(1)}, bf16[192,512]{1,0:T(8,128)(2,1)S(1)}, u32[]{:S(2)}, u32[]{:S(2)}) collective-permute-start(bf16[192,512]{1,0:T(8,128)(2,1)S(1)} %fusion.18), channel_id=1, source_target_pairs={{0,1},{3,2},{4,5},{7,6},{8,9},{11,10},{12,13},{15,14},{16,17},{19,... | collective-permute-start | bytes 589832 | tf_op jit(solution)/shard_map/ppermute | solution.py:707
  290.9 11.4 %collective-permute-start.34 = (bf16[192,512]{1,0:T(8,128)(2,1)S(1)}, bf16[192,512]{1,0:T(8,128)(2,1)S(1)}, u32[]{:S(2)}, u32[]{:S(2)}) collective-permute-start(bf16[192,512]{1,0:T(8,128)(2,1)S(1)} %fusion.17), channel_id=1, source_target_pairs={{0,1},{3,2},{4,5},{7,6},{8,9},{11,10},{12,13},{15,14},{16,17},{19,... | collective-permute-start | bytes 589832 | tf_op jit(solution)/shard_map/ppermute | solution.py:707
  300.7 59.7 %collective-permute-start.53 = (bf16[192,1536]{1,0:T(8,128)(2,1)S(1)}, bf16[192,1536]{1,0:T(8,128)(2,1)S(1)}, u32[]{:S(2)}, u32[]{:S(2)}) collective-permute-start(bf16[192,1536]{1,0:T(8,128)(2,1)S(1)} %fusion.9), channel_id=1, source_target_pairs={{0,8},{4,12},{8,0},{12,4},{16,24},{20,28},{24,16},{28,20},{1,9},{5... | collective-permute-start | bytes 1769480 | tf_op jit(solution)/shard_map/ppermute | solution.py:693
  302.3 60.7 %collective-permute-start.48 = (bf16[192,1536]{1,0:T(8,128)(2,1)S(1)}, bf16[192,1536]{1,0:T(8,128)(2,1)S(1)}, u32[]{:S(2)}, u32[]{:S(2)}) collective-permute-start(bf16[192,1536]{1,0:T(8,128)(2,1)S(1)} %fusion.7), channel_id=1, source_target_pairs={{0,8},{4,12},{8,0},{12,4},{16,24},{20,28},{24,16},{28,20},{1,9},{5... | collective-permute-start | bytes 1769480 | tf_op jit(solution)/shard_map/ppermute | solution.py:693
  303.5 65.4 %collective-permute-start.63 = (bf16[384,768]{1,0:T(8,128)(2,1)S(1)}, bf16[384,768]{1,0:T(8,128)(2,1)S(1)}, u32[]{:S(2)}, u32[]{:S(2)}) collective-permute-start(bf16[384,768]{1,0:T(8,128)(2,1)S(1)} %fusion.13), channel_id=1, source_target_pairs={{0,8},{4,12},{8,0},{12,4},{16,24},{20,28},{24,16},{28,20},{1,9},{5... | collective-permute-start | bytes 1769480 | tf_op jit(solution)/shard_map/ppermute | solution.py:693
  305.0 65.4 %collective-permute-start.58 = (bf16[384,768]{1,0:T(8,128)(2,1)S(1)}, bf16[384,768]{1,0:T(8,128)(2,1)S(1)}, u32[]{:S(2)}, u32[]{:S(2)}) collective-permute-start(bf16[384,768]{1,0:T(8,128)(2,1)S(1)} %fusion.11), channel_id=1, source_target_pairs={{0,8},{4,12},{8,0},{12,4},{16,24},{20,28},{24,16},{28,20},{1,9},{5... | collective-permute-start | bytes 1769480 | tf_op jit(solution)/shard_map/ppermute | solution.py:693
  308.0 33.7 %collective-permute-start.31 = (bf16[192,512]{1,0:T(8,128)(2,1)S(1)}, bf16[192,512]{1,0:T(8,128)(2,1)S(1)}, u32[]{:S(2)}, u32[]{:S(2)}) collective-permute-start(bf16[192,512]{1,0:T(8,128)(2,1)S(1)} %add_convert_fusion.32), channel_id=1, source_target_pairs={{1,0},{2,3},{5,4},{6,7},{9,8},{10,11},{13,12},{14,15},{17,16},{18,... | collective-permute-start | bytes 589832 | tf_op jit(solution)/shard_map/ppermute | solution.py:711
  359.1 13.0 %collective-permute-start.26 = (bf16[192,768]{1,0:T(8,128)(2,1)S(1)}, bf16[192,768]{1,0:T(8,128)(2,1)S(1)}, u32[]{:S(2)}, u32[]{:S(2)}) collective-permute-start(bf16[192,768]{1,0:T(8,128)(2,1)S(1)} %add_convert_fusion.20), channel_id=1, source_target_pairs={{1,0},{2,3},{5,4},{6,7},{9,8},{10,11},{13,12},{14,15},{17,16},{18,... | collective-permute-start | bytes 884744 | tf_op jit(solution)/shard_map/ppermute | solution.py:711
  360.4 13.2 %collective-permute-start.46 = (bf16[192,768]{1,0:T(8,128)(2,1)S(1)}, bf16[192,768]{1,0:T(8,128)(2,1)S(1)}, u32[]{:S(2)}, u32[]{:S(2)}) collective-permute-start(bf16[192,768]{1,0:T(8,128)(2,1)S(1)} %add_convert_fusion.16), channel_id=1, source_target_pairs={{1,0},{2,3},{5,4},{6,7},{9,8},{10,11},{13,12},{14,15},{17,16},{18,... | collective-permute-start | bytes 884744 | tf_op jit(solution)/shard_map/ppermute | solution.py:711
  363.0 18.4 %collective-permute-start.54 = (bf16[192,1536]{1,0:T(8,128)(2,1)S(1)}, bf16[192,1536]{1,0:T(8,128)(2,1)S(1)}, u32[]{:S(2)}, u32[]{:S(2)}) collective-permute-start(bf16[192,1536]{1,0:T(8,128)(2,1)S(1)} %fusion.3), channel_id=1, source_target_pairs={{0,1},{3,2},{4,5},{7,6},{8,9},{11,10},{12,13},{15,14},{16,17},{19,... | collective-permute-start | bytes 1769480 | tf_op jit(solution)/shard_map/ppermute | solution.py:707
  368.9 25.1 %collective-permute-start.49 = (bf16[192,1536]{1,0:T(8,128)(2,1)S(1)}, bf16[192,1536]{1,0:T(8,128)(2,1)S(1)}, u32[]{:S(2)}, u32[]{:S(2)}) collective-permute-start(bf16[192,1536]{1,0:T(8,128)(2,1)S(1)} %fusion.4), channel_id=1, source_target_pairs={{0,1},{3,2},{4,5},{7,6},{8,9},{11,10},{12,13},{15,14},{16,17},{19,... | collective-permute-start | bytes 1769480 | tf_op jit(solution)/shard_map/ppermute | solution.py:707
  370.5 33.5 %collective-permute-start.64 = (bf16[384,768]{1,0:T(8,128)(2,1)S(1)}, bf16[384,768]{1,0:T(8,128)(2,1)S(1)}, u32[]{:S(2)}, u32[]{:S(2)}) collective-permute-start(bf16[384,768]{1,0:T(8,128)(2,1)S(1)} %fusion.1), channel_id=1, source_target_pairs={{0,1},{3,2},{4,5},{7,6},{8,9},{11,10},{12,13},{15,14},{16,17},{19,... | collective-permute-start | bytes 1769480 | tf_op jit(solution)/shard_map/ppermute | solution.py:707
  372.1 38.2 %collective-permute-start.59 = (bf16[384,768]{1,0:T(8,128)(2,1)S(1)}, bf16[384,768]{1,0:T(8,128)(2,1)S(1)}, u32[]{:S(2)}, u32[]{:S(2)}) collective-permute-start(bf16[384,768]{1,0:T(8,128)(2,1)S(1)} %fusion.2), channel_id=1, source_target_pairs={{0,1},{3,2},{4,5},{7,6},{8,9},{11,10},{12,13},{15,14},{16,17},{19,... | collective-permute-start | bytes 1769480 | tf_op jit(solution)/shard_map/ppermute | solution.py:707
  381.5 29.7 %collective-permute-start.55 = (bf16[192,1536]{1,0:T(8,128)(2,1)S(1)}, bf16[192,1536]{1,0:T(8,128)(2,1)S(1)}, u32[]{:S(2)}, u32[]{:S(2)}) collective-permute-start(bf16[192,1536]{1,0:T(8,128)(2,1)S(1)} %add_convert_fusion.9), channel_id=1, source_target_pairs={{1,2},{2,1},{5,6},{6,5},{9,10},{10,9},{13,14},{14,13},{17,18},{18,... | collective-permute-start | bytes 1769480 | tf_op jit(solution)/shard_map/ppermute | solution.py:709
  394.1 21.4 %collective-permute-start.50 = (bf16[192,1536]{1,0:T(8,128)(2,1)S(1)}, bf16[192,1536]{1,0:T(8,128)(2,1)S(1)}, u32[]{:S(2)}, u32[]{:S(2)}) collective-permute-start(bf16[192,1536]{1,0:T(8,128)(2,1)S(1)} %add_convert_fusion.13), channel_id=1, source_target_pairs={{1,2},{2,1},{5,6},{6,5},{9,10},{10,9},{13,14},{14,13},{17,18},{18,... | collective-permute-start | bytes 1769480 | tf_op jit(solution)/shard_map/ppermute | solution.py:709
  411.3 44.7 %collective-permute-start.56 = (bf16[192,1536]{1,0:T(8,128)(2,1)S(1)}, bf16[192,1536]{1,0:T(8,128)(2,1)}, u32[]{:S(2)}, u32[]{:S(2)}) collective-permute-start(bf16[192,1536]{1,0:T(8,128)(2,1)S(1)} %add_convert_fusion.8), channel_id=1, source_target_pairs={{1,0},{2,3},{5,4},{6,7},{9,8},{10,11},{13,12},{14,15},{17,16},{18,... | collective-permute-start | bytes 1769480 | tf_op jit(solution)/shard_map/ppermute | solution.py:711
  412.8 32.0 %collective-permute-start.66 = (bf16[384,768]{1,0:T(8,128)(2,1)S(1)}, bf16[384,768]{1,0:T(8,128)(2,1)S(1)}, u32[]{:S(2)}, u32[]{:S(2)}) collective-permute-start(bf16[384,768]{1,0:T(8,128)(2,1)S(1)} %add_convert_fusion), channel_id=1, source_target_pairs={{1,0},{2,3},{5,4},{6,7},{9,8},{10,11},{13,12},{14,15},{17,16},{18,... | collective-permute-start | bytes 1769480 | tf_op jit(solution)/shard_map/ppermute | solution.py:711
  414.2 39.6 %collective-permute-start.61 = (bf16[384,768]{1,0:T(8,128)(2,1)S(1)}, bf16[384,768]{1,0:T(8,128)(2,1)S(1)}, u32[]{:S(2)}, u32[]{:S(2)}) collective-permute-start(bf16[384,768]{1,0:T(8,128)(2,1)S(1)} %add_convert_fusion.4), channel_id=1, source_target_pairs={{1,0},{2,3},{5,4},{6,7},{9,8},{10,11},{13,12},{14,15},{17,16},{18,... | collective-permute-start | bytes 1769480 | tf_op jit(solution)/shard_map/ppermute | solution.py:711
  415.7 44.6 %collective-permute-start.51 = (bf16[192,1536]{1,0:T(8,128)(2,1)S(1)}, bf16[192,1536]{1,0:T(8,128)(2,1)}, u32[]{:S(2)}, u32[]{:S(2)}) collective-permute-start(bf16[192,1536]{1,0:T(8,128)(2,1)S(1)} %add_convert_fusion.12), channel_id=1, source_target_pairs={{1,0},{2,3},{5,4},{6,7},{9,8},{10,11},{13,12},{14,15},{17,16},{18,... | collective-permute-start | bytes 1769480 | tf_op jit(solution)/shard_map/ppermute | solution.py:711
  (95 other events, 655.2 us)

commit v2 on v1

v2 whole, which is shorter than its diff:
```python
import functools
import math

import jax
import jax.numpy as jnp
from jax import lax
from jax.experimental import pallas as pl
from jax.experimental.pallas import tpu as pltpu
from jax.sharding import PartitionSpec as P

D = 768
HEADS = 12
HEAD_DIM = 64
FF = 3072
SEQ = 512
GROUPS = 3
THIRD = D // GROUPS
WIDE = 512
NARROW = D - WIDE
PAIR = 2 * HEAD_DIM
BLOCK = 128
REACH = 96
ROWS = 256
MIB = 1024 * 1024

epsilon = 1e-05
masked_score = -1e30
score_scale = HEAD_DIM ** (-0.5)
gelu_scale = math.sqrt(2.0 / math.pi)
gelu_cubic = 0.044715

f32 = jnp.float32
bf16 = jnp.bfloat16

WINDOWS = [
    (max(0, start - REACH), min(SEQ, start + BLOCK + REACH)) for start in range(0, SEQ, BLOCK)
]
WINDOW = BLOCK + 2 * REACH

in_smem = pl.BlockSpec(memory_space=pltpu.SMEM)
in_vmem = pl.BlockSpec(memory_space=pltpu.VMEM)
in_any = pl.BlockSpec(memory_space=pl.ANY)


def shape_of(dims, dtype):
    return jax.ShapeDtypeStruct(dims, dtype)


def dot(left, right):
    return lax.dot_general(left, right, (((1,), (0,)), ((), ())), preferred_element_type=f32)


def dot_nt(left, right):
    return lax.dot_general(left, right, (((1,), (1,)), ((), ())), preferred_element_type=f32)


def dot_tn(left, right):
    return lax.dot_general(left, right, (((0,), (0,)), ((), ())), preferred_element_type=f32)


def normalise(values):
    average = jnp.mean(values, axis=-1, keepdims=True)
    centred = values - average
    spread = jnp.mean(centred * centred, axis=-1, keepdims=True)
    root = lax.rsqrt(spread + epsilon)
    return centred * root, root


def norm_back(scaled, root, gain, incoming):
    weighted = incoming * gain
    average = jnp.mean(weighted, axis=-1, keepdims=True)
    slope = jnp.mean(weighted * scaled, axis=-1, keepdims=True)
    return root * (weighted - average - scaled * slope)


def column_sums(values):
    return jnp.sum(values, axis=0, keepdims=True)


class Order:
    def __init__(self):
        self.token = []

    def call(
        self,
        kernel,
        args,
        in_specs,
        outs,
        out_specs,
        scratch=(),
        grid=(),
        limit=24,
        name=None,
        prefetch=None,
        waits=(),
        aliases=None,
        cost=0,
    ):
        given = len(args)
        extra = list(self.token) + list(waits)
        ahead = [] if prefetch is None else [prefetch]
        count = len(ahead)

        def wrapped(*refs):
            kernel(*refs[: count + given], *refs[count + given + len(extra) :])

        results = pl.pallas_call(
            wrapped,
            out_shape=outs,
            grid_spec=pltpu.PrefetchScalarGridSpec(
                num_scalar_prefetch=count,
                grid=grid,
                in_specs=list(in_specs) + [in_any] * len(extra),
                out_specs=out_specs,
                scratch_shapes=list(scratch),
            ),
            compiler_params=pltpu.CompilerParams(vmem_limit_bytes=limit * MIB),
            cost_estimate=pl.CostEstimate(flops=1 + cost * 10**9, bytes_accessed=1 + cost * MIB, transcendentals=cost * 10**6),
            input_output_aliases=aliases or {},
            name=name,
        )(*ahead, *args, *extra)
        self.token = [min(results, key=lambda out: out.size)]
        return results

    def hold(self, arrays, waits=()):
        return self.call(
            lambda *refs: None,
            arrays,
            [in_any] * len(arrays),
            [shape_of(array.shape, array.dtype) for array in arrays],
            [in_any] * len(arrays),
            name="hold",
            waits=waits,
            aliases={k: k for k in range(len(arrays))},
        )


def part_copies(places, parts, whole, sems, columns=None):
    rows = whole.shape[0] // len(parts)
    width = slice(None) if columns is None else columns
    return [
        pltpu.make_async_copy(
            part.at[pl.ds(0, rows), width],
            whole.at[pl.ds(pl.multiple_of(places[k] * rows, 16), rows)],
            sems.at[k],
        )
        for k, part in enumerate(parts)
    ]


def start_all(copies):
    for copy in copies:
        copy.start()


def wait_all(copies):
    for copy in copies:
        copy.wait()


def sums_pass(order, places, folds=(), adds=(), pays=(), waits=()):
    args, outs, steps = [], [], []

    def give(*arrays):
        args.extend(arrays)
        return list(range(len(args) - len(arrays), len(args)))

    def make(dims, dtype):
        outs.append(shape_of(dims, dtype))
        return len(outs) - 1

    for pairs in folds:
        rows, dtype = pairs[0][0].shape[1], pairs[0][0].dtype
        width = sum(near.shape[2] for near, _ in pairs)
        given = [give(near, received) for near, received in pairs]
        steps.append(("fold", given, [make((rows, width), dtype) for _ in range(2)]))
    for left, right in adds:
        steps.append(("add", give(left, right), [make(left.shape, left.dtype)]))
    for mine, received, older, crossed in pays:
        given = give(mine, received, older, crossed)
        steps.append(("pay", given, [make(mine.shape, mine.dtype) for _ in range(2)]))
    count = len(args)

    def kernel(places_ref, *refs):
        ins, results = refs[:count], refs[count:]
        inner = jnp.logical_and(places_ref[4] > 0, places_ref[4] < 3)
        for kind, given, made in steps:
            if kind == "fold":
                first = 0
                for near, received in given:
                    width = ins[near].shape[2]
                    for slot, out in enumerate(made):
                        total = ins[near][slot].astype(f32) + ins[received][slot].astype(f32)
                        results[out][:, first : first + width] = total.astype(results[out].dtype)
                    first += width
            elif kind == "add":
                total = ins[given[0]][...].astype(f32) + ins[given[1]][...].astype(f32)
                results[made[0]][...] = total.astype(results[made[0]].dtype)
            else:
                fresh = ins[given[0]][...].astype(f32) + ins[given[1]][...].astype(f32)
                older = ins[given[2]][...].astype(f32) + ins[given[3]][...].astype(f32)
                results[made[0]][...] = fresh.astype(results[made[0]].dtype)
                results[made[1]][...] = jnp.where(inner, older, fresh).astype(results[made[1]].dtype)

    found = order.call(
        kernel,
        [places, *args],
        [in_smem] + [in_vmem] * len(args),
        outs,
        [in_vmem] * len(outs),
        limit=40,
        name="sums",
        waits=waits,
    )
    found = list(found)
    return found[0] if len(found) == 1 else found


def cast_kernel(count, *refs):
    for source, target in zip(refs[:count], refs[count:]):
        target[...] = source[...].astype(bf16)


def cast_pass(order, arrays):
    return order.call(
        functools.partial(cast_kernel, len(arrays)),
        arrays,
        [in_vmem] * len(arrays),
        [shape_of(array.shape, bf16) for array in arrays],
        [in_vmem] * len(arrays),
        limit=32,
        name="cast",
    )


def pack_kernel(sizes, places, down, short, down_out, slice_out, short_out, rows):
    down_out[...] = down[...].astype(bf16)
    height = down.shape[0] // 4
    first = pl.multiple_of(places[4] * height, 16)
    slice_out[...] = down[pl.ds(first, height)].astype(bf16)
    rows[...] = jnp.zeros_like(rows)
    offset = 0
    for line, size in enumerate(sizes):
        rows[line : line + 1, :size] = short[:, offset : offset + size]
        offset += size
    short_out[...] = rows[...].astype(bf16)


def pack_pass(order, places, down, short, sizes):
    return order.call(
        functools.partial(pack_kernel, sizes),
        [places, down, short],
        [in_smem, in_vmem, in_vmem],
        [
            shape_of(down.shape, bf16),
            shape_of((down.shape[0] // 4, down.shape[1]), bf16),
            shape_of((16, D), bf16),
        ],
        [in_vmem] * 3,
        scratch=[pltpu.VMEM((16, D), f32)],
        limit=32,
        name="pack",
    )


def wide_cast_kernel(left, right, out):
    out[:, :D] = left[...].astype(bf16)
    out[:, D:] = right[...].astype(bf16)


def wide_cast_pass(order, left, right):
    return order.call(
        wide_cast_kernel,
        [left, right],
        [in_vmem] * 2,
        [shape_of((left.shape[0], D + FF), bf16)],
        [in_vmem],
        limit=32,
        name="wide_cast",
    )[0]


def stack_kernel(first, second, out):
    out[0] = first[...]
    out[1] = second[...]


def stack_pass(order, first, second, waits=()):
    return order.call(
        stack_kernel,
        [first, second],
        [in_vmem] * 2,
        [shape_of((2,) + first.shape, first.dtype)],
        [in_vmem],
        name="stack",
        waits=waits,
    )[0]


def line_kernel(places, own, up_one, up_two, up_three, down_one, down_two, down_three, out, sems):
    floor = places[4]
    size = own.shape[0]

    def copy(piece, level, index):
        target = out.at[pl.ds(pl.multiple_of(level * size, 16), size)]
        return pltpu.make_async_copy(piece, target, sems.at[index])

    copies = [(None, copy(own, floor, 0))]
    for step, piece in enumerate((up_one, up_two, up_three), 1):
        copies.append((floor >= step, copy(piece, floor - step, step)))
    for step, piece in enumerate((down_one, down_two, down_three), 1):
        copies.append((floor + step <= 3, copy(piece, floor + step, step + 3)))
    for act in ("start", "wait"):
        for valid, one in copies:
            if valid is None:
                getattr(one, act)()
            else:
                pl.when(valid)(getattr(one, act))


def line_pass(order, places, pieces, waits=()):
    rows, width = pieces[0].shape
    return order.call(
        line_kernel,
        [places, *pieces],
        [in_smem] + [in_any] * 7,
        [shape_of((4 * rows, width), bf16)],
        [in_any],
        scratch=[pltpu.SemaphoreType.DMA((7,))],
        name="line",
        waits=waits,
    )[0]


def project_kernel(count, packed, places, rows, short, *rest):
    if not packed:
        given_hidden, rest = rest[0], rest[1:]
    else:
        other_short, rest = rest[0], rest[1:]
    parts, rest = rest[:count], rest[count:]
    query_out, wide_out, narrow_out, normed_out, vectors_out, hidden_out, weight, sems = rest
    copies = part_copies(places, parts, weight, sems)
    start_all(copies)
    shard = D // count
    if packed:
        vectors = jnp.zeros((8, D), f32)
        line = lax.broadcasted_iota(jnp.int32, (8, D), 0)
        for k in range(count):
            block = (other_short if k % 2 else short)[k // 2].astype(f32)[:8]
            vectors += pltpu.roll(jnp.where(line < 7, block, 0.0), places[k] * shard, 1)
            start = pl.multiple_of(places[k] * D, 128)
            hidden_out[:, pl.ds(start, D)] = block[7:8]
    else:
        vectors = short[...]
        hidden_out[...] = given_hidden[...]
    vectors_out[...] = vectors
    scaled, _ = normalise(rows[...].astype(f32))
    normed_out[...] = (scaled * vectors[0:1] + vectors[1:2]).astype(bf16)
    wait_all(copies)

    def block(column, width):
        return dot(normed_out[...], weight[:, column : column + width]).astype(bf16)

    for kind in range(2):
        for first in range(0, WIDE, 256):
            wide_out[kind, :, first : first + 256] = block((kind + 1) * D + first, 256)
    for kind in range(2):
        for first in range(0, NARROW, 256):
            narrow_out[kind, :, first : first + 256] = block((kind + 1) * D + WIDE + first, 256)
    for first in range(0, D, 256):
        query_out[:, first : first + 256] = block(first, 256)


def project(order, places, rows, parts, given, waits=()):
    count = len(parts)
    return order.call(
        functools.partial(project_kernel, count, count > 1),
        [places, rows, *given, *parts],
        [in_smem] + [in_vmem] * 3 + [in_any] * count,
        [
            shape_of((SEQ, D), bf16),
            shape_of((2, SEQ, WIDE), bf16),
            shape_of((2, SEQ, NARROW), bf16),
            shape_of((SEQ, D), bf16),
            shape_of((8, D), f32),
            shape_of((1, FF), f32),
        ],
        [in_vmem] * 6,
        scratch=[pltpu.VMEM((D, 3 * D), bf16), pltpu.SemaphoreType.DMA((count,))],
        name="project",
        waits=waits,
    )


def fill_page_bias(page_row, page_column, bias):
    for index, (low, high) in enumerate(WINDOWS):
        start = index * BLOCK
        same = page_column[low:high] == page_row[:, start : start + BLOCK]
        bias[index, : high - low] = jnp.where(same, 0.0, masked_score)


def two_heads(block):
    lane = lax.broadcasted_iota(jnp.int32, block.shape, 1)
    zero = jnp.zeros_like(block)
    return jnp.concatenate(
        [jnp.where(lane < HEAD_DIM, block, zero), jnp.where(lane < HEAD_DIM, zero, block)], axis=0
    )


def head_rows(both):
    return jnp.concatenate([both[:HEAD_DIM, :BLOCK], both[HEAD_DIM:, BLOCK:]], axis=0).T


def page_bias(bias, index, size):
    block = bias[index, :size]
    return jnp.concatenate([block, block], axis=1)


def attend_kernel(
    query, key, value, key_two, value_two, page_row, page_column, context, log_total, bias
):
    @pl.when(pl.program_id(0) == 0)
    def _():
        fill_page_bias(page_row, page_column, bias)

    for index, (low, high) in enumerate(WINDOWS):
        start = index * BLOCK
        queries = two_heads(query[start : start + BLOCK] * score_scale)
        allowed = page_bias(bias, index, high - low)
        scores = dot_nt(key[0, low:high], queries) + allowed
        scores_two = dot_nt(key_two[0, low:high], queries) + allowed
        largest = jnp.maximum(
            jnp.max(scores, axis=0, keepdims=True), jnp.max(scores_two, axis=0, keepdims=True)
        )
        exponent = jnp.exp(scores - largest)
        exponent_two = jnp.exp(scores_two - largest)
        total = column_sums(exponent) + column_sums(exponent_two)
        inverse = 1.0 / total
        shares = (exponent * inverse).astype(bf16)
        shares_two = (exponent_two * inverse).astype(bf16)
        both = dot_tn(value[0, low:high], shares) + dot_tn(value_two[0, low:high], shares_two)
        context[start : start + BLOCK] = head_rows(both).astype(bf16)
        log_row = largest + jnp.log(total)
        log_total[0, 0:1, start : start + BLOCK] = log_row[:, :BLOCK]
        log_total[0, 1:2, start : start + BLOCK] = log_row[:, BLOCK:]


def pair_specs(query_first, key_first):
    query = pl.BlockSpec((SEQ, PAIR), lambda step: (0, query_first + step))
    key = pl.BlockSpec((1, SEQ, PAIR), lambda step: (0, 0, key_first + step))
    value = pl.BlockSpec((1, SEQ, PAIR), lambda step: (1, 0, key_first + step))
    page_row = pl.BlockSpec((1, SEQ), lambda step: (0, 0))
    page_column = pl.BlockSpec((SEQ, 1), lambda step: (0, 0))
    narrow = pl.BlockSpec((SEQ, PAIR), lambda step: (0, step))
    logs = pl.BlockSpec((1, 2, SEQ), lambda step: (key_first + step, 0, 0))
    return query, key, value, page_row, page_column, narrow, logs


def attend(order, query_first, queries, own, other, page_row, page_column, cost=0):
    width = own.shape[2]
    steps = width // PAIR
    query, key, value, row_spec, column_spec, narrow, logs = pair_specs(query_first, 0)
    return order.call(
        attend_kernel,
        [queries, own, own, other, other, page_row, page_column],
        [query, key, value, key, value, row_spec, column_spec],
        [shape_of((SEQ, width), bf16), shape_of((steps, 2, SEQ), f32)],
        [narrow, logs],
        scratch=[pltpu.VMEM((len(WINDOWS), WINDOW, BLOCK), f32)],
        grid=(steps,),
        name="attend",
        cost=cost,
    )


def attend_back_kernel(
    query,
    key,
    value,
    key_two,
    value_two,
    context_grad,
    log_total,
    page_row,
    page_column,
    query_grad,
    own_grad,
    other_grad,
    bias,
    other_sum,
):
    @pl.when(pl.program_id(0) == 0)
    def _():
        fill_page_bias(page_row, page_column, bias)

    own_grad[...] = jnp.zeros_like(own_grad)
    other_sum[...] = jnp.zeros_like(other_sum)
    for index, (low, high) in enumerate(WINDOWS):
        start = index * BLOCK
        queries = two_heads(query[start : start + BLOCK] * score_scale)
        grads = two_heads(context_grad[start : start + BLOCK])
        log_row = jnp.concatenate(
            [
                log_total[0, 0:1, start : start + BLOCK],
                log_total[0, 1:2, start : start + BLOCK],
            ],
            axis=1,
        )
        allowed = page_bias(bias, index, high - low)
        keys, keys_two = key[0, low:high], key_two[0, low:high]
        shares = jnp.exp(dot_nt(keys, queries) + allowed - log_row)
        shares_two = jnp.exp(dot_nt(keys_two, queries) + allowed - log_row)
        share_grad = dot_nt(value[0, low:high], grads)
        share_grad_two = dot_nt(value_two[0, low:high], grads)
        centre = column_sums(shares * share_grad) + column_sums(shares_two * share_grad_two)
        score_grad = (shares * (share_grad - centre)).astype(bf16)
        score_grad_two = (shares_two * (share_grad_two - centre)).astype(bf16)
        own_grad[0, low:high] += dot(score_grad, queries)
        own_grad[1, low:high] += dot(shares.astype(bf16), grads)
        other_sum[0, low:high] += dot(score_grad_two, queries)
        other_sum[1, low:high] += dot(shares_two.astype(bf16), grads)
        both = dot_tn(keys, score_grad) + dot_tn(keys_two, score_grad_two)
        query_grad[start : start + BLOCK] = (head_rows(both) * score_scale).astype(bf16)
    other_grad[...] = other_sum[...].astype(bf16)


def attend_back(
    order, query_first, key_first, queries, own, other, context_grad, logs, page_row, page_column
):
    steps = THIRD // PAIR
    query, key, value, row_spec, column_spec, narrow, log_spec = pair_specs(query_first, key_first)
    pair = pl.BlockSpec((2, SEQ, PAIR), lambda step: (0, 0, step))
    return order.call(
        attend_back_kernel,
        [queries, own, own, other, other, context_grad, logs, page_row, page_column],
        [query, key, value, key, value, query, log_spec, row_spec, column_spec],
        [
            shape_of((SEQ, THIRD), bf16),
            shape_of((2, SEQ, THIRD), f32),
            shape_of((2, SEQ, THIRD), bf16),
        ],
        [narrow, pair, pair],
        scratch=[
            pltpu.VMEM((len(WINDOWS), WINDOW, BLOCK), f32),
            pltpu.VMEM((2, SEQ, PAIR), f32),
        ],
        grid=(steps,),
        name="attend_back",
    )


def wide_copies(places, parts, w_out, w_up, out_sems, up_sems):
    count = len(parts)
    rows, slot = D // count, FF // count
    out_copies, up_copies = [], []
    for k, part in enumerate(parts):
        target = pl.ds(pl.multiple_of(places[k] * rows, 16), rows)
        out_copies.append(
            pltpu.make_async_copy(part.at[pl.ds(0, rows), pl.ds(0, D)], w_out.at[target], out_sems.at[k])
        )
    for c in range(count):
        columns = pl.ds(pl.multiple_of(D + places[c] * slot, 128), slot)
        one = []
        for k, part in enumerate(parts):
            target = pl.ds(pl.multiple_of(places[k] * rows, 16), rows)
            one.append(
                pltpu.make_async_copy(
                    part.at[pl.ds(0, rows), columns], w_up.at[c, target], up_sems.at[c, k]
                )
            )
        up_copies.append(one)
    return out_copies, up_copies


def down_copies(parts, w_down, sems):
    return [pltpu.make_async_copy(part, w_down.at[k], sems.at[k]) for k, part in enumerate(parts)]


def weight_scratch(count):
    return [
        pltpu.VMEM((D, D), bf16),
        pltpu.VMEM((count, D, FF // count), bf16),
        pltpu.VMEM((count, FF // count, D), bf16),
        pltpu.SemaphoreType.DMA((count,)),
        pltpu.SemaphoreType.DMA((count, count)),
        pltpu.SemaphoreType.DMA((count,)),
    ]


def same_block(dims):
    return pl.BlockSpec(dims, lambda step, places: (0,) * len(dims))


def slot_block(rows, slot):
    return pl.BlockSpec((rows, slot), lambda step, places: (0, places[step]))


def middle_kernel(count, places, rows, context, context_two, tangent, vectors, partner, hidden_bias, *rest):
    wide_parts, down_parts, rest = rest[:count], rest[count : 2 * count], rest[2 * count :]
    middle_out, second_out, hidden_out, slope_out, modal_out, inner_out = rest[:6]
    total, w_out, w_up, w_down, out_sems, up_sems, down_sems = rest[6:]
    out_copies, up_copies = wide_copies(places, wide_parts, w_out, w_up, out_sems, up_sems)
    last_copies = down_copies(down_parts, w_down, down_sems)
    step = pl.program_id(0)

    @pl.when(step == 0)
    def _():
        start_all(out_copies)
        for one in up_copies:
            start_all(one)
        start_all(last_copies)
        wait_all(out_copies)
        middle = rows[...].astype(f32) + dot(context[...], w_out[:WIDE])
        middle += dot(context_two[...], w_out[WIDE:])
        middle_out[...] = middle
        scaled, _ = normalise(middle)
        second_out[...] = (scaled * vectors[2:3] + vectors[3:4]).astype(bf16)
        total[...] = middle + vectors[4:5]

    for k in range(count):

        @pl.when(step == k)
        def _():
            wait_all(up_copies[k])
            last_copies[k].wait()

    slot = FF // count
    size = 256
    for first in range(0, slot, size):
        part = slice(first, first + size)
        upper = dot(second_out[...], w_up[step, :, part]) + hidden_bias[:, part]
        square = upper * upper
        angle = jnp.tanh(upper * (gelu_scale + (gelu_cubic * gelu_scale) * square))
        half = 0.5 + 0.5 * angle
        hidden_out[:, part] = (upper * half).astype(bf16)
        bend = 2.0 * gelu_scale + (6.0 * gelu_cubic * gelu_scale) * square
        slope_out[:, part] = (half + half * (1.0 - half) * (upper * bend)).astype(bf16)
    total[...] += dot(hidden_out[...], w_down[step])

    @pl.when(step == count - 1)
    def _():
        modal_out[...] = total[...].astype(bf16)
        modal = modal_out[...].astype(f32)
        own = jnp.sum(modal * vectors[5:6], axis=1, keepdims=True)
        cross = jnp.sum(modal * partner[6:7], axis=1, keepdims=True)
        met = jnp.sum(modal * tangent[...].astype(f32), axis=1, keepdims=True)
        lane = lax.broadcasted_iota(jnp.int32, (SEQ, 128), 1)
        columns = jnp.where(lane == 0, own, jnp.where(lane == 1, cross, met))
        inner_out[...] = columns.T[:8]


def middle_pass(
    order, places, rows, contexts, tangent, vectors, partner, hidden_bias, wides, downs
):
    count = len(downs)
    slot = FF // count
    return order.call(
        functools.partial(middle_kernel, count),
        [rows, *contexts, tangent, vectors, partner, hidden_bias, *wides, *downs],
        [same_block((SEQ, D)), same_block((SEQ, WIDE)), same_block((SEQ, NARROW))]
        + [same_block((SEQ, D)), same_block((8, D)), same_block((8, D)), slot_block(1, slot)]
        + [in_any] * (2 * count),
        [
            shape_of((SEQ, D), f32),
            shape_of((SEQ, D), bf16),
            shape_of((SEQ, FF), bf16),
            shape_of((SEQ, FF), bf16),
            shape_of((SEQ, D), bf16),
            shape_of((8, SEQ), f32),
        ],
        [
            same_block((SEQ, D)),
            same_block((SEQ, D)),
            slot_block(SEQ, slot),
            slot_block(SEQ, slot),
            same_block((SEQ, D)),
            same_block((8, SEQ)),
        ],
        scratch=[pltpu.VMEM((SEQ, D), f32)] + weight_scratch(count),
        grid=(count,),
        limit=52,
        name="middle",
        prefetch=places,
    )


def gate_kernel(
    own, other, tangent, partner_tangent, vectors, partner, grad_out, low_out, columns_out, sums
):
    gate = jax.nn.sigmoid(own[0:1] + other[1:2])
    gate_two = jax.nn.sigmoid(other[0:1] + own[1:2])
    logit = other[2:3] * gate * (1.0 - gate)
    logit_two = own[2:3] * gate_two * (1.0 - gate_two)
    padding = jnp.zeros((124, SEQ), f32)
    columns = jnp.concatenate([gate, logit, gate_two, logit_two, padding], axis=0).T
    columns_out[...] = columns
    grad = (
        tangent[...].astype(f32)
        + columns[:, 1:2] * vectors[5:6]
        + partner_tangent[...].astype(f32) * columns[:, 2:3]
        + columns[:, 3:4] * partner[6:7]
    )
    grad_out[...] = grad
    low_out[...] = grad.astype(bf16)
    sums[...] = column_sums(grad)


def gate_pass(order, own, other, tangent, partner_tangent, vectors, partner):
    return order.call(
        gate_kernel,
        [own, other, tangent, partner_tangent, vectors, partner],
        [in_vmem] * 6,
        [
            shape_of((SEQ, D), f32),
            shape_of((SEQ, D), bf16),
            shape_of((SEQ, 128), f32),
            shape_of((1, D), f32),
        ],
        [in_vmem] * 4,
        name="gate",
    )


def mix_kernel(own, other, columns, mixed, own_sums, other_sums):
    own_rows = own[...].astype(f32)
    other_rows = other[...].astype(f32)
    mixed[...] = (own_rows + columns[:, 0:1] * other_rows).astype(bf16)
    own_sums[...] = column_sums(columns[:, 1:2] * own_rows)
    other_sums[...] = column_sums(columns[:, 1:2] * other_rows)


def mix_pass(order, own, other, columns):
    return order.call(
        mix_kernel,
        [own, other, columns],
        [in_vmem] * 3,
        [shape_of((SEQ, D), bf16), shape_of((1, D), f32), shape_of((1, D), f32)],
        [in_vmem] * 3,
        name="mix",
    )


def chain_kernel(count, places, low, grad, slope, middle, vectors, *rest):
    wide_parts, down_parts, rest = rest[:count], rest[count : 2 * count], rest[2 * count :]
    upper_out, upper_sums, total_out, total_low_out, context_out, gain_sums, bias_sums = rest[:7]
    normed_grad, w_out, w_up, w_down, out_sems, up_sems, down_sems = rest[7:]
    out_copies, up_copies = wide_copies(places, wide_parts, w_out, w_up, out_sems, up_sems)
    first_copies = down_copies(down_parts, w_down, down_sems)
    step = pl.program_id(0)

    @pl.when(step == 0)
    def _():
        for k in range(count):
            first_copies[k].start()
            start_all(up_copies[k])
        start_all(out_copies)
        normed_grad[...] = jnp.zeros_like(normed_grad)

    for k in range(count):

        @pl.when(step == k)
        def _():
            first_copies[k].wait()
            wait_all(up_copies[k])

    slot = FF // count
    size = 256
    for first in range(0, slot, size):
        part = slice(first, first + size)
        upper = dot_nt(low[...], w_down[step, part]) * slope[:, part].astype(f32)
        upper_sums[:, part] = column_sums(upper)
        upper_out[:, part] = upper.astype(bf16)
    normed_grad[...] += dot_nt(upper_out[...], w_up[step])

    @pl.when(step == count - 1)
    def _():
        wait_all(out_copies)
        scaled, root = normalise(middle[...])
        incoming = normed_grad[...]
        gain_sums[...] = column_sums(incoming * scaled)
        bias_sums[...] = column_sums(incoming)
        total = grad[...] + norm_back(scaled, root, vectors[2:3], incoming)
        total_out[...] = total
        total_low_out[...] = total.astype(bf16)
        context_out[...] = dot_nt(total_low_out[...], w_out[...]).astype(bf16)


def chain_pass(order, places, low, grad, slope, middle, vectors, wides, downs):
    count = len(downs)
    slot = FF // count
    return order.call(
        functools.partial(chain_kernel, count),
        [low, grad, slope, middle, vectors, *wides, *downs],
        [same_block((SEQ, D)), same_block((SEQ, D)), slot_block(SEQ, slot)]
        + [same_block((SEQ, D)), same_block((8, D))]
        + [in_any] * (2 * count),
        [
            shape_of((SEQ, FF), bf16),
            shape_of((1, FF), f32),
            shape_of((SEQ, D), f32),
            shape_of((SEQ, D), bf16),
            shape_of((SEQ, D), bf16),
            shape_of((1, D), f32),
            shape_of((1, D), f32),
        ],
        [slot_block(SEQ, slot), slot_block(1, slot)]
        + [same_block((SEQ, D))] * 3
        + [same_block((1, D))] * 2,
        scratch=[pltpu.VMEM((SEQ, D), f32)] + weight_scratch(count),
        grid=(count,),
        limit=52,
        name="chain",
        prefetch=places,
    )


def slots_of(count):
    return (list(range(0, count, 2)), list(range(1, count, 2)))


def row_grads_kernel(count, widths, lefts, rights, summed, places, *rest):
    left, rest = rest[:lefts], rest[lefts:]
    sources, rest = rest[:rights], rest[rights:]
    if summed:
        pair_low, rest = rest[0], rest[1:]
        pair_low[...] = (sources[0][...] + sources[1][...].astype(f32)).astype(bf16)
        blocks = [pair_low[kind] for kind in range(2)]
    else:
        blocks = []
        for source in sources:
            step = min(source.shape[1], 512)
            blocks += [source[:, k : k + step] for k in range(0, source.shape[1], step)]
    outs, whole = rest[:-1], rest[-1]
    near, far = slots_of(count)
    rows = D // count
    turned = jnp.concatenate([one[...].T for one in left], axis=0)
    each = 2 if far else 1
    for index, width in enumerate(widths):
        low = 0
        while low < width:
            right = blocks.pop(0)
            whole[:, low : low + right.shape[1]] = dot(turned, right).astype(bf16)
            low += right.shape[1]
        for out, slots in zip(outs[each * index : each * index + each], (near, far)):
            for place, slot in enumerate(slots):
                begin = pl.multiple_of(places[slot] * rows, 16)
                out[place] = whole[pl.ds(begin, rows), :width]


def row_grads(order, places, left, sources, widths, count, summed=False):
    near, far = slots_of(count)
    rows = D // count
    outs = []
    for width in widths:
        outs.append(shape_of((len(near), rows, width), bf16))
        if far:
            outs.append(shape_of((len(far), rows, width), bf16))
    low = [shape_of(sources[0].shape, bf16)] if summed else []
    return order.call(
        functools.partial(row_grads_kernel, count, widths, len(left), len(sources), summed),
        [places, *left, *sources],
        [in_smem] + [in_vmem] * (len(left) + len(sources)),
        low + outs,
        [in_vmem] * len(low + outs),
        scratch=[pltpu.VMEM((D, max(widths)), bf16)],
        limit=32,
        name="row_grads",
    )


def down_grads_kernel(count, first, height, fold, places, low, hidden, *outs):
    near, far = slots_of(count)
    width = FF // count
    turned = low[:, first : first + height].T
    rows = height // fold
    for out, slots in zip(outs, (near, far)):
        for place, slot in enumerate(slots):
            begin = pl.multiple_of(places[slot] * width, 128)
            block = dot(turned, hidden[:, pl.ds(begin, width)]).astype(bf16)
            for k in range(fold):
                out[place, :, k * width : (k + 1) * width] = block[k * rows : (k + 1) * rows]


def down_grads(order, places, low, hidden, first, height, fold, count):
    near, far = slots_of(count)
    width = FF // count
    outs = [shape_of((len(near), height // fold, fold * width), bf16)]
    if far:
        outs.append(shape_of((len(far), height // fold, fold * width), bf16))
    return order.call(
        functools.partial(down_grads_kernel, count, first, height, fold),
        [places, low, hidden],
        [in_smem, in_vmem, in_vmem],
        outs,
        [in_vmem] * len(outs),
        limit=32,
        name="down_grads",
    )


def by_rows(width):
    return pl.BlockSpec((ROWS, width), lambda step: (step, 0))


def whole_block(dims):
    return pl.BlockSpec(dims, lambda step: (0,) * len(dims))


def first_kernel(count, places, queries, pairs, total, rows, vectors, short, *rest):
    parts, rest = rest[:count], rest[count:]
    grad_out, short_out, weight, sems = rest
    copies = part_copies(places, parts, weight, sems)

    @pl.when(pl.program_id(0) == 0)
    def _():
        start_all(copies)
        short_out[...] = jnp.zeros_like(short_out)
        gain_two, bias_two, output_bias, gate_self, gate_cross, hidden_bias = short
        for line, member in enumerate((gain_two, bias_two, output_bias, gate_self, gate_cross)):
            short_out[line + 2 : line + 3] = member[...]
        for line in range(FF // D):
            short_out[line + 8 : line + 9] = hidden_bias[:, line * D : (line + 1) * D]
        wait_all(copies)

    normed_grad = jnp.zeros((ROWS, D), f32)
    for group in range(GROUPS):
        first = group * THIRD
        normed_grad += dot_nt(queries[group][...], weight[:, first : first + THIRD])
        for kind in range(2):
            start = (kind + 1) * D + first
            normed_grad += dot_nt(pairs[group][kind], weight[:, start : start + THIRD])
    scaled, root = normalise(rows[...].astype(f32))
    short_out[0:1] += column_sums(normed_grad * scaled)
    short_out[1:2] += column_sums(normed_grad)
    grad_out[...] = total[...] + norm_back(scaled, root, vectors[0:1], normed_grad)


def first_pass(order, places, queries, pairs, total, rows, vectors, short, parts):
    count = len(parts)
    pair = pl.BlockSpec((2, ROWS, THIRD), lambda step: (0, step, 0))
    shorts = len(short)

    def kernel(places_ref, q0, q1, q2, p0, p1, p2, total_ref, rows_ref, vectors_ref, *rest):
        first_kernel(
            count,
            places_ref,
            (q0, q1, q2),
            (p0, p1, p2),
            total_ref,
            rows_ref,
            vectors_ref,
            rest[:shorts],
            *rest[shorts:],
        )

    return order.call(
        kernel,
        [places, *queries, *pairs, total, rows, vectors, *short, *parts],
        [in_smem]
        + [by_rows(THIRD)] * GROUPS
        + [pair] * GROUPS
        + [by_rows(D), by_rows(D), whole_block((8, D))]
        + [whole_block(member.shape) for member in short]
        + [in_any] * count,
        [shape_of((SEQ, D), f32), shape_of((16, D), f32)],
        [by_rows(D), whole_block((16, D))],
        scratch=[pltpu.VMEM((D, 3 * D), bf16), pltpu.SemaphoreType.DMA((count,))],
        grid=(SEQ // ROWS,),
        limit=28,
        name="first",
    )


def settle_kernel(kind, count, places, *refs):
    totals, returned, outs = refs[:count], refs[count : 2 * count], refs[2 * count :]
    inner = jnp.logical_and(places[4] > 0, places[4] < 3)
    values = [jnp.where(inner, a[...], b[...]).astype(f32) for a, b in zip(totals, returned)]
    out = outs[0]
    if kind == "turn":
        first = 0
        for value in values:
            rows = value.shape[0]
            for k in range(0, value.shape[1], D):
                out[:, first : first + rows] = value[:, k : k + D].T
                first += rows
    elif kind == "columns":
        first = 0
        for value in values:
            out[:, first : first + value.shape[1]] = value
            first += value.shape[1]
    else:
        outs[1][...] = values[0][:, :D]
        out[:, :D] = values[0][:, D:]
        for group in range(GROUPS):
            for part in range(2):
                start = (part + 1) * D + group * THIRD
                block = values[1 + group][:, part * THIRD : (part + 1) * THIRD]
                out[:, start : start + THIRD] = block


def settle(order, kind, places, blocks, dims):
    count = len(blocks)
    found = order.call(
        functools.partial(settle_kernel, kind, count),
        [places] + [block[0] for block in blocks] + [block[1] for block in blocks],
        [in_smem] + [in_vmem] * (2 * count),
        [shape_of(each, f32) for each in dims],
        [in_vmem] * len(dims),
        name="settle",
    )
    return found[0] if len(dims) == 1 else found


def swap_bit(value, axis, bit):
    size = lax.axis_size(axis)
    return lax.ppermute(value, axis, [(source, source ^ (1 << bit)) for source in range(size)])


def from_partner(value):
    size = lax.axis_size("stream")
    half = size // 2
    return lax.ppermute(value, "stream", [(source, (source + half) % size) for source in range(size)])


def along(value, pairs):
    return lax.ppermute(value, "dp", pairs)


def up_line(value, steps):
    return along(value, [(floor, floor + 1) for floor in range(steps - 1, 3)])


def down_line(value, steps):
    return along(value, [(floor, floor - 1) for floor in range(1, 5 - steps)])


def swap_outer(value):
    return along(value, [(0, 1), (1, 0), (2, 3), (3, 2)])


def to_inner(value):
    return along(value, [(0, 1), (3, 2)])


def over_middle(value):
    return along(value, [(1, 2), (2, 1)])


def to_outer(value):
    return along(value, [(1, 0), (2, 3)])


def core(value):
    return swap_bit(value, "stream", 0)


def across(value):
    return swap_bit(value, "stream", 1)


def modality_groups():
    size = lax.axis_size("stream")
    half = size // 2
    return [list(range(half)), list(range(half, size))]


def body(
    regions,
    cotangent,
    page_lens,
    qkv_weight,
    out_weight,
    up_weight,
    down_weight,
    ln1_gain,
    ln1_bias,
    ln2_gain,
    ln2_bias,
    up_bias,
    down_bias,
    gate_own,
    gate_other,
):
    half = lax.axis_size("stream") // 2
    depth = lax.axis_size("dp")
    paired = half == 4 and depth == 4
    side = lax.axis_index("stream") % half
    floor = lax.axis_index("dp")
    count = 4 if paired else 1
    slots = jnp.arange(4, dtype=jnp.int32)
    picks = jnp.bitwise_xor(side.astype(jnp.int32), slots) if paired else jnp.zeros_like(slots)
    places = jnp.concatenate([picks, floor.astype(jnp.int32)[None]])
    order = Order()
    short = (ln1_gain, ln1_bias, ln2_gain, ln2_bias, down_bias, gate_own, gate_other, up_bias)
    sizes = [member.size for member in short]
    partner_tangent = from_partner(cotangent)

    lengths = lax.dynamic_slice_in_dim(page_lens, side * depth + floor, 1, 0)
    positions = jnp.arange(SEQ, dtype=jnp.int32)
    page_ends = jnp.cumsum(lengths[0], dtype=jnp.int32)
    pages = jnp.sum((page_ends[:, None] <= positions[None, :]).astype(jnp.int32), axis=0)
    page_row, page_column = pages[None, :], pages[:, None]

    def attend_all(wide, other):
        first, cost = (0, 0) if wide is own_wide else (WIDE // PAIR, 60)
        return attend(order, first, queries, wide, other, page_row, page_column, cost)

    if paired:
        (qkv_shard,) = cast_pass(order, [qkv_weight])
        qkv_across, qkv_near = across(qkv_shard), core(qkv_shard)
        short_all = jnp.concatenate(short)[None]
        down_shard, down_slice, short_shard = pack_pass(order, places, down_weight, short_all, sizes)
        short_across, slice_across = across(short_shard), across(down_slice)
        wide_shard = wide_cast_pass(order, out_weight, up_weight)
        wide_near, down_near = core(wide_shard), core(down_shard)
        short_pair = stack_pass(order, short_shard, short_across)
        (qkv_across,) = order.hold([qkv_across], waits=[partner_tangent])
        short_far, qkv_far = core(short_pair), core(qkv_across)
        qkv_parts = [qkv_shard, qkv_near, qkv_across, qkv_far]
        queries, own_wide, own_narrow, normed, vectors, hidden_bias = project(
            order, places, regions, qkv_parts, (short_pair, short_far), [wide_near, down_near]
        )
        other_wide, other_narrow = from_partner(own_wide), from_partner(own_narrow)
        own_slice, wide_shard = order.hold([slice_across, wide_shard])
        wide_across = across(wide_shard)
        up_one, down_one = up_line(own_slice, 1), down_line(own_slice, 1)
        up_one, down_one = order.hold([up_one, down_one])
        up_two, down_two = up_line(up_one, 2), down_line(down_one, 2)
        up_two, down_two = order.hold([up_two, down_two])
        up_three, down_three = up_line(up_two, 3), down_line(down_two, 3)
        context_wide, logs_wide = attend_all(own_wide, other_wide)
        pieces = (own_slice, up_one, up_two, up_three, down_one, down_two, down_three)
        down_across = line_pass(order, places, pieces)
        down_far = core(down_across)
        wide_across, vectors = order.hold([wide_across, vectors])
        partner = from_partner(vectors)
        wide_far = core(wide_across)
        context_narrow, logs_narrow = attend_all(own_narrow, other_narrow)
        wide_parts = [wide_shard, wide_near, wide_across, wide_far]
        down_parts = [down_shard, down_near, down_across, down_far]
    else:

        def gather(shard):
            return [
                lax.all_gather(shard, "stream", axis_index_groups=modality_groups(), tiled=True)
            ]

        packed = jnp.concatenate([member.astype(bf16) for member in short])[None]
        found = gather(packed)[0].astype(f32)
        shard = D // half
        rows = [found[:, k * shard : (k + 1) * shard].reshape(1, D) for k in range(7)]
        given = (
            jnp.concatenate(rows + [jnp.zeros((1, D), f32)], axis=0),
            found[:, 7 * shard :].reshape(1, FF),
        )
        qkv_parts = gather(qkv_weight.astype(bf16))
        wide_parts = gather(jnp.concatenate([out_weight, up_weight], axis=1).astype(bf16))
        down_parts = gather(down_weight.astype(bf16))
        queries, own_wide, own_narrow, normed, vectors, hidden_bias = project(
            order, places, regions, qkv_parts, given
        )
        other_wide, other_narrow = from_partner(own_wide), from_partner(own_narrow)
        partner = from_partner(vectors)
        context_wide, logs_wide = attend_all(own_wide, other_wide)
        context_narrow, logs_narrow = attend_all(own_narrow, other_narrow)

    contexts = [context_wide, context_narrow]
    middle, second, hidden, slope, modal, inner_own = middle_pass(
        order,
        places,
        regions,
        contexts,
        partner_tangent,
        vectors,
        partner,
        hidden_bias,
        wide_parts,
        down_parts,
    )
    inner_other = from_partner(inner_own)
    modal_grad, modal_low, columns, output_bias_grad = gate_pass(
        order, inner_own, inner_other, cotangent, partner_tangent, vectors, partner
    )

    def attend_back_group(group):
        query_first = group * THIRD // PAIR
        wide = group * THIRD < WIDE
        query_grad, own_grad, other_grad = attend_back(
            order,
            query_first,
            query_first if wide else 0,
            queries,
            own_wide if wide else own_narrow,
            other_wide if wide else other_narrow,
            context_grad,
            logs_wide if wide else logs_narrow,
            page_row,
            page_column,
        )
        query_grads.append(query_grad)
        own_grads.append(own_grad)
        returned.append(from_partner(other_grad))

    def pair_group(group):
        pair_grad, *flat = row_grads(
            order,
            places,
            [normed],
            [own_grads[group], returned[group]],
            [2 * THIRD],
            count,
            summed=True,
        )
        pair_grads.append(pair_grad)
        return flat

    def last_pass():
        short_grads = (
            gain_two_grad,
            bias_two_grad,
            output_bias_grad,
            gate_self_grad,
            gate_cross_grad,
            hidden_bias_grad,
        )
        return first_pass(
            order,
            places,
            query_grads,
            pair_grads,
            middle_grad,
            regions,
            vectors,
            short_grads,
            qkv_parts,
        )

    query_grads, own_grads, returned, pair_grads = [], [], [], []
    if paired:
        d1, far = down_grads(order, places, modal_low, hidden, 0, 384, 2, count)
        d1_core = core(far)
        d2, far = down_grads(order, places, modal_low, hidden, 384, 384, 2, count)
        d2_core = core(far)
        (modal,) = order.hold([modal])
        partner_modal = from_partner(modal)
        d1, away = sums_pass(order, places, folds=[[(d1, d1_core)]])
        d1_in = across(away)
        upper_low, hidden_bias_grad, middle_grad, middle_low, context_grad, gain_two_grad, bias_two_grad = (
            chain_pass(
                order, places, modal_low, modal_grad, slope, middle, vectors, wide_parts, down_parts
            )
        )
        u1, far_one, u2, far_two = row_grads(order, places, [second], [upper_low], [1536, 1536], count)
        u1_core, u2_core = core(far_one), core(far_two)
        d2, away, d1 = sums_pass(order, places, folds=[[(d2, d2_core)]], adds=[(d1, d1_in)])
        d2_in, d1_in = across(away), to_inner(d1)
        attend_back_group(0)
        mixed_rows, gate_self_grad, gate_cross_grad = mix_pass(order, modal, partner_modal, columns)
        o1, far_one = row_grads(order, places, contexts, [middle_low], [D], count)
        o1_core = core(far_one)
        u1, away, u2, away_two, d2, d1 = sums_pass(
            order,
            places,
            folds=[[(u1, u1_core)], [(u2, u2_core)]],
            adds=[(d2, d2_in), (d1, d1_in)],
        )
        u1_in, d2_in, d1_mid = across(away), to_inner(d2), over_middle(d1)
        attend_back_group(1)
        d2, u1, u1_pay = sums_pass(
            order,
            places,
            adds=[(d2, d2_in)],
            pays=[(u1, u1_in, d1, d1_mid)],
            waits=[returned[0], o1_core],
        )
        (away_two,) = order.hold([away_two])
        u2_in, u1_in, d2_mid = across(away_two), swap_outer(u1_pay), over_middle(d2)
        attend_back_group(2)
        q1, far_two = row_grads(order, places, [normed], query_grads, [D], count)
        q1_core = core(far_two)
        p1, far = pair_group(0)
        p1_core = core(far)
        u1, u2, u2_pay = sums_pass(
            order, places, adds=[(u1, u1_in)], pays=[(u2, u2_in, d2, d2_mid)], waits=[returned[1]]
        )
        d1_out = u1_in
        u2_in, u1_mid = swap_outer(u2_pay), over_middle(u1)
        oq, away, p1, away_two = sums_pass(
            order, places, folds=[[(o1, o1_core), (q1, q1_core)], [(p1, p1_core)]]
        )
        oq_in, p1_in = across(away), across(away_two)
        p2, far = pair_group(1)
        p2_core = core(far)
        p3, far = pair_group(2)
        p3_core = core(far)
        region_grad, short_rows = last_pass()
        s_core = core(short_rows)
        p2, away, p3, away_two, u2, short_rows, oq, oq_pay = sums_pass(
            order,
            places,
            folds=[[(p2, p2_core)], [(p3, p3_core)]],
            adds=[(u2, u2_in), (short_rows, s_core)],
            pays=[(oq, oq_in, u1, u1_mid)],
            waits=[p1_in],
        )
        d2_out = u2_in
        oq_in, u2_mid = swap_outer(oq_pay), over_middle(u2)
        p2_in, p3_in, s_in = across(away), across(away_two), across(short_rows)
        down_grad = settle(order, "turn", places, [(u1_pay, d1_out), (u2_pay, d2_out)], [(D, D)])
        p1, p2, p3, short_rows = sums_pass(
            order, places, adds=[(p1, p1_in), (p2, p2_in), (p3, p3_in), (short_rows, s_in)]
        )
        p1_in, p2_in, p3_in = to_inner(p1), to_inner(p2), to_inner(p3)
        oq, u2 = sums_pass(order, places, adds=[(oq, oq_in), (u2, u2_mid)])
        u1_out = oq_in
        oq_mid, u2_out = over_middle(oq), to_outer(u2)
        p1, p2 = sums_pass(order, places, adds=[(p1, p1_in), (p2, p2_in)])
        s_in = to_inner(short_rows)
        p1_mid, p2_mid = over_middle(p1), over_middle(p2)
        p3, oq = sums_pass(order, places, adds=[(p3, p3_in), (oq, oq_mid)], waits=[u2_out])
        p3_mid, oq_out = over_middle(p3), to_outer(oq)
        up_grad = settle(order, "columns", places, [(oq_pay, u1_out), (u2, u2_out)], [(D // 4, FF)])
        short_rows, p1, p2 = sums_pass(
            order, places, adds=[(short_rows, s_in), (p1, p1_mid), (p2, p2_mid)]
        )
        s_mid, p1_out, p2_out = over_middle(short_rows), to_outer(p1), to_outer(p2)
        p3, short_rows = sums_pass(order, places, adds=[(p3, p3_mid), (short_rows, s_mid)])
        p3_out, s_out = to_outer(p3), to_outer(short_rows)
        qkv_grad, out_grad = settle(
            order,
            "pairs",
            places,
            [(oq, oq_out), (p1, p1_out), (p2, p2_out), (p3, p3_out)],
            [(D // 4, 3 * D), (D // 4, D)],
        )
        inner = jnp.logical_and(floor > 0, floor < 3)
        short_rows = jnp.where(inner, short_rows, s_out)
    else:
        (down_block,) = down_grads(order, places, modal_low, hidden, 0, D, 1, count)
        upper_low, hidden_bias_grad, middle_grad, middle_low, context_grad, gain_two_grad, bias_two_grad = (
            chain_pass(
                order, places, modal_low, modal_grad, slope, middle, vectors, wide_parts, down_parts
            )
        )
        (up_block,) = row_grads(order, places, [second], [upper_low], [FF], count)
        (out_block,) = row_grads(order, places, contexts, [middle_low], [D], count)
        for group in range(GROUPS):
            attend_back_group(group)
        partner_modal = from_partner(modal)
        mixed_rows, gate_self_grad, gate_cross_grad = mix_pass(order, modal, partner_modal, columns)
        (query_block,) = row_grads(order, places, [normed], query_grads, [D], count)
        pair_blocks = [pair_group(group)[0] for group in range(GROUPS)]
        region_grad, short_rows = last_pass()

        def total(block):
            groups = modality_groups()
            owned = lax.psum_scatter(
                block.astype(f32), "stream", axis_index_groups=groups, tiled=True
            )
            return lax.psum(owned, "dp")

        down_grad = total(down_block[0].T)
        up_grad, out_grad = total(up_block[0]), total(out_block[0])
        qkv_grad = total(
            jnp.concatenate(
                [query_block[0]]
                + [block[0, :, :THIRD] for block in pair_blocks]
                + [block[0, :, THIRD:] for block in pair_blocks],
                axis=1,
            )
        )
        short_rows = lax.psum(
            lax.psum(short_rows, "stream", axis_index_groups=modality_groups()), "dp"
        )

    shard = D // half
    own_rows = lax.dynamic_slice_in_dim(short_rows, side * shard, shard, 1)
    hidden_rows = short_rows[8 : 8 + FF // D].reshape(FF)
    own_hidden = lax.dynamic_slice_in_dim(hidden_rows, side * (FF // half), FF // half, 0)
    return (
        mixed_rows,
        region_grad,
        qkv_grad,
        out_grad,
        up_grad,
        down_grad,
        own_rows[0],
        own_rows[1],
        own_rows[2],
        own_rows[3],
        own_hidden,
        own_rows[4],
        own_rows[5],
        own_rows[6],
    )


def solution(mesh):
    in_specs = (
        P(("stream", "dp"), None),
        P(("stream", "dp"), None),
        P(),
        P("stream", None),
        P("stream", None),
        P("stream", None),
        P("stream", None),
        P("stream"),
        P("stream"),
        P("stream"),
        P("stream"),
        P("stream"),
        P("stream"),
        P("stream"),
        P("stream"),
    )
    out_specs = (
        P(("stream", "dp"), None),
        P(("stream", "dp"), None),
        P("stream", None),
        P("stream", None),
        P("stream", None),
        P("stream", None),
        P("stream"),
        P("stream"),
        P("stream"),
        P("stream"),
        P("stream"),
        P("stream"),
        P("stream"),
        P("stream"),
    )
    return jax.shard_map(body, mesh=mesh, in_specs=in_specs, out_specs=out_specs, check_vma=False)
```

time: 472 us -> 319 us (0.68)
  waiting for transfers between devices: 217 us -> 78.7 us
  other arithmetic: 31.4 us -> 0.33 us
  Pallas kernels: 97.9 us -> 116 us
  starting transfers between devices: 81.7 us -> 92.7 us
  local copies, waits for them, and re-layouts: 32.8 us -> 22.5 us
    ppermute x30, waiting for transfers between devices: 130 us -> 36.2 us  [along(): return lax.ppermute(value, 'dp', pairs)]
    ppermute x32 -> x30, waiting for transfers between devices: 73.4 us -> 26 us  [swap_bit(): lax.ppermute(value, axis, [(source, source ^ 1 << bit) for source in rang...]
    convert_element_type x53 -> x0, other arithmetic: 27.4 us -> none  [the longest x36 12.2 us: add_low(): return (left.astype(f32) + right.astype(f32)).astype(left.dtype)]
    pallas_call x19 -> x47, Pallas kernels: 97.9 us -> 116 us  [call(): pl.pallas_call(wrapped, out_shape=outs, grid_spec=pltpu.PrefetchScalarGri...]
    ppermute x30, starting transfers between devices: 45.8 us -> 61.8 us  [along(): return lax.ppermute(value, 'dp', pairs)]
    unnamed x150 -> x124, local copies, waits for them, and re-layouts: 27.7 us -> 20.8 us
    ppermute x10 -> x9, starting transfers between devices: 12.9 us -> 9.52 us  [from_partner(): lax.ppermute(value, 'stream', [(source, (source + half) % size) for sourc...]
    ppermute x10 -> x9, waiting for transfers between devices: 14 us -> 16.5 us  [from_partner(): lax.ppermute(value, 'stream', [(source, (source + half) % size) for sourc...]
  transfers between devices with their start and end apart: 72 -> 69, of which waited for: 25 -> 22; matrix products, arithmetic and copies ran while one was open for 6% -> 1% of each run, Pallas kernels for 12% -> 28%
where the time goes in v2:
time: 319 us; the launch traced here: 313 us
  Pallas kernels  116 us (36%)
  starting transfers between devices  92.7 us (29%)
  waiting for transfers between devices  78.7 us (25%)
  local copies, waits for them, and re-layouts  22.5 us (7%)
    pallas_call x47, Pallas kernels, call(): pl.pallas_call(wrapped, out_shape=outs, grid_spec=pltpu.PrefetchScalarGri...  116 us
    ppermute x30, starting transfers between devices, along(): return lax.ppermute(value, 'dp', pairs)  61.8 us
    ppermute x30, waiting for transfers between devices, along(): return lax.ppermute(value, 'dp', pairs)  36.2 us
    ppermute x30, waiting for transfers between devices, swap_bit(): lax.ppermute(value, axis, [(source, source ^ 1 << bit) for source in rang...  26 us
    ppermute x30, starting transfers between devices, swap_bit(): lax.ppermute(value, axis, [(source, source ^ 1 << bit) for source in rang...  21.4 us
    unnamed x124, local copies, waits for them, and re-layouts  20.8 us
    ppermute x9, waiting for transfers between devices, from_partner(): lax.ppermute(value, 'stream', [(source, (source + half) % size) for sourc...  16.5 us
    ppermute x9, starting transfers between devices, from_partner(): lax.ppermute(value, 'stream', [(source, (source + half) % size) for sourc...  9.52 us
  transfers between devices with their start and end apart: 69, of which 22 were waited for; matrix products, arithmetic and copies ran while one was open for 1% of the time, Pallas kernels for 28%

profile of v2, /device:TPU:0, one launch (start us, length us, event | category | flops | bytes accessed | tf_op | source)
XLA Modules:
  0.0 312.6 jit_solution(17586262737607214165)
XLA Ops:
  2.3 3.0 collective-permute-start.3
  7.1 1.7 copy-done.32
  13.2 12.2 %collective-permute-done.refs_1_ = bf16[16,768]{1,0:T(8,128)(2,1)S(1)} collective-permute-done((bf16[16,768]{1,0:T(8,128)(2,1)S(1)}, bf16[16,768]{1,0:T(8,128)(2,1)S(1)}, u32[]{:S(2)}, u32[]{:S(2)}) %collective-permute-start) | collective-permute-done | bytes 24608 | tf_op jit(solution)/shard_map/ppermute | solution.py:1017
  26.2 3.1 collective-permute-done.1.refs_3_
  29.2 1.7 collective-permute-start.9
  31.1 4.4 %project.1 = (bf16[512,768]{1,0:T(8,128)(2,1)S(1)}, bf16[2,512,512]{2,1,0:T(8,128)(2,1)S(1)}, bf16[2,512,256]{2,1,0:T(8,128)(2,1)}, bf16[512,768]{1,0:T(8,128)(2...) custom-call(s32[5]{0:T(128)S(1)} %pad_add_fusion.refs_0_, bf16[512,768]{1,0:T(8,128)(2,1)S(1)} %copy-done.20, ...), custom_call_target="tpu_custom_call" | custom-call | flops 1 | bytes 1 | tf_op jit(solution)/shard_map/project/pallas_call | solution.py:108
  36.4 1.9 collective-permute-done.9.refs_0_
  38.3 1.7 collective-permute-start.15
  41.6 3.5 %collective-permute-start.10 = (bf16[192,768]{1,0:T(8,128)(2,1)S(1)}, bf16[192,768]{1,0:T(8,128)(2,1)S(1)}, u32[]{:S(2)}, u32[]{:S(2)}) collective-permute-start(bf16[192,768]{1,0:T(8,128)(2,1)S(1)} %get-tuple-element.139.refs_2_.refs_1_), channel_id=1, source_target_pairs={{0,1},{1,2},{2,3},{4,5},{5,6},{6,7},{8,9},{9,10},{10,11},{12,13},{... | collective-permute-start | bytes 884744 | tf_op jit(solution)/shard_map/ppermute | solution.py:1027
  46.3 3.8 %collective-permute-done.10.refs_0_ = bf16[192,768]{1,0:T(8,128)(2,1)S(1)} collective-permute-done((bf16[192,768]{1,0:T(8,128)(2,1)S(1)}, bf16[192,768]{1,0:T(8,128)(2,1)S(1)}, u32[]{:S(2)}, u32[]{:S(2)}) %collective-permute-start.10) | collective-permute-done | bytes 294944 | tf_op jit(solution)/shard_map/ppermute | solution.py:1027
  50.2 4.1 %collective-permute-done.11.refs_1_ = bf16[192,768]{1,0:T(8,128)(2,1)S(1)} collective-permute-done((bf16[192,768]{1,0:T(8,128)(2,1)S(1)}, bf16[192,768]{1,0:T(8,128)(2,1)S(1)}, u32[]{:S(2)}, u32[]{:S(2)}) %collective-permute-start.11) | collective-permute-done | bytes 294944 | tf_op jit(solution)/shard_map/ppermute | solution.py:1027
  56.9 9.2 %collective-permute-done.13.refs_1_ = bf16[192,768]{1,0:T(8,128)(2,1)} collective-permute-done((bf16[192,768]{1,0:T(8,128)(2,1)S(1)}, bf16[192,768]{1,0:T(8,128)(2,1)}, u32[]{:S(2)}, u32[]{:S(2)}) %collective-permute-start.13) | collective-permute-done | bytes 294944 | tf_op jit(solution)/shard_map/ppermute | solution.py:1027
  70.5 7.7 %attend.2 = (bf16[512,512]{1,0:T(8,128)(2,1)S(1)}, f32[4,2,512]{2,1,0:T(2,128)S(1)}) custom-call(bf16[512,768]{1,0:T(8,128)(2,1)S(1)} %copy-done.7, bf16[2,512,512]{2,1,0:T(8,128)(2,1)S(1)} %get-tuple-element.136.refs_1_.refs_2_, bf16[2,512,512]{2,1,0:T(8,128)(2,1)S(1)} %get-tuple-element.136.refs_1_.refs_2_, ...), custom_call_target="tpu_custom_call" | custom-call | flops 1 | bytes 1 | tf_op jit(solution)/shard_map/attend/pallas_call | solution.py:108
  78.3 2.0 line.1.refs_2_.refs_14_.refs_12_
  81.9 4.9 %attend.3 = (bf16[512,256]{1,0:T(8,128)(2,1)S(1)}, f32[2,2,512]{2,1,0:T(2,128)S(1)}) custom-call(bf16[512,768]{1,0:T(8,128)(2,1)S(1)} %copy-done.8, bf16[2,512,256]{2,1,0:T(8,128)(2,1)} %get-tuple-element.144.refs_1_.refs_2_, bf16[2,512,256]{2,1,0:T(8,128)(2,1)} %get-tuple-element.144.refs_1_.refs_2_, ...), custom_call_target="tpu_custom_call" | custom-call | flops 60000002048 | bytes 62914560 | tf_op jit(solution)/shard_map/attend/pallas_call | solution.py:108
  88.3 18.2 %middle.1 = (f32[512,768]{1,0:T(8,128)}, bf16[512,768]{1,0:T(8,128)(2,1)S(1)}, bf16[512,3072]{1,0:T(8,128)(2,1)}, bf16[512,3072]{1,0:T(8,128)(2,1)}, bf16[512,768]{1,0:T(8,128)(2,1)}, /*index=5*/f32[8,512]{1,0:T(8,128)S(1)}) custom-call(s32[5]{0:T(128)S(1)} %pad_add_fusion.refs_0_, bf16[512,768]{1,0:T(8,128)(2,1)} %refs_8_.1, ...), custom_call_target="tpu_custom_call" | custom-call | flops 1 | bytes 1 | tf_op jit(solution)/shard_map/middle/pallas_call | solution.py:108
  107.7 2.6 collective-permute-done.21.refs_1_
  110.3 1.9 gate.1
  113.4 2.3 copy-done.9
  115.6 2.0 down_grads.2
  117.7 3.0 down_grads.3
  123.3 15.9 %chain.1 = (bf16[512,3072]{1,0:T(8,128)(2,1)}, f32[1,3072]{1,0:T(1,128)S(1)}, f32[512,768]{1,0:T(8,128)}, bf16[512,768]{1,0:T(8,128)(2,1)S(1)}, bf16[512,768]{1,...) custom-call(s32[5]{0:T(128)S(1)} %pad_add_fusion.refs_0_, bf16[512,768]{1,0:T(8,128)(2,1)} %copy-done.15, ...), custom_call_target="tpu_custom_call" | custom-call | flops 1 | bytes 1 | tf_op jit(solution)/shard_map/chain/pallas_call | solution.py:108
  139.3 1.9 copy-done.27
  142.3 3.4 %row_grads.6 = (bf16[2,192,1536]{2,1,0:T(8,128)(2,1)S(1)}, bf16[2,192,1536]{2,1,0:T(8,128)(2,1)S(1)}, bf16[2,192,1536]{2,1,0:T(8,128)(2,1)S(1)}, bf16[2,192,1536]{2,1,0:T(8,128)(2,1)S(1)}) custom-call(s32[5]{0:T(128)S(1)} %pad_add_fusion.refs_0_, bf16[512,768]{1,0:T(8,128)(2,1)S(1)} %copy-done.42, bf16[512,3072]{1,0:T(8,128)(2,1)S(1)} %copy-done.27, ...), custom_call_target="tpu_custom_call" | custom-call | flops 1 | bytes 1 | tf_op jit(solution)/shard_map/row_grads/pallas_call | solution.py:108
  150.5 5.2 %collective-permute-start.29 = (bf16[192,1536]{1,0:T(8,128)(2,1)S(1)}, bf16[192,1536]{1,0:T(8,128)(2,1)S(1)}, u32[]{:S(2)}, u32[]{:S(2)}) collective-permute-start(bf16[192,1536]{1,0:T(8,128)(2,1)S(1)} %get-tuple-element.180.refs_7_), channel_id=1, source_target_pairs={{0,1},{3,2},{4,5},{7,6},{8,9},{11,10},{12,13},{15,14},{16,17},{19,... | collective-permute-start | bytes 1769480 | tf_op jit(solution)/shard_map/ppermute | solution.py:1027
  155.8 5.7 %attend_back.3 = (bf16[512,256]{1,0:T(8,128)(2,1)S(1)}, f32[2,512,256]{2,1,0:T(8,128)S(1)}, bf16[2,512,256]{2,1,0:T(8,128)(2,1)S(1)}) custom-call(bf16[512,768]{1,0:T(8,128)(2,1)S(1)} %copy-done.8, bf16[2,512,512]{2,1,0:T(8,128)(2,1)S(1)} %get-tuple-element.136.refs_1_.refs_2_, bf16[2,512,512]{2,1,0:T(8,128)(2,1)S(1)} %get-tuple-element.136.refs_1_.refs_2_, ...), custom_call_target="tpu_custom_call" | custom-call | flops 1 | bytes 1 | tf_op jit(solution)/shard_map/attend_back/pallas_call | solution.py:108
  161.5 4.3 %collective-permute-done.22.refs_1_ = bf16[512,768]{1,0:T(8,128)(2,1)S(1)} collective-permute-done((bf16[512,768]{1,0:T(8,128)(2,1)S(1)}, bf16[512,768]{1,0:T(8,128)(2,1)S(1)}, u32[]{:S(2)}, u32[]{:S(2)}) %collective-permute-start.22) | collective-permute-done | bytes 786464 | tf_op jit(solution)/shard_map/ppermute | solution.py:1023
  172.6 5.2 %collective-permute-start.30 = (bf16[192,1536]{1,0:T(8,128)(2,1)S(1)}, bf16[192,1536]{1,0:T(8,128)(2,1)S(1)}, u32[]{:S(2)}, u32[]{:S(2)}) collective-permute-start(bf16[192,1536]{1,0:T(8,128)(2,1)S(1)} %get-tuple-element.187.refs_1_), channel_id=1, source_target_pairs={{0,1},{3,2},{4,5},{7,6},{8,9},{11,10},{12,13},{15,14},{16,17},{19,... | collective-permute-start | bytes 1769480 | tf_op jit(solution)/shard_map/ppermute | solution.py:1027
  181.2 5.7 %attend_back.4 = (bf16[512,256]{1,0:T(8,128)(2,1)S(1)}, f32[2,512,256]{2,1,0:T(8,128)S(1)}, bf16[2,512,256]{2,1,0:T(8,128)(2,1)S(1)}) custom-call(bf16[512,768]{1,0:T(8,128)(2,1)S(1)} %copy-done.8, bf16[2,512,512]{2,1,0:T(8,128)(2,1)S(1)} %get-tuple-element.136.refs_1_.refs_2_, bf16[2,512,512]{2,1,0:T(8,128)(2,1)S(1)} %get-tuple-element.136.refs_1_.refs_2_, ...), custom_call_target="tpu_custom_call" | custom-call | flops 1 | bytes 1 | tf_op jit(solution)/shard_map/attend_back/pallas_call | solution.py:108
  186.9 7.0 %collective-permute-done.33.refs_8_.refs_3_ = bf16[2,512,256]{2,1,0:T(8,128)(2,1)S(1)} collective-permute-done((bf16[2,512,256]{2,1,0:T(8,128)(2,1)S(1)}, bf16[2,512,256]{2,1,0:T(8,128)(2,1)S(1)}, u32[]{:S(2)}, u32[]{:S(2)}) %collective-permute-start.33) | collective-permute-done | bytes 524320 | tf_op jit(solution)/shard_map/ppermute | solution.py:1023
  197.0 1.8 collective-permute-start.38
  199.6 6.5 %attend_back.5 = (bf16[512,256]{1,0:T(8,128)(2,1)S(1)}, f32[2,512,256]{2,1,0:T(8,128)S(1)}, bf16[2,512,256]{2,1,0:T(8,128)(2,1)S(1)}) custom-call(bf16[512,768]{1,0:T(8,128)(2,1)S(1)} %copy-done.8, bf16[2,512,256]{2,1,0:T(8,128)(2,1)} %get-tuple-element.144.refs_1_.refs_2_, bf16[2,512,256]{2,1,0:T(8,128)(2,1)} %get-tuple-element.144.refs_1_.refs_2_, ...), custom_call_target="tpu_custom_call" | custom-call | flops 1 | bytes 1 | tf_op jit(solution)/shard_map/attend_back/pallas_call | solution.py:108
  215.1 3.8 %collective-permute-start.45 = (bf16[192,1536]{1,0:T(8,128)(2,1)S(1)}, bf16[192,1536]{1,0:T(8,128)(2,1)S(1)}, u32[]{:S(2)}, u32[]{:S(2)}) collective-permute-start(bf16[192,1536]{1,0:T(8,128)(2,1)S(1)} %get-tuple-element.223.refs_2_), channel_id=1, source_target_pairs={{0,1},{1,0},{2,3},{3,2},{4,5},{5,4},{6,7},{7,6},{8,9},{9,8},{10,11... | collective-permute-start | bytes 1769480 | tf_op jit(solution)/shard_map/ppermute | solution.py:1027
  220.8 2.5 collective-permute-done.41.refs_3_
  224.6 5.3 %first.1 = (f32[512,768]{1,0:T(8,128)}, f32[16,768]{1,0:T(8,128)S(1)}) custom-call(s32[5]{0:T(128)S(1)} %pad_add_fusion.refs_0_, bf16[512,256]{1,0:T(8,128)(2,1)S(1)} %get-tuple-element.174.refs_3_.refs_2_.refs_1_, bf16[512,256]{1,0:T(8,128)(2,1)S(1)} %get-tuple-element.185.refs_7_.refs_3_.refs_2_, ...), custom_call_target="tpu_custom_call" | custom-call | flops 1 | bytes 1 | tf_op jit(solution)/shard_map/first/pallas_call | solution.py:108
  234.7 1.9 collective-permute-start.53
  240.9 2.7 settle.3.refs_9_
  243.6 5.8 %collective-permute-done.51.refs_8_ = f32[16,768]{1,0:T(8,128)S(1)} collective-permute-done((f32[16,768]{1,0:T(8,128)S(1)}, f32[16,768]{1,0:T(8,128)S(1)}, u32[]{:S(2)}, u32[]{:S(2)}) %collective-permute-start.51) | collective-permute-done | bytes 49184 | tf_op jit(solution)/shard_map/ppermute | solution.py:1017
  249.3 1.7 copy-done.13
  254.6 7.1 %collective-permute-start.56 = (bf16[192,512]{1,0:T(8,128)(2,1)S(1)}, bf16[192,512]{1,0:T(8,128)(2,1)S(1)}, u32[]{:S(2)}, u32[]{:S(2)}) collective-permute-start(bf16[192,512]{1,0:T(8,128)(2,1)S(1)} %get-tuple-element.238.refs_1_), channel_id=1, source_target_pairs={{0,1},{3,2},{4,5},{7,6},{8,9},{11,10},{12,13},{15,14},{16,17},{19,... | collective-permute-start | bytes 589832 | tf_op jit(solution)/shard_map/ppermute | solution.py:1027
  264.2 2.7 collective-permute-done.56.refs_2_
  267.0 4.2 %collective-permute-done.57.refs_4_ = bf16[192,512]{1,0:T(8,128)(2,1)S(1)} collective-permute-done((bf16[192,512]{1,0:T(8,128)(2,1)S(1)}, bf16[192,512]{1,0:T(8,128)(2,1)S(1)}, u32[]{:S(2)}, u32[]{:S(2)}) %collective-permute-start.57) | collective-permute-done | bytes 196640 | tf_op jit(solution)/shard_map/ppermute | solution.py:1027
  276.1 10.8 %collective-permute-start.59 = (f32[16,768]{1,0:T(8,128)S(1)}, f32[16,768]{1,0:T(8,128)S(1)}, u32[]{:S(2)}, u32[]{:S(2)}) collective-permute-start(f32[16,768]{1,0:T(8,128)S(1)} %get-tuple-element.236.refs_5_.refs_1_), channel_id=1, source_target_pairs={{0,1},{3,2},{4,5},{7,6},{8,9},{11,10},{12,13},{15,14},{16,17},{19,... | collective-permute-start | bytes 147464 | tf_op jit(solution)/shard_map/ppermute | solution.py:1027
  286.9 2.1 settle.4.refs_7_
  297.9 5.4 %collective-permute-done.68 = f32[16,768]{1,0:T(8,128)S(1)} collective-permute-done((f32[16,768]{1,0:T(8,128)S(1)}, f32[16,768]{1,0:T(8,128)S(1)}, u32[]{:S(2)}, u32[]{:S(2)}) %collective-permute-start.68) | collective-permute-done | bytes 49184 | tf_op jit(solution)/shard_map/ppermute | solution.py:1027
  306.2 2.1 collective-permute-done.66.refs_7_
  308.3 2.1 collective-permute-done.67.refs_8_
  310.4 2.1 settle.5
  (276 shorter events, 90.8 us)
Async XLA Ops:
  2.3 23.2 %collective-permute-start.3 = (bf16[192,2304]{1,0:T(8,128)(2,1)S(1)}, bf16[192,2304]{1,0:T(8,128)(2,1)S(1)}, u32[]{:S(2)}, u32[]{:S(2)}) collective-permute-start(bf16[192,2304]{1,0:T(8,128)(2,1)S(1)} %cast.1.refs_3_.refs_4_.refs_16_), channel_id=1, source_target_pairs={{0,8},{4,12},{8,0},{12,4},{16,24},{20,28},{24,16},{28,20},{1,9},{5... | collective-permute-start | bytes 2654216 | tf_op jit(solution)/shard_map/ppermute | solution.py:1017
  5.3 20.2 %collective-permute-start.4 = (bf16[512,768]{1,0:T(8,128)(2,1)}, bf16[512,768]{1,0:T(8,128)(2,1)S(1)}, u32[]{:S(2)}, u32[]{:S(2)}) collective-permute-start(bf16[512,768]{1,0:T(8,128)(2,1)} %refs_2_.1), channel_id=1, source_target_pairs={{0,16},{4,20},{8,24},{12,28},{16,0},{20,4},{24,8},{28,12},{1,17},{... | collective-permute-start | bytes 2359304 | tf_op jit(solution)/shard_map/ppermute | solution.py:1023
  12.2 18.8 %collective-permute-start.6 = (bf16[192,3840]{1,0:T(8,128)(2,1)}, bf16[192,3840]{1,0:T(8,128)(2,1)S(1)}, u32[]{:S(2)}, u32[]{:S(2)}) collective-permute-start(bf16[192,3840]{1,0:T(8,128)(2,1)} %wide_cast.1.refs_2_.refs_1_), channel_id=1, source_target_pairs={{0,4},{4,0},{8,12},{12,8},{16,20},{20,16},{24,28},{28,24},{1,5},{5... | collective-permute-start | bytes 4423688 | tf_op jit(solution)/shard_map/ppermute | solution.py:1017
  12.2 18.8 %collective-permute-start.7 = (bf16[768,768]{1,0:T(8,128)(2,1)S(1)}, bf16[768,768]{1,0:T(8,128)(2,1)S(1)}, u32[]{:S(2)}, u32[]{:S(2)}) collective-permute-start(bf16[768,768]{1,0:T(8,128)(2,1)S(1)} %get-tuple-element.134.refs_12_.refs_10_), channel_id=1, source_target_pairs={{0,4},{4,0},{8,12},{12,8},{16,20},{20,16},{24,28},{28,24},{1,5},{5... | collective-permute-start | bytes 3538952 | tf_op jit(solution)/shard_map/ppermute | solution.py:1017
  12.7 12.8 %collective-permute-start = (bf16[16,768]{1,0:T(8,128)(2,1)S(1)}, bf16[16,768]{1,0:T(8,128)(2,1)S(1)}, u32[]{:S(2)}, u32[]{:S(2)}) collective-permute-start(bf16[16,768]{1,0:T(8,128)(2,1)S(1)} %get-tuple-element.133.refs_2_.refs_0_), channel_id=1, source_target_pairs={{0,8},{4,12},{8,0},{12,4},{16,24},{20,28},{24,16},{28,20},{1,9},{5... | collective-permute-start | bytes 73736 | tf_op jit(solution)/shard_map/ppermute | solution.py:1017
  38.3 42.1 %collective-permute-start.15 = (bf16[192,3840]{1,0:T(8,128)(2,1)}, bf16[192,3840]{1,0:T(8,128)(2,1)}, u32[]{:S(2)}, u32[]{:S(2)}) collective-permute-start(bf16[192,3840]{1,0:T(8,128)(2,1)} %get-tuple-element.145.refs_8_.refs_6_), channel_id=1, source_target_pairs={{0,8},{4,12},{8,0},{12,4},{16,24},{20,28},{24,16},{28,20},{1,9},{5... | collective-permute-start | bytes 4423688 | tf_op jit(solution)/shard_map/ppermute | solution.py:1017
  40.0 29.3 %collective-permute-start.8 = (bf16[2,512,512]{2,1,0:T(8,128)(2,1)S(1)}, bf16[2,512,512]{2,1,0:T(8,128)(2,1)S(1)}, u32[]{:S(2)}, u32[]{:S(2)}) collective-permute-start(bf16[2,512,512]{2,1,0:T(8,128)(2,1)S(1)} %get-tuple-element.136.refs_1_.refs_2_), channel_id=1, source_target_pairs={{0,16},{4,20},{8,24},{12,28},{16,0},{20,4},{24,8},{28,12},{1,17},{... | collective-permute-start | bytes 3145736 | tf_op jit(solution)/shard_map/ppermute | solution.py:1023
  55.0 11.1 %collective-permute-start.13 = (bf16[192,768]{1,0:T(8,128)(2,1)S(1)}, bf16[192,768]{1,0:T(8,128)(2,1)}, u32[]{:S(2)}, u32[]{:S(2)}) collective-permute-start(bf16[192,768]{1,0:T(8,128)(2,1)S(1)} %get-tuple-element.141.refs_5_), channel_id=1, source_target_pairs={{1,0},{2,1},{5,4},{6,5},{9,8},{10,9},{13,12},{14,13},{17,16},{18,1... | collective-permute-start | bytes 884744 | tf_op jit(solution)/shard_map/ppermute | solution.py:1027
  56.3 25.1 %collective-permute-start.14 = (bf16[2,512,256]{2,1,0:T(8,128)(2,1)}, bf16[2,512,256]{2,1,0:T(8,128)(2,1)}, u32[]{:S(2)}, u32[]{:S(2)}) collective-permute-start(bf16[2,512,256]{2,1,0:T(8,128)(2,1)} %get-tuple-element.144.refs_1_.refs_2_), channel_id=1, source_target_pairs={{0,16},{4,20},{8,24},{12,28},{16,0},{20,4},{24,8},{28,12},{1,17},{... | collective-permute-start | bytes 1572872 | tf_op jit(solution)/shard_map/ppermute | solution.py:1023
  66.1 12.1 %collective-permute-start.16 = (bf16[192,768]{1,0:T(8,128)(2,1)S(1)}, bf16[192,768]{1,0:T(8,128)(2,1)}, u32[]{:S(2)}, u32[]{:S(2)}) collective-permute-start(bf16[192,768]{1,0:T(8,128)(2,1)S(1)} %get-tuple-element.142.refs_7_.refs_3_), channel_id=1, source_target_pairs={{2,3},{6,7},{10,11},{14,15},{18,19},{22,23},{26,27},{30,31}} | collective-permute-start | bytes 884744 | tf_op jit(solution)/shard_map/ppermute | solution.py:1027
  67.5 10.7 %collective-permute-start.17 = (bf16[192,768]{1,0:T(8,128)(2,1)}, bf16[192,768]{1,0:T(8,128)(2,1)}, u32[]{:S(2)}, u32[]{:S(2)}) collective-permute-start(bf16[192,768]{1,0:T(8,128)(2,1)} %get-tuple-element.147.refs_6_), channel_id=1, source_target_pairs={{1,0},{5,4},{9,8},{13,12},{17,16},{21,20},{25,24},{29,28}} | collective-permute-start | bytes 884744 | tf_op jit(solution)/shard_map/ppermute | solution.py:1027
  120.8 26.6 %collective-permute-start.24 = (bf16[2,192,1536]{2,1,0:T(8,128)(2,1)}, bf16[2,192,1536]{2,1,0:T(8,128)(2,1)S(1)}, u32[]{:S(2)}, u32[]{:S(2)}) collective-permute-start(bf16[2,192,1536]{2,1,0:T(8,128)(2,1)} %get-tuple-element.167), channel_id=1, source_target_pairs={{0,4},{4,0},{8,12},{12,8},{16,20},{20,16},{24,28},{28,24},{1,5},{5... | collective-permute-start | bytes 3538952 | tf_op jit(solution)/shard_map/ppermute | solution.py:1017
  122.8 24.6 %collective-permute-start.25 = (bf16[192,1536]{1,0:T(8,128)(2,1)}, bf16[192,1536]{1,0:T(8,128)(2,1)}, u32[]{:S(2)}, u32[]{:S(2)}) collective-permute-start(bf16[192,1536]{1,0:T(8,128)(2,1)} %get-tuple-element.168), channel_id=1, source_target_pairs={{0,8},{4,12},{8,0},{12,4},{16,24},{20,28},{24,16},{28,20},{1,9},{5... | collective-permute-start | bytes 1769480 | tf_op jit(solution)/shard_map/ppermute | solution.py:1017
  145.7 23.1 %collective-permute-start.26 = (bf16[2,192,1536]{2,1,0:T(8,128)(2,1)S(1)}, bf16[2,192,1536]{2,1,0:T(8,128)(2,1)S(1)}, u32[]{:S(2)}, u32[]{:S(2)}) collective-permute-start(bf16[2,192,1536]{2,1,0:T(8,128)(2,1)S(1)} %get-tuple-element.176), channel_id=1, source_target_pairs={{0,4},{4,0},{8,12},{12,8},{16,20},{20,16},{24,28},{28,24},{1,5},{5... | collective-permute-start | bytes 3538952 | tf_op jit(solution)/shard_map/ppermute | solution.py:1017
  145.8 23.1 %collective-permute-start.27 = (bf16[2,192,1536]{2,1,0:T(8,128)(2,1)S(1)}, bf16[2,192,1536]{2,1,0:T(8,128)(2,1)S(1)}, u32[]{:S(2)}, u32[]{:S(2)}) collective-permute-start(bf16[2,192,1536]{2,1,0:T(8,128)(2,1)S(1)} %get-tuple-element.178), channel_id=1, source_target_pairs={{0,4},{4,0},{8,12},{12,8},{16,20},{20,16},{24,28},{28,24},{1,5},{5... | collective-permute-start | bytes 3538952 | tf_op jit(solution)/shard_map/ppermute | solution.py:1017
  146.3 19.5 %collective-permute-start.22 = (bf16[512,768]{1,0:T(8,128)(2,1)S(1)}, bf16[512,768]{1,0:T(8,128)(2,1)S(1)}, u32[]{:S(2)}, u32[]{:S(2)}) collective-permute-start(bf16[512,768]{1,0:T(8,128)(2,1)S(1)} %hold.12.refs_3_.refs_0_), channel_id=1, source_target_pairs={{0,16},{4,20},{8,24},{12,28},{16,0},{20,4},{24,8},{28,12},{1,17},{... | collective-permute-start | bytes 2359304 | tf_op jit(solution)/shard_map/ppermute | solution.py:1023
  149.0 19.9 %collective-permute-start.28 = (bf16[192,1536]{1,0:T(8,128)(2,1)S(1)}, bf16[192,1536]{1,0:T(8,128)(2,1)S(1)}, u32[]{:S(2)}, u32[]{:S(2)}) collective-permute-start(bf16[192,1536]{1,0:T(8,128)(2,1)S(1)} %get-tuple-element.179), channel_id=1, source_target_pairs={{0,8},{4,12},{8,0},{12,4},{16,24},{20,28},{24,16},{28,20},{1,9},{5... | collective-permute-start | bytes 1769480 | tf_op jit(solution)/shard_map/ppermute | solution.py:1017
  150.5 18.3 %collective-permute-start.29 = (bf16[192,1536]{1,0:T(8,128)(2,1)S(1)}, bf16[192,1536]{1,0:T(8,128)(2,1)S(1)}, u32[]{:S(2)}, u32[]{:S(2)}) collective-permute-start(bf16[192,1536]{1,0:T(8,128)(2,1)S(1)} %get-tuple-element.180.refs_7_), channel_id=1, source_target_pairs={{0,1},{3,2},{4,5},{7,6},{8,9},{11,10},{12,13},{15,14},{16,17},{19,... | collective-permute-start | bytes 1769480 | tf_op jit(solution)/shard_map/ppermute | solution.py:1027
  168.8 25.1 %collective-permute-start.34 = (bf16[2,192,768]{2,1,0:T(8,128)(2,1)S(1)}, bf16[2,192,768]{2,1,0:T(8,128)(2,1)S(1)}, u32[]{:S(2)}, u32[]{:S(2)}) collective-permute-start(bf16[2,192,768]{2,1,0:T(8,128)(2,1)S(1)} %get-tuple-element.191), channel_id=1, source_target_pairs={{0,4},{4,0},{8,12},{12,8},{16,20},{20,16},{24,28},{28,24},{1,5},{5... | collective-permute-start | bytes 1769480 | tf_op jit(solution)/shard_map/ppermute | solution.py:1017
  172.6 21.3 %collective-permute-start.30 = (bf16[192,1536]{1,0:T(8,128)(2,1)S(1)}, bf16[192,1536]{1,0:T(8,128)(2,1)S(1)}, u32[]{:S(2)}, u32[]{:S(2)}) collective-permute-start(bf16[192,1536]{1,0:T(8,128)(2,1)S(1)} %get-tuple-element.187.refs_1_), channel_id=1, source_target_pairs={{0,1},{3,2},{4,5},{7,6},{8,9},{11,10},{12,13},{15,14},{16,17},{19,... | collective-permute-start | bytes 1769480 | tf_op jit(solution)/shard_map/ppermute | solution.py:1027
  177.8 16.1 %collective-permute-start.31 = (bf16[192,1536]{1,0:T(8,128)(2,1)S(1)}, bf16[192,1536]{1,0:T(8,128)(2,1)S(1)}, u32[]{:S(2)}, u32[]{:S(2)}) collective-permute-start(bf16[192,1536]{1,0:T(8,128)(2,1)S(1)} %get-tuple-element.188), channel_id=1, source_target_pairs={{0,8},{4,12},{8,0},{12,4},{16,24},{20,28},{24,16},{28,20},{1,9},{5... | collective-permute-start | bytes 1769480 | tf_op jit(solution)/shard_map/ppermute | solution.py:1017
  179.4 14.5 %collective-permute-start.32 = (bf16[192,1536]{1,0:T(8,128)(2,1)S(1)}, bf16[192,1536]{1,0:T(8,128)(2,1)S(1)}, u32[]{:S(2)}, u32[]{:S(2)}) collective-permute-start(bf16[192,1536]{1,0:T(8,128)(2,1)S(1)} %get-tuple-element.189.refs_5_), channel_id=1, source_target_pairs={{1,2},{2,1},{5,6},{6,5},{9,10},{10,9},{13,14},{14,13},{17,18},{18,... | collective-permute-start | bytes 1769480 | tf_op jit(solution)/shard_map/ppermute | solution.py:1027
  180.1 13.8 %collective-permute-start.33 = (bf16[2,512,256]{2,1,0:T(8,128)(2,1)S(1)}, bf16[2,512,256]{2,1,0:T(8,128)(2,1)S(1)}, u32[]{:S(2)}, u32[]{:S(2)}) collective-permute-start(bf16[2,512,256]{2,1,0:T(8,128)(2,1)S(1)} %copy-done.51), channel_id=1, source_target_pairs={{0,16},{4,20},{8,24},{12,28},{16,0},{20,4},{24,8},{28,12},{1,17},{... | collective-permute-start | bytes 1572872 | tf_op jit(solution)/shard_map/ppermute | solution.py:1023
  194.9 14.5 %collective-permute-start.39 = (bf16[192,1536]{1,0:T(8,128)(2,1)S(1)}, bf16[192,1536]{1,0:T(8,128)(2,1)S(1)}, u32[]{:S(2)}, u32[]{:S(2)}) collective-permute-start(bf16[192,1536]{1,0:T(8,128)(2,1)S(1)} %hold.13.refs_9_), channel_id=1, source_target_pairs={{0,8},{4,12},{8,0},{12,4},{16,24},{20,28},{24,16},{28,20},{1,9},{5... | collective-permute-start | bytes 1769480 | tf_op jit(solution)/shard_map/ppermute | solution.py:1017
  195.9 13.0 %collective-permute-start.35 = (bf16[2,512,256]{2,1,0:T(8,128)(2,1)S(1)}, bf16[2,512,256]{2,1,0:T(8,128)(2,1)S(1)}, u32[]{:S(2)}, u32[]{:S(2)}) collective-permute-start(bf16[2,512,256]{2,1,0:T(8,128)(2,1)S(1)} %get-tuple-element.199), channel_id=1, source_target_pairs={{0,16},{4,20},{8,24},{12,28},{16,0},{20,4},{24,8},{28,12},{1,17},{... | collective-permute-start | bytes 1572872 | tf_op jit(solution)/shard_map/ppermute | solution.py:1023
  197.0 14.1 %collective-permute-start.38 = (bf16[192,1536]{1,0:T(8,128)(2,1)S(1)}, bf16[192,1536]{1,0:T(8,128)(2,1)S(1)}, u32[]{:S(2)}, u32[]{:S(2)}) collective-permute-start(bf16[192,1536]{1,0:T(8,128)(2,1)S(1)} %get-tuple-element.204.refs_1_), channel_id=1, source_target_pairs={{0,1},{1,0},{2,3},{3,2},{4,5},{5,4},{6,7},{7,6},{8,9},{9,8},{10,11... | collective-permute-start | bytes 1769480 | tf_op jit(solution)/shard_map/ppermute | solution.py:1027
  198.7 12.3 %collective-permute-start.40 = (bf16[192,1536]{1,0:T(8,128)(2,1)S(1)}, bf16[192,1536]{1,0:T(8,128)(2,1)S(1)}, u32[]{:S(2)}, u32[]{:S(2)}) collective-permute-start(bf16[192,1536]{1,0:T(8,128)(2,1)S(1)} %get-tuple-element.192.refs_1_.refs_5_), channel_id=1, source_target_pairs={{1,2},{2,1},{5,6},{6,5},{9,10},{10,9},{13,14},{14,13},{17,18},{18,... | collective-permute-start | bytes 1769480 | tf_op jit(solution)/shard_map/ppermute | solution.py:1027
  209.4 13.9 %collective-permute-start.41 = (bf16[2,512,256]{2,1,0:T(8,128)(2,1)S(1)}, bf16[2,512,256]{2,1,0:T(8,128)(2,1)S(1)}, u32[]{:S(2)}, u32[]{:S(2)}) collective-permute-start(bf16[2,512,256]{2,1,0:T(8,128)(2,1)S(1)} %get-tuple-element.210), channel_id=1, source_target_pairs={{0,16},{4,20},{8,24},{12,28},{16,0},{20,4},{24,8},{28,12},{1,17},{... | collective-permute-start | bytes 1572872 | tf_op jit(solution)/shard_map/ppermute | solution.py:1023
  213.0 18.4 %collective-permute-start.42 = (bf16[192,512]{1,0:T(8,128)(2,1)S(1)}, bf16[192,512]{1,0:T(8,128)(2,1)S(1)}, u32[]{:S(2)}, u32[]{:S(2)}) collective-permute-start(bf16[192,512]{1,0:T(8,128)(2,1)S(1)} %get-tuple-element.219), channel_id=1, source_target_pairs={{0,8},{4,12},{8,0},{12,4},{16,24},{20,28},{24,16},{28,20},{1,9},{5... | collective-permute-start | bytes 589832 | tf_op jit(solution)/shard_map/ppermute | solution.py:1017
  214.5 19.0 %collective-permute-start.47 = (bf16[192,1536]{1,0:T(8,128)(2,1)S(1)}, bf16[192,1536]{1,0:T(8,128)(2,1)S(1)}, u32[]{:S(2)}, u32[]{:S(2)}) collective-permute-start(bf16[192,1536]{1,0:T(8,128)(2,1)S(1)} %get-tuple-element.226), channel_id=1, source_target_pairs={{0,8},{4,12},{8,0},{12,4},{16,24},{20,28},{24,16},{28,20},{1,9},{5... | collective-permute-start | bytes 1769480 | tf_op jit(solution)/shard_map/ppermute | solution.py:1017
  215.1 18.5 %collective-permute-start.45 = (bf16[192,1536]{1,0:T(8,128)(2,1)S(1)}, bf16[192,1536]{1,0:T(8,128)(2,1)S(1)}, u32[]{:S(2)}, u32[]{:S(2)}) collective-permute-start(bf16[192,1536]{1,0:T(8,128)(2,1)S(1)} %get-tuple-element.223.refs_2_), channel_id=1, source_target_pairs={{0,1},{1,0},{2,3},{3,2},{4,5},{5,4},{6,7},{7,6},{8,9},{9,8},{10,11... | collective-permute-start | bytes 1769480 | tf_op jit(solution)/shard_map/ppermute | solution.py:1027
  218.8 14.7 %collective-permute-start.48 = (bf16[192,1536]{1,0:T(8,128)(2,1)S(1)}, bf16[192,1536]{1,0:T(8,128)(2,1)S(1)}, u32[]{:S(2)}, u32[]{:S(2)}) collective-permute-start(bf16[192,1536]{1,0:T(8,128)(2,1)S(1)} %get-tuple-element.206.refs_7_.refs_11_), channel_id=1, source_target_pairs={{1,2},{2,1},{5,6},{6,5},{9,10},{10,9},{13,14},{14,13},{17,18},{18,... | collective-permute-start | bytes 1769480 | tf_op jit(solution)/shard_map/ppermute | solution.py:1027
  234.7 17.0 %collective-permute-start.53 = (bf16[192,1536]{1,0:T(8,128)(2,1)S(1)}, bf16[192,1536]{1,0:T(8,128)(2,1)S(1)}, u32[]{:S(2)}, u32[]{:S(2)}) collective-permute-start(bf16[192,1536]{1,0:T(8,128)(2,1)S(1)} %get-tuple-element.234.refs_1_), channel_id=1, source_target_pairs={{0,1},{1,0},{2,3},{3,2},{4,5},{5,4},{6,7},{7,6},{8,9},{9,8},{10,11... | collective-permute-start | bytes 1769480 | tf_op jit(solution)/shard_map/ppermute | solution.py:1027
  236.6 15.1 %collective-permute-start.54 = (bf16[192,1536]{1,0:T(8,128)(2,1)S(1)}, bf16[192,1536]{1,0:T(8,128)(2,1)S(1)}, u32[]{:S(2)}, u32[]{:S(2)}) collective-permute-start(bf16[192,1536]{1,0:T(8,128)(2,1)S(1)} %get-tuple-element.235.refs_3_), channel_id=1, source_target_pairs={{1,2},{2,1},{5,6},{6,5},{9,10},{10,9},{13,14},{14,13},{17,18},{18,... | collective-permute-start | bytes 1769480 | tf_op jit(solution)/shard_map/ppermute | solution.py:1027
  237.3 12.0 %collective-permute-start.49 = (bf16[192,512]{1,0:T(8,128)(2,1)S(1)}, bf16[192,512]{1,0:T(8,128)(2,1)S(1)}, u32[]{:S(2)}, u32[]{:S(2)}) collective-permute-start(bf16[192,512]{1,0:T(8,128)(2,1)S(1)} %get-tuple-element.228), channel_id=1, source_target_pairs={{0,8},{4,12},{8,0},{12,4},{16,24},{20,28},{24,16},{28,20},{1,9},{5... | collective-permute-start | bytes 589832 | tf_op jit(solution)/shard_map/ppermute | solution.py:1017
  252.6 20.9 %collective-permute-start.55 = (bf16[192,1536]{1,0:T(8,128)(2,1)S(1)}, bf16[192,1536]{1,0:T(8,128)(2,1)S(1)}, u32[]{:S(2)}, u32[]{:S(2)}) collective-permute-start(bf16[192,1536]{1,0:T(8,128)(2,1)S(1)} %get-tuple-element.237.refs_5_.refs_3_), channel_id=1, source_target_pairs={{1,2},{2,1},{5,6},{6,5},{9,10},{10,9},{13,14},{14,13},{17,18},{18,... | collective-permute-start | bytes 1769480 | tf_op jit(solution)/shard_map/ppermute | solution.py:1027
  253.3 20.1 %collective-permute-start.58 = (bf16[192,1536]{1,0:T(8,128)(2,1)S(1)}, bf16[192,1536]{1,0:T(8,128)(2,1)S(1)}, u32[]{:S(2)}, u32[]{:S(2)}) collective-permute-start(bf16[192,1536]{1,0:T(8,128)(2,1)S(1)} %get-tuple-element.241.refs_2_), channel_id=1, source_target_pairs={{1,0},{2,3},{5,4},{6,7},{9,8},{10,11},{13,12},{14,15},{17,16},{18,... | collective-permute-start | bytes 1769480 | tf_op jit(solution)/shard_map/ppermute | solution.py:1027
  254.6 12.4 %collective-permute-start.56 = (bf16[192,512]{1,0:T(8,128)(2,1)S(1)}, bf16[192,512]{1,0:T(8,128)(2,1)S(1)}, u32[]{:S(2)}, u32[]{:S(2)}) collective-permute-start(bf16[192,512]{1,0:T(8,128)(2,1)S(1)} %get-tuple-element.238.refs_1_), channel_id=1, source_target_pairs={{0,1},{3,2},{4,5},{7,6},{8,9},{11,10},{12,13},{15,14},{16,17},{19,... | collective-permute-start | bytes 589832 | tf_op jit(solution)/shard_map/ppermute | solution.py:1027
  262.9 10.5 %collective-permute-start.52 = (bf16[192,512]{1,0:T(8,128)(2,1)S(1)}, bf16[192,512]{1,0:T(8,128)(2,1)S(1)}, u32[]{:S(2)}, u32[]{:S(2)}) collective-permute-start(bf16[192,512]{1,0:T(8,128)(2,1)S(1)} %get-tuple-element.232.refs_1_), channel_id=1, source_target_pairs={{0,1},{3,2},{4,5},{7,6},{8,9},{11,10},{12,13},{15,14},{16,17},{19,... | collective-permute-start | bytes 589832 | tf_op jit(solution)/shard_map/ppermute | solution.py:1027
  271.8 17.2 %collective-permute-start.60 = (bf16[192,512]{1,0:T(8,128)(2,1)S(1)}, bf16[192,512]{1,0:T(8,128)(2,1)S(1)}, u32[]{:S(2)}, u32[]{:S(2)}) collective-permute-start(bf16[192,512]{1,0:T(8,128)(2,1)S(1)} %get-tuple-element.240.refs_5_.refs_3_), channel_id=1, source_target_pairs={{1,2},{2,1},{5,6},{6,5},{9,10},{10,9},{13,14},{14,13},{17,18},{18,... | collective-permute-start | bytes 589832 | tf_op jit(solution)/shard_map/ppermute | solution.py:1027
  272.5 16.6 %collective-permute-start.61 = (bf16[192,512]{1,0:T(8,128)(2,1)S(1)}, bf16[192,512]{1,0:T(8,128)(2,1)S(1)}, u32[]{:S(2)}, u32[]{:S(2)}) collective-permute-start(bf16[192,512]{1,0:T(8,128)(2,1)S(1)} %get-tuple-element.243.refs_5_), channel_id=1, source_target_pairs={{1,2},{2,1},{5,6},{6,5},{9,10},{10,9},{13,14},{14,13},{17,18},{18,... | collective-permute-start | bytes 589832 | tf_op jit(solution)/shard_map/ppermute | solution.py:1027
  274.1 36.2 %collective-permute-start.64 = (bf16[192,1536]{1,0:T(8,128)(2,1)S(1)}, bf16[192,1536]{1,0:T(8,128)(2,1)S(1)}, u32[]{:S(2)}, u32[]{:S(2)}) collective-permute-start(bf16[192,1536]{1,0:T(8,128)(2,1)S(1)} %get-tuple-element.242.refs_1_), channel_id=1, source_target_pairs={{1,0},{2,3},{5,4},{6,7},{9,8},{10,11},{13,12},{14,15},{17,16},{18,... | collective-permute-start | bytes 1769480 | tf_op jit(solution)/shard_map/ppermute | solution.py:1027
  275.4 16.6 %collective-permute-start.62 = (bf16[192,512]{1,0:T(8,128)(2,1)S(1)}, bf16[192,512]{1,0:T(8,128)(2,1)S(1)}, u32[]{:S(2)}, u32[]{:S(2)}) collective-permute-start(bf16[192,512]{1,0:T(8,128)(2,1)S(1)} %get-tuple-element.244.refs_5_.refs_1_), channel_id=1, source_target_pairs={{1,2},{2,1},{5,6},{6,5},{9,10},{10,9},{13,14},{14,13},{17,18},{18,... | collective-permute-start | bytes 589832 | tf_op jit(solution)/shard_map/ppermute | solution.py:1027
  276.1 12.9 %collective-permute-start.59 = (f32[16,768]{1,0:T(8,128)S(1)}, f32[16,768]{1,0:T(8,128)S(1)}, u32[]{:S(2)}, u32[]{:S(2)}) collective-permute-start(f32[16,768]{1,0:T(8,128)S(1)} %get-tuple-element.236.refs_5_.refs_1_), channel_id=1, source_target_pairs={{0,1},{3,2},{4,5},{7,6},{8,9},{11,10},{12,13},{15,14},{16,17},{19,... | collective-permute-start | bytes 147464 | tf_op jit(solution)/shard_map/ppermute | solution.py:1027
  292.7 10.6 %collective-permute-start.68 = (f32[16,768]{1,0:T(8,128)S(1)}, f32[16,768]{1,0:T(8,128)S(1)}, u32[]{:S(2)}, u32[]{:S(2)}) collective-permute-start(f32[16,768]{1,0:T(8,128)S(1)} %get-tuple-element.249.refs_9_), channel_id=1, source_target_pairs={{1,0},{2,3},{5,4},{6,7},{9,8},{10,11},{13,12},{14,15},{17,16},{18,... | collective-permute-start | bytes 147464 | tf_op jit(solution)/shard_map/ppermute | solution.py:1027
  294.0 12.2 %collective-permute-start.65 = (bf16[192,512]{1,0:T(8,128)(2,1)S(1)}, bf16[192,512]{1,0:T(8,128)(2,1)S(1)}, u32[]{:S(2)}, u32[]{:S(2)}) collective-permute-start(bf16[192,512]{1,0:T(8,128)(2,1)S(1)} %get-tuple-element.245.refs_2_), channel_id=1, source_target_pairs={{1,0},{2,3},{5,4},{6,7},{9,8},{10,11},{13,12},{14,15},{17,16},{18,... | collective-permute-start | bytes 589832 | tf_op jit(solution)/shard_map/ppermute | solution.py:1027
  295.3 13.0 %collective-permute-start.66 = (bf16[192,512]{1,0:T(8,128)(2,1)S(1)}, bf16[192,512]{1,0:T(8,128)(2,1)S(1)}, u32[]{:S(2)}, u32[]{:S(2)}) collective-permute-start(bf16[192,512]{1,0:T(8,128)(2,1)S(1)} %get-tuple-element.246.refs_3_), channel_id=1, source_target_pairs={{1,0},{2,3},{5,4},{6,7},{9,8},{10,11},{13,12},{14,15},{17,16},{18,... | collective-permute-start | bytes 589832 | tf_op jit(solution)/shard_map/ppermute | solution.py:1027
  296.6 13.8 %collective-permute-start.67 = (bf16[192,512]{1,0:T(8,128)(2,1)S(1)}, bf16[192,512]{1,0:T(8,128)(2,1)S(1)}, u32[]{:S(2)}, u32[]{:S(2)}) collective-permute-start(bf16[192,512]{1,0:T(8,128)(2,1)S(1)} %get-tuple-element.248.refs_4_), channel_id=1, source_target_pairs={{1,0},{2,3},{5,4},{6,7},{9,8},{10,11},{13,12},{14,15},{17,16},{18,... | collective-permute-start | bytes 589832 | tf_op jit(solution)/shard_map/ppermute | solution.py:1027
  (83 other events, 597.5 us)
